TPU v7x, 32 devices: a whole 2x2x4 slice. The times are simulated.
32 devices in a mesh: dp: 8 (over z, y), row: 2 (over x), col: 2 (over core).
Axes of the slice: x: 2, y: 2, z: 4, core: 2. Of those that a mesh axis runs over, the one named last changes fastest.
Arguments:
- tokens: bfloat16 [8192, 2048], P(('dp', 'col'), 'row'), may hold values from -6 to 6
- segments: int32 [8, 1024], P('dp'), may hold values from 0 to 3, never falling along the last dimension, each value on 1 to 512 neighbouring positions
- ln1_gain: float32 [2048], P('row'), may hold values from 0.5 to 1.5
- ln1_bias: float32 [2048], P('row'), may hold values from -2 to 2
- qkv_weight: bfloat16 [2048, 3, 2048], P('row', None, 'col'), may hold values from -0.125 to 0.125
- qkv_bias: float32 [3, 2048], P(None, 'col'), may hold values from -2 to 2
- out_weight: bfloat16 [2048, 2048], P('col', 'row'), may hold values from -1.5 to 1.5
- ln2_gain: float32 [2048], P('row'), may hold values from 0.5 to 1.5
- ln2_bias: float32 [2048], P('row'), may hold values from -2 to 2
- gate_up_weight: bfloat16 [2048, 2, 5632], P('row', None, 'col'), may hold values from -0.125 to 0.125
- down_weight: bfloat16 [5632, 2048], P('col', 'row'), may hold values from -0.078125 to 0.078125
- cotangent: bfloat16 [8192, 2048], P(('dp', 'col'), 'row'), may hold values from -6 to 6
Outputs:
- result: bfloat16 [8192, 2048], P(('dp', 'col'), 'row')
- input_grad: float32 [8192, 2048], P(('dp', 'col'), 'row')
- ln1_gain_grad: float32 [2048], P('row')
- ln1_bias_grad: float32 [2048], P('row')
- qkv_weight_grad: float32 [2048, 3, 2048], P('row', None, 'col')
- qkv_bias_grad: float32 [3, 2048], P(None, 'col')
- out_weight_grad: float32 [2048, 2048], P('col', 'row')
- ln2_gain_grad: float32 [2048], P('row')
- ln2_bias_grad: float32 [2048], P('row')
- gate_up_weight_grad: float32 [2048, 2, 5632], P('row', None, 'col')
- down_weight_grad: float32 [5632, 2048], P('col', 'row')
All inputs are finite; a program needn't handle non-finite values.
Results may differ from a plain program's by a relative error of at most 0.025.
Values may be sent and summed in bfloat16 or wider, within the bound.
A program may use at most 256 MiB of HBM per device.

v0:
```python
import math

import jax
import jax.numpy as jnp
from jax import lax
from jax.sharding import PartitionSpec as P

D = 2048
HEAD = 64
ROT = 16


EPSILON = 1e-05
ROPE_BASE = 10000.0
NEGATIVE = -1e30


def token_gather(values):
    return lax.all_gather(values, "col", axis=0, tiled=True)


def token_sum(values):
    return lax.psum_scatter(
        values.astype(jnp.bfloat16), "col", scatter_dimension=0, tiled=True
    ).astype(jnp.float32)


def head_sum(values):
    return lax.psum_scatter(values, "row", scatter_dimension=2, tiled=True)


def head_gather(values):
    return lax.all_gather(values, "row", axis=2, tiled=True)


def hidden_sum(values):
    return lax.psum_scatter(
        values.astype(jnp.bfloat16), "row", scatter_dimension=0, tiled=True
    ).astype(jnp.float32)


def hidden_gather(values):
    return lax.all_gather(values, "row", axis=0, tiled=True)


def row_totals(first_sum, second_sum):
    return lax.psum((first_sum, second_sum), "row")


def norm_forward(values, feature_count, norm_gain, norm_shift):
    first_sum, second_sum = row_totals(jnp.sum(values, axis=-1), jnp.sum(values * values, axis=-1))
    center_mean = first_sum / feature_count
    spread = second_sum / feature_count - center_mean * center_mean
    inverse = lax.rsqrt(spread + EPSILON)[:, None]
    normal = (values - center_mean[:, None]) * inverse
    return (normal * norm_gain + norm_shift, normal, inverse)


def norm_backward(grad_norm, normal, inverse, norm_gain, feature_count):
    scaled = grad_norm * norm_gain
    first_sum, second_sum = row_totals(jnp.sum(scaled, axis=-1), jnp.sum(scaled * normal, axis=-1))
    grad_input = inverse * (
        scaled - first_sum[:, None] / feature_count - normal * (second_sum[:, None] / feature_count)
    )
    return (grad_input, jnp.sum(grad_norm * normal, axis=0), jnp.sum(grad_norm, axis=0))


def doc_positions(segment_ids):
    places = jnp.arange(segment_ids.shape[0], dtype=jnp.int32)
    starts = jnp.concatenate([jnp.ones((1,), dtype=bool), segment_ids[1:] != segment_ids[:-1]])
    first_place = lax.cummax(jnp.where(starts, places, jnp.zeros_like(places)), axis=0)
    return places - first_place


def rotary_tables(segment_ids):
    places = doc_positions(segment_ids).astype(jnp.float32)
    freq_index = jnp.arange(ROT // 2, dtype=jnp.float32)
    inverse = jnp.exp(freq_index * (-2.0 / ROT) * math.log(ROPE_BASE))
    angles = places[:, None] * inverse[None, :]
    return (jnp.cos(angles)[:, None, :], jnp.sin(angles)[:, None, :])


def rotary(head_rows, cosines, sines):
    half_rot = ROT // 2
    first_half = head_rows[..., :half_rot]
    second_half = head_rows[..., half_rot:ROT]
    return jnp.concatenate(
        [
            first_half * cosines - second_half * sines,
            second_half * cosines + first_half * sines,
            head_rows[..., ROT:],
        ],
        axis=-1,
    )


def silu_product(gate_rows, up_rows):
    return jax.nn.silu(gate_rows) * up_rows


def score_block(query_rows, key_rows, query_ids, key_ids, begin_row, factor):
    scores = (
        jnp.einsum("qhd,khd->hqk", query_rows, key_rows, preferred_element_type=jnp.float32)
        * factor
    )
    query_places = begin_row + jnp.arange(query_rows.shape[0], dtype=jnp.int32)
    key_places = jnp.arange(key_rows.shape[0], dtype=jnp.int32)
    allowed = (query_ids[:, None] == key_ids[None, :]) & (
        key_places[None, :] <= query_places[:, None]
    )
    return jnp.where(allowed[None], scores, NEGATIVE)


def local(
    tokens,
    segments,
    ln1_gain,
    ln1_bias,
    qkv_weight,
    qkv_bias,
    out_weight,
    ln2_gain,
    ln2_bias,
    gate_up_weight,
    down_weight,
    cotangent,
):
    feature_count = D
    row_count = lax.axis_size("row")
    segment_ids = segments[0]
    length = segment_ids.shape[0]
    head_width = qkv_weight.shape[2] // row_count
    local_heads = head_width // HEAD
    factor = HEAD ** (-0.5)
    block_rows = min(512, length)
    block_count = length // block_rows
    cosines, sines = rotary_tables(segment_ids)
    inputs = tokens.astype(jnp.float32)
    normed_one, normal_one, inverse_one = norm_forward(inputs, feature_count, ln1_gain, ln1_bias)
    act_one = token_gather(normed_one.astype(jnp.bfloat16))
    joined_qkv = head_sum(
        jnp.einsum("sd,dkh->skh", act_one, qkv_weight, preferred_element_type=jnp.float32)
    )
    offset = lax.dynamic_slice_in_dim(qkv_bias, lax.axis_index("row") * head_width, head_width, 1)
    joined_qkv = (joined_qkv + offset).reshape(length, 3, local_heads, HEAD)
    queries = rotary(joined_qkv[:, 0], cosines, sines).astype(jnp.bfloat16)
    key_heads = rotary(joined_qkv[:, 1], cosines, sines).astype(jnp.bfloat16)
    value_heads = joined_qkv[:, 2].astype(jnp.bfloat16)
    block_outputs = []
    log_totals = []
    for block_index in range(block_count):
        begin_row = block_index * block_rows
        finish = begin_row + block_rows
        scores = score_block(
            queries[begin_row:finish],
            key_heads[:finish],
            segment_ids[begin_row:finish],
            segment_ids[:finish],
            begin_row,
            factor,
        )
        maxima = jnp.max(scores, axis=-1, keepdims=True)
        shifted = jnp.exp(scores - maxima)
        totals = jnp.sum(shifted, axis=-1, keepdims=True)
        weights = (shifted / totals).astype(jnp.bfloat16)
        block_outputs.append(
            jnp.einsum(
                "hqk,khd->qhd", weights, value_heads[:finish], preferred_element_type=jnp.float32
            )
        )
        log_totals.append(maxima + jnp.log(totals))
    attended = (
        jnp.concatenate(block_outputs, axis=0).astype(jnp.bfloat16).reshape(length, 1, head_width)
    )
    attended_all = head_gather(attended).reshape(length, -1)
    branch = token_sum(jnp.dot(attended_all, out_weight, preferred_element_type=jnp.float32))
    hidden_state = inputs + branch
    normed_two, normal_two, inverse_two = norm_forward(
        hidden_state, feature_count, ln2_gain, ln2_bias
    )
    act_two = token_gather(normed_two.astype(jnp.bfloat16))
    gate_up = hidden_sum(
        jnp.einsum("sd,dkf->skf", act_two, gate_up_weight, preferred_element_type=jnp.float32)
    )
    inner_act = silu_product(gate_up[:, 0], gate_up[:, 1]).astype(jnp.bfloat16)
    inner_all = hidden_gather(inner_act)
    feed_out = token_sum(jnp.dot(inner_all, down_weight, preferred_element_type=jnp.float32))
    result = (hidden_state + feed_out).astype(jnp.bfloat16)
    grad_out = cotangent.astype(jnp.float32)
    grad_rows = token_gather(cotangent)
    down_grad = jnp.einsum("sf,sd->fd", inner_all, grad_rows, preferred_element_type=jnp.float32)
    grad_inner = hidden_sum(
        jnp.einsum("sd,fd->sf", grad_rows, down_weight, preferred_element_type=jnp.float32)
    )
    unused_value, pullback = jax.vjp(silu_product, gate_up[:, 0], gate_up[:, 1])
    grad_gate, grad_up = pullback(grad_inner)
    grad_local = jnp.stack([grad_gate, grad_up], axis=1).astype(jnp.bfloat16)
    grad_pair = hidden_gather(grad_local)
    gate_up_grad = jnp.einsum("sd,skf->dkf", act_two, grad_pair, preferred_element_type=jnp.float32)
    grad_act_two = token_sum(
        jnp.einsum("skf,dkf->sd", grad_pair, gate_up_weight, preferred_element_type=jnp.float32)
    )
    grad_norm_two, ln2_gain_grad, ln2_bias_grad = norm_backward(
        grad_act_two, normal_two, inverse_two, ln2_gain, feature_count
    )
    grad_hidden = grad_out + grad_norm_two
    grad_branch = token_gather(grad_hidden.astype(jnp.bfloat16))
    out_grad = jnp.einsum(
        "sh,sd->hd", attended_all, grad_branch, preferred_element_type=jnp.float32
    )
    grad_partial = jnp.einsum(
        "sd,hd->sh", grad_branch, out_weight, preferred_element_type=jnp.float32
    )
    grad_attended = (
        head_sum(grad_partial.reshape(length, 1, -1))
        .astype(jnp.bfloat16)
        .reshape(length, local_heads, HEAD)
    )
    grad_query_blocks = []
    grad_keys = jnp.zeros(key_heads.shape, jnp.float32)
    grad_values = jnp.zeros(value_heads.shape, jnp.float32)
    for block_index in range(block_count):
        begin_row = block_index * block_rows
        finish = begin_row + block_rows
        scores = score_block(
            queries[begin_row:finish],
            key_heads[:finish],
            segment_ids[begin_row:finish],
            segment_ids[:finish],
            begin_row,
            factor,
        )
        weights = jnp.exp(scores - log_totals[block_index])
        low_weights = weights.astype(jnp.bfloat16)
        grad_block = grad_attended[begin_row:finish]
        grad_values = grad_values.at[:finish].add(
            jnp.einsum("hqk,qhd->khd", low_weights, grad_block, preferred_element_type=jnp.float32)
        )
        grad_weights = jnp.einsum(
            "qhd,khd->hqk", grad_block, value_heads[:finish], preferred_element_type=jnp.float32
        )
        grad_scores = (
            weights * (grad_weights - jnp.sum(weights * grad_weights, axis=-1, keepdims=True))
        ).astype(jnp.bfloat16)
        grad_query_blocks.append(
            jnp.einsum(
                "hqk,khd->qhd", grad_scores, key_heads[:finish], preferred_element_type=jnp.float32
            )
            * factor
        )
        grad_keys = grad_keys.at[:finish].add(
            jnp.einsum(
                "hqk,qhd->khd",
                grad_scores,
                queries[begin_row:finish],
                preferred_element_type=jnp.float32,
            )
            * factor
        )
    grad_queries = jnp.concatenate(grad_query_blocks, axis=0)
    grad_joined = jnp.stack(
        [rotary(grad_queries, cosines, -sines), rotary(grad_keys, cosines, -sines), grad_values],
        axis=1,
    )
    grad_joined = grad_joined.reshape(length, 3, head_width).astype(jnp.bfloat16)
    grad_joined_all = head_gather(grad_joined)
    qkv_grad = jnp.einsum(
        "sd,skh->dkh", act_one, grad_joined_all, preferred_element_type=jnp.float32
    )
    qkv_offset_grad = jnp.sum(grad_joined_all, axis=0, dtype=jnp.float32)
    grad_act_one = token_sum(
        jnp.einsum("skh,dkh->sd", grad_joined_all, qkv_weight, preferred_element_type=jnp.float32)
    )
    grad_norm_one, ln1_gain_grad, ln1_bias_grad = norm_backward(
        grad_act_one, normal_one, inverse_one, ln1_gain, feature_count
    )
    input_grad = grad_hidden + grad_norm_one
    ln1_gain_grad, ln1_bias_grad, ln2_gain_grad, ln2_bias_grad = lax.psum(
        (ln1_gain_grad, ln1_bias_grad, ln2_gain_grad, ln2_bias_grad), ("dp", "col")
    )
    down_grad, gate_up_grad, out_grad, qkv_grad, qkv_offset_grad = (
        lax.psum(down_grad.astype(jnp.bfloat16), "dp").astype(jnp.float32),
        lax.psum(gate_up_grad.astype(jnp.bfloat16), "dp").astype(jnp.float32),
        lax.psum(out_grad.astype(jnp.bfloat16), "dp").astype(jnp.float32),
        lax.psum(qkv_grad.astype(jnp.bfloat16), "dp").astype(jnp.float32),
        lax.psum(qkv_offset_grad.astype(jnp.bfloat16), "dp").astype(jnp.float32),
    )
    return (
        result,
        input_grad,
        ln1_gain_grad,
        ln1_bias_grad,
        qkv_grad,
        qkv_offset_grad,
        out_grad,
        ln2_gain_grad,
        ln2_bias_grad,
        gate_up_grad,
        down_grad,
    )


def solution(mesh):
    in_specs = (
        P(("dp", "col"), "row"),
        P("dp", None),
        P("row"),
        P("row"),
        P("row", None, "col"),
        P(None, "col"),
        P("col", "row"),
        P("row"),
        P("row"),
        P("row", None, "col"),
        P("col", "row"),
        P(("dp", "col"), "row"),
    )
    out_specs = (
        P(("dp", "col"), "row"),
        P(("dp", "col"), "row"),
        P("row"),
        P("row"),
        P("row", None, "col"),
        P(None, "col"),
        P("col", "row"),
        P("row"),
        P("row"),
        P("row", None, "col"),
        P("col", "row"),
    )
    return jax.shard_map(local, mesh=mesh, in_specs=in_specs, out_specs=out_specs, check_vma=False)
```

profile of v0, /device:TPU:0, one launch (start us, length us, event | category | flops | bytes accessed | tf_op | source)
XLA Modules:
  0.0 1893.6 jit_solution(16917403263635142123)
XLA Ops:
  18.2 12.5 all-gather.9.cloned.1.call-done
  30.7 12.1 fusion.58
  45.9 142.8 %reduce-scatter.9.cloned.1.call-done = f32[1024,3,512]{2,0,1:T(8,128)} async-done(((f32[1024,3,1024]{2,0,1:T(8,128)}), f32[1024,3,512]{2,0,1:T(8,128)}) %reduce-scatter.9.cloned.1.call-update) | async-done | bytes 6291472 | tf_op jit(solution)/shard_map/reduce_scatter | solution.py:29
  240.2 32.8 %all-gather.11.cloned.1.call-done = bf16[1024,1,1024]{0,2,1:T(8,128)(2,1)} async-done(((bf16[1024,1,512]{0,2,1:T(8,128)(2,1)}), bf16[1024,1,1024]{0,2,1:T(8,128)(2,1)}) %all-gather.11.cloned.1.call-update) | async-done | bytes 2097168 | tf_op jit(solution)/shard_map/all_gather | solution.py:33
  298.2 11.3 all-gather.13.cloned.1.call-done
  309.5 18.4 fusion.10
  328.0 10.9 convolution_convert_fusion.2
  339.2 123.2 %reduce-scatter.13.cloned.1.call-done = bf16[512,2,2816]{2,0,1:T(8,128)(2,1)} async-done(((bf16[1024,2,2816]{2,0,1:T(8,128)(2,1)}), bf16[512,2,2816]{2,0,1:T(8,128)(2,1)}) %reduce-scatter.13.cloned.1.call-update) | async-done | bytes 5767184 | tf_op jit(solution)/shard_map/reduce_scatter | solution.py:37
  470.3 65.9 %reduce-scatter.17.cloned.1.call-done = bf16[512,2816]{1,0:T(8,128)(2,1)} async-done(((bf16[1024,2816]{1,0:T(8,128)(2,1)}), bf16[512,2816]{1,0:T(8,128)(2,1)}) %reduce-scatter.17.cloned.1.call-update) | async-done | bytes 2883600 | tf_op jit(solution)/shard_map/reduce_scatter | solution.py:37
  547.2 139.8 %all-gather.19.cloned.1.call-done = bf16[1024,2,2816]{2,0,1:T(8,128)(2,1)} async-done(((bf16[512,2,2816]{2,0,1:T(8,128)(2,1)}), bf16[1024,2,2816]{2,0,1:T(8,128)(2,1)}) %all-gather.19.cloned.1.call-update) | async-done | bytes 11534352 | tf_op jit(solution)/shard_map/all_gather | solution.py:43
  687.0 18.9 %bitcast_convert_fusion.1 = bf16[1024,1024]{1,0:T(8,128)(2,1)} fusion(bf16[1024,2,2816]{2,0,1:T(8,128)(2,1)} %all-gather.19.cloned.1.call-done, bf16[1024,2,2816]{2,1,0:T(2,128)(2,1)} %param.33), kind=kOutput, calls=%fused_computation.42 | convolution fusion | flops 11812208640 | bytes 25165824 | tf_op jit(solution)/shard_map/skf,dkf->sd/dot_general | solution.py:201
  727.9 11.8 all-gather.21.cloned.1.call-done
  745.8 55.5 %reduce-scatter.21.cloned.1.call-done = f32[1024,1,512]{2,0,1:T(8,128)} async-done(((f32[1024,1,1024]{2,0,1:T(8,128)}), f32[1024,1,512]{2,0,1:T(8,128)}) %reduce-scatter.21.cloned.1.call-update) | async-done | bytes 2097168 | tf_op jit(solution)/shard_map/reduce_scatter | solution.py:29
  821.7 11.5 multiply_reduce_fusion
  843.9 11.8 multiply_convert_fusion
  868.4 79.9 %all-gather.23.cloned.1.call-done = bf16[1024,3,1024]{2,0,1:T(8,128)(2,1)} async-done(((bf16[1024,3,512]{2,0,1:T(8,128)(2,1)}), bf16[1024,3,1024]{2,0,1:T(8,128)(2,1)}) %all-gather.23.cloned.1.call-update) | async-done | bytes 6291472 | tf_op jit(solution)/shard_map/all_gather | solution.py:33
  948.3 11.8 bitcast_convert_fusion
  960.2 64.0 %all-gather.15.cloned.1.call-done = bf16[1024,2816]{1,0:T(8,128)(2,1)} async-done(((bf16[512,2816]{1,0:T(8,128)(2,1)}), bf16[1024,2816]{1,0:T(8,128)(2,1)}) %all-gather.15.cloned.1.call-update) | async-done | bytes 5767184 | tf_op jit(solution)/shard_map/all_gather | solution.py:43
  1035.1 11.3 convolution_convert_fusion.1
  1046.4 19.3 %convolution_convert_fusion = bf16[1024,2,2816]{2,0,1:T(8,128)(2,1)} fusion(bf16[1024,2,2816]{2,0,1:T(8,128)(2,1)} %all-gather.19.cloned.1.call-done, bf16[1024,1024]{1,0:T(8,128)(2,1)S(1)} %copy-done.45), kind=kOutput, calls=%fused_computation.23 | convolution fusion | flops 11816927232 | bytes 25165824 | tf_op jit(solution)/shard_map/sd,skf->dkf/dot_general | solution.py:199
  1083.2 22.5 %psum.130 = bf16[3,1024]{1,0:T(4,128)(2,1)S(1)} all-reduce(bf16[3,1024]{1,0:T(4,128)(2,1)S(1)} %reduce_sum.170), channel_id=1, replica_groups=mesh['dp'=8,'row'=2,'col'=2] {'dp'}, use_global_device_ids=true, to_apply=%region_38.39 | all-reduce | flops 3072 | bytes 12288 | tf_op jit(solution)/shard_map/psum | solution.py:286
  1113.5 62.4 %all-reduce.2 = (f32[1024]{0:T(1024)}, f32[1024]{0:T(1024)}, f32[1024]{0:T(1024)}, f32[1024]{0:T(1024)}) all-reduce(f32[1024]{0:T(1024)S(1)} %get-tuple-element.99, f32[1024]{0:T(1024)S(1)} %get-tuple-element.106, f32[1024]{0:T(1024)S(1)} %copy-done.39, f32[1024]{0:T(1024)S(1)} %copy-done.40), channel_id=1, replica_groups=mesh['dp'=8,'row'=2,'col'=2] {'dp','col'}, use_global_device_ids=true, to_apply=%region_33.34 | all-reduce | flops 4096 | bytes 32768 | tf_op jit(solution)/shard_map/psum | solution.py:278
  1180.4 666.1 %all-reduce.10.cloned.1.call-done = (bf16[1024,2,2816]{2,0,1:T(8,128)(2,1)}, bf16[1024,3,1024]{2,0,1:T(8,128)(2,1)}, bf16[1024,1024]{1,0:T(8,128)(2,1)}, bf16[2816,1024]{1,0:T(8,128)(2,1)}) async-done(((bf16[1024,2,2816]{2,0,1:T(8,128)(2,1)}, bf16[1024,3,1024]{2,0,1:T(8,128)(2,1)}, bf16[1024,1024]{1,0:T(8,128)(2,1)}, bf16[2816,1024]{1,0:T(8,128)(2,1)}), (bf16[1024,2,2816]{2,0,1:T(8,128)(2,1)}, ...) | async-done | bytes 25690128 | tf_op jit(solution)/shard_map/psum | solution.py:283
  1850.9 23.9 %copy.56 = f32[1024,2,2816]{2,1,0:T(2,128)} copy(bf16[1024,2,2816]{2,0,1:T(8,128)(2,1)} %get-tuple-element.121) | data formatting | bytes 34603008
  (235 shorter events, 238.2 us)
Async XLA Ops:
  7.2 265.8 %copy-start = (bf16[1024,1024]{1,0:T(8,128)(2,1)S(1)}, bf16[1024,1024]{1,0:T(8,128)(2,1)}, u32[]{:S(2)}) copy-start(bf16[1024,1024]{1,0:T(8,128)(2,1)} %param.30) | copy-start | bytes 6291460
  7.2 23.5 %all-gather.9.cloned.1.call-start = ((), (), s32[]{:S(2)}) async-start(), calls=%async_computation.8 | async-start | bytes 3145728 | tf_op jit(solution)/shard_map/all_gather | solution.py:19
  18.1 170.5 %reduce-scatter.9.cloned.1.call-start = ((), (), s32[]{:S(2)}) async-start(), calls=%async_computation.9 | async-start | bytes 18874368 | tf_op jit(solution)/shard_map/reduce_scatter | solution.py:29
  42.8 230.2 %all-gather.11.cloned.1.call-start = ((), (), s32[]{:S(2)}) async-start(), calls=%async_computation.10 | async-start | bytes 3145728 | tf_op jit(solution)/shard_map/all_gather | solution.py:33
  45.1 162.4 %copy-start.20 = (f32[1024,8]{0,1:T(8,128)}, f32[1024,8]{0,1:T(8,128)S(1)}, u32[]{:S(2)}) copy-start(f32[1024,8]{0,1:T(8,128)S(1)} %get-tuple-element.148) | copy-start | bytes 98308
  239.7 48.4 %reduce-scatter.11.cloned.1.call-start = ((), (), s32[]{:S(2)}) async-start(), calls=%async_computation.11 | async-start | bytes 3145728 | tf_op jit(solution)/shard_map/reduce_scatter | solution.py:23
  278.3 31.2 %all-gather.13.cloned.1.call-start = ((), (), s32[]{:S(2)}) async-start(), calls=%async_computation.12 | async-start | bytes 3145728 | tf_op jit(solution)/shard_map/all_gather | solution.py:19
  294.8 429.1 %copy-start.26 = (f32[512]{0:T(512)}, f32[512]{0:T(512)S(1)}, u32[]{:S(2)}) copy-start(f32[512]{0:T(512)S(1)} %get-tuple-element.151) | copy-start | bytes 6148
  294.8 429.1 %copy-start.28 = (f32[512]{0:T(512)}, f32[512]{0:T(512)S(1)}, u32[]{:S(2)}) copy-start(f32[512]{0:T(512)S(1)} %get-tuple-element.152) | copy-start | bytes 6148
  297.6 30.4 %all-gather.17.cloned.1.call-start = ((), (), s32[]{:S(2)}) async-start(), calls=%async_computation.16 | async-start | bytes 3145728 | tf_op jit(solution)/shard_map/all_gather | solution.py:19
  298.2 164.2 %reduce-scatter.13.cloned.1.call-start = ((), (), s32[]{:S(2)}) async-start(), calls=%async_computation.13 | async-start | bytes 17301504 | tf_op jit(solution)/shard_map/reduce_scatter | solution.py:37
  327.9 208.3 %reduce-scatter.17.cloned.1.call-start = ((), (), s32[]{:S(2)}) async-start(), calls=%async_computation.17 | async-start | bytes 8650752 | tf_op jit(solution)/shard_map/reduce_scatter | solution.py:37
  339.0 348.0 %all-gather.19.cloned.1.call-start = ((), (), s32[]{:S(2)}) async-start(), calls=%async_computation.18 | async-start | bytes 17301504 | tf_op jit(solution)/shard_map/all_gather | solution.py:43
  547.1 168.6 %reduce-scatter.19.cloned.1.call-start = ((), (), s32[]{:S(2)}) async-start(), calls=%async_computation.19 | async-start | bytes 3145728 | tf_op jit(solution)/shard_map/reduce_scatter | solution.py:23
  705.9 33.8 %all-gather.21.cloned.1.call-start = ((), (), s32[]{:S(2)}) async-start(), calls=%async_computation.20 | async-start | bytes 3145728 | tf_op jit(solution)/shard_map/all_gather | solution.py:19
  727.8 73.5 %reduce-scatter.21.cloned.1.call-start = ((), (), s32[]{:S(2)}) async-start(), calls=%async_computation.21 | async-start | bytes 6291456 | tf_op jit(solution)/shard_map/reduce_scatter | solution.py:29
  745.7 202.6 %all-gather.23.cloned.1.call-start = ((), (), s32[]{:S(2)}) async-start(), calls=%async_computation.22 | async-start | bytes 9437184 | tf_op jit(solution)/shard_map/all_gather | solution.py:33
  867.8 156.4 %all-gather.15.cloned.1.call-start = ((), (), s32[]{:S(2)}) async-start(), calls=%async_computation.14 | async-start | bytes 8650752 | tf_op jit(solution)/shard_map/all_gather | solution.py:43
  868.3 238.0 %reduce-scatter.23.cloned.1.call-start = ((), (), s32[]{:S(2)}) async-start(), calls=%async_computation.23 | async-start | bytes 3145728 | tf_op jit(solution)/shard_map/reduce_scatter | solution.py:23
  960.1 215.8 %reduce-scatter.15.cloned.1.call-start = ((), (), s32[]{:S(2)}) async-start(), calls=%async_computation.15 | async-start | bytes 3145728 | tf_op jit(solution)/shard_map/reduce_scatter | solution.py:23
  1035.0 811.5 %all-reduce.10.cloned.1.call-start = ((), (), s32[]{:S(2)}) async-start(), calls=%async_computation.24 | async-start | bytes 51380224 | tf_op jit(solution)/shard_map/psum | solution.py:283
  1078.5 97.4 %copy-start.6 = (bf16[512,1024]{1,0:T(8,128)(2,1)S(1)}, bf16[512,1024]{1,0:T(8,128)(2,1)}, u32[]{:S(2)}) copy-start(bf16[512,1024]{1,0:T(8,128)(2,1)} %reduce-scatter.11.cloned.1.call-done) | copy-start | bytes 3145732
  1078.5 97.4 %copy-start.7 = (bf16[512,1024]{1,0:T(8,128)(2,1)S(1)}, bf16[512,1024]{1,0:T(8,128)(2,1)}, u32[]{:S(2)}) copy-start(bf16[512,1024]{1,0:T(8,128)(2,1)} %param.35) | copy-start | bytes 3145732
  1078.5 97.4 %copy-start.25 = (f32[1024]{0:T(1024)S(1)}, f32[1024]{0:T(1024)}, u32[]{:S(2)}) copy-start(f32[1024]{0:T(1024)} %param.31) | copy-start | bytes 12292
  (48 other events, 1024.0 us)
Sparse Core Ops, SparseCore 0:
  18.2 12.3 all-gather.8
  42.9 145.6 reduce-scatter.8
  239.8 33.1 all-gather.10
  278.5 9.6 reduce-scatter.10
  297.7 11.7 all-gather.12
  311.0 11.7 all-gather.16
  328.0 134.3 reduce-scatter.12
  464.8 71.3 reduce-scatter.16
  547.2 139.6 all-gather.18
  706.1 9.6 reduce-scatter.18
  727.9 11.7 all-gather.20
  745.8 55.4 reduce-scatter.20
  867.9 80.3 all-gather.22
  949.7 74.4 all-gather.14
  1026.9 9.6 reduce-scatter.22
  1039.3 10.7 reduce-scatter.14
  1078.5 767.9 all-reduce.9
where the time goes:
time: 1900 us; the launch traced here: 1890 us
  waiting for transfers between devices  1430 us (75%)
  matrix products  193 us (10%)
  other arithmetic  112 us (6%)
  blocking collectives  106 us (6%)
  local copies, waits for them, and re-layouts  40.3 us (2%)
    psum x1, waiting for transfers between devices, local(): lax.psum(gate_up_grad.astype(jnp.bfloat16), 'dp').astype(jnp.float32)  666 us
    all_gather x2, waiting for transfers between devices, hidden_gather(): return lax.all_gather(values, 'row', axis=0, tiled=True)  204 us
    reduce_scatter x2, waiting for transfers between devices, head_sum(): return lax.psum_scatter(values, 'row', scatter_dimension=2, tiled=True)  198 us
    reduce_scatter x2, waiting for transfers between devices, hidden_sum(): lax.psum_scatter(values.astype(jnp.bfloat16), 'row', scatter_dimension=0,...  189 us
    all_gather x2, waiting for transfers between devices, head_gather(): return lax.all_gather(values, 'row', axis=2, tiled=True)  113 us
    psum x1, blocking collectives, local(): lax.psum((ln1_gain_grad, ln1_bias_grad, ln2_gain_grad, ln2_bias_grad), ('...  62.4 us
  transfers between devices with their start and end apart: 17, of which 14 were waited for; matrix products, arithmetic and copies ran while one was open for 6% of the time, Pallas kernels for 0%

commit v1 on v0

v1 whole, which is shorter than its diff:
```python
import math

import jax
import jax.numpy as jnp
from jax import lax
from jax.sharding import PartitionSpec as P

HEAD = 64
ROT = 16
EPSILON = 1e-05
ROPE_BASE = 10000.0
NEGATIVE = -1e30
BF = jnp.bfloat16
F32 = jnp.float32
SWAP = [(0, 1), (1, 0)]


def swap(v, axis):
    return lax.ppermute(v, axis, SWAP)


def ordered(flag, mine, other, axis=0):
    first = jnp.where(flag == 0, mine, other)
    second = jnp.where(flag == 0, other, mine)
    return jnp.concatenate([first, second], axis=axis)


def piece(v, index, count, axis=0):
    size = v.shape[axis] // count
    return lax.dynamic_slice_in_dim(v, index * size, size, axis)


def add(a, b):
    return (a.astype(F32) + b.astype(F32)).astype(BF)


def dot(a, b):
    return jnp.dot(a, b, preferred_element_type=F32)


def dot_t(a, b):
    return lax.dot_general(a, b, (((1,), (1,)), ((), ())), preferred_element_type=F32)


def t_dot(a, b):
    return lax.dot_general(a, b, (((0,), (0,)), ((), ())), preferred_element_type=F32)


class Place:
    def __init__(self):
        self.r = lax.axis_index("row")
        self.c = lax.axis_index("col")
        self.d = lax.axis_index("dp")
        self.count = lax.axis_size("dp")
        self.y = lax.rem(self.d, 2)
        self.zp = lax.rem(self.d // 2, 2)
        self.z = self.d // 2
        self.mid = (self.z == 1) | (self.z == 2)
        self.upper = (self.z >= 2).astype(jnp.int32)


def dp_perm(bit, count):
    return [(i, i ^ bit) for i in range(count)]


def fetch(send, place, y_first):
    count = place.count
    if count % 4:
        return swap(send, "row")
    if y_first:
        index = place.zp * 2 + place.y
        steps = ((1, place.y), (2, place.zp))
    else:
        index = place.y * 2 + place.zp
        steps = ((2, place.zp), (1, place.y))
    held = swap(piece(send, index, 4), "row")
    for bit, flag in steps:
        other = lax.ppermute(held, "dp", dp_perm(bit, count))
        held = ordered(flag, held, other)
    return held


def cross(v):
    half = v.shape[-1] // 2
    return jnp.concatenate([v[..., half:], v[..., :half]], axis=-1)


def gather_blocks(block, place):
    other = cross(swap(block, "row"))
    pair = ordered(place.r, block, other)
    rest = swap(pair, "col")
    return ordered(place.c, pair, rest)


def reduce_blocks(partial, place):
    kept = piece(partial, place.c, 2)
    got = swap(piece(partial, 1 - place.c, 2), "col")
    held = add(kept, got)
    kept = piece(held, place.r, 2)
    got = cross(swap(piece(held, 1 - place.r, 2), "row"))
    return kept.astype(F32) + got.astype(F32)


def norm_forward(values, gain, shift):
    count = values.shape[-1]
    mean = jnp.sum(values, axis=-1, keepdims=True) / count
    spread = jnp.sum(values * values, axis=-1, keepdims=True) / count - mean * mean
    inverse = lax.rsqrt(spread + EPSILON)
    normal = (values - mean) * inverse
    return normal * gain + shift, normal, inverse


def norm_backward(grad, normal, inverse, gain):
    count = grad.shape[-1]
    scaled = grad * gain
    first = jnp.sum(scaled, axis=-1, keepdims=True) / count
    second = jnp.sum(scaled * normal, axis=-1, keepdims=True) / count
    grad_input = inverse * (scaled - first - normal * second)
    return grad_input, jnp.sum(grad * normal, axis=0), jnp.sum(grad, axis=0)


def doc_positions(segment_ids):
    places = jnp.arange(segment_ids.shape[0], dtype=jnp.int32)
    starts = jnp.concatenate([jnp.ones((1,), dtype=bool), segment_ids[1:] != segment_ids[:-1]])
    first_place = lax.cummax(jnp.where(starts, places, jnp.zeros_like(places)), axis=0)
    return places - first_place


def rotary_tables(segment_ids):
    places = doc_positions(segment_ids).astype(F32)
    freq_index = jnp.arange(ROT // 2, dtype=F32)
    inverse = jnp.exp(freq_index * (-2.0 / ROT) * math.log(ROPE_BASE))
    angles = places[:, None] * inverse[None, :]
    return (jnp.cos(angles)[:, None, :], jnp.sin(angles)[:, None, :])


def rotary(head_rows, cosines, sines):
    half_rot = ROT // 2
    first_half = head_rows[..., :half_rot]
    second_half = head_rows[..., half_rot:ROT]
    return jnp.concatenate(
        [
            first_half * cosines - second_half * sines,
            second_half * cosines + first_half * sines,
            head_rows[..., ROT:],
        ],
        axis=-1,
    )


def score_block(query_rows, key_rows, query_ids, key_ids, begin_row, factor):
    scores = (
        jnp.einsum("qhd,khd->hqk", query_rows, key_rows, preferred_element_type=F32) * factor
    )
    query_places = begin_row + jnp.arange(query_rows.shape[0], dtype=jnp.int32)
    key_places = jnp.arange(key_rows.shape[0], dtype=jnp.int32)
    allowed = (query_ids[:, None] == key_ids[None, :]) & (
        key_places[None, :] <= query_places[:, None]
    )
    return jnp.where(allowed[None], scores, NEGATIVE)


def attention_forward(queries, keys, values, ids, factor):
    length = ids.shape[0]
    rows = min(512, length)
    outs, logs = [], []
    for begin in range(0, length, rows):
        end = begin + rows
        scores = score_block(queries[begin:end], keys[:end], ids[begin:end], ids[:end], begin, factor)
        maxima = jnp.max(scores, axis=-1, keepdims=True)
        shifted = jnp.exp(scores - maxima)
        totals = jnp.sum(shifted, axis=-1, keepdims=True)
        weights = (shifted / totals).astype(BF)
        outs.append(
            jnp.einsum("hqk,khd->qhd", weights, values[:end], preferred_element_type=F32)
        )
        logs.append(maxima + jnp.log(totals))
    return jnp.concatenate(outs, axis=0).astype(BF), logs


def attention_backward(queries, keys, values, grads, logs, ids, factor):
    length = ids.shape[0]
    rows = min(512, length)
    grad_queries = []
    grad_keys = jnp.zeros(keys.shape, F32)
    grad_values = jnp.zeros(values.shape, F32)
    for index, begin in enumerate(range(0, length, rows)):
        end = begin + rows
        scores = score_block(queries[begin:end], keys[:end], ids[begin:end], ids[:end], begin, factor)
        weights = jnp.exp(scores - logs[index])
        block = grads[begin:end]
        grad_values = grad_values.at[:end].add(
            jnp.einsum("hqk,qhd->khd", weights.astype(BF), block, preferred_element_type=F32)
        )
        grad_weights = jnp.einsum("qhd,khd->hqk", block, values[:end], preferred_element_type=F32)
        grad_scores = (
            weights * (grad_weights - jnp.sum(weights * grad_weights, axis=-1, keepdims=True))
        ).astype(BF)
        grad_queries.append(
            jnp.einsum("hqk,khd->qhd", grad_scores, keys[:end], preferred_element_type=F32) * factor
        )
        grad_keys = grad_keys.at[:end].add(
            jnp.einsum("hqk,qhd->khd", grad_scores, queries[begin:end], preferred_element_type=F32)
            * factor
        )
    return jnp.concatenate(grad_queries, axis=0), grad_keys, grad_values


class Reducer:
    def __init__(self, place):
        self.place = place
        both = [(2 * i, 2 * i + 1) for i in range(8)]
        middle = [(2, 4), (4, 2), (3, 5), (5, 3)]
        outer = [pair for i in (0, 1, 6, 7) for pair in (both[i], both[i][::-1])]
        self.middle = outer + [(2 * i + k, 2 * j + k) for i, j in middle for k in (0, 1)]
        self.middle_y = outer + [
            (2 * i + k, 2 * (i ^ 1) + k) for i in (2, 3, 4, 5) for k in (0, 1)
        ]
        self.inward = [(0, 2), (1, 3), (6, 4), (7, 5)]
        self.outward = [(j, i) for i, j in self.inward]

    def along_y(self, v):
        return lax.ppermute(v, "dp", dp_perm(1, 8))

    def centre(self, v):
        return lax.ppermute(v, ("dp", "col"), self.middle)

    def centre_y(self, v):
        return lax.ppermute(v, ("dp", "col"), self.middle_y)

    def edge(self, inward, outward):
        mid = self.place.mid
        if outward is None:
            return lax.ppermute(inward, "dp", self.inward)
        if inward is None:
            return lax.ppermute(outward, "dp", self.outward)
        return lax.ppermute(jnp.where(mid, outward, inward), "dp", dp_perm(2, 8))

    def line(self, raws, centre):
        count = len(raws)
        totals, outs = [None] * count, [None] * count
        for step in range(count + 2):
            raw = raws[step] if step < count else None
            done = totals[step - 2] if step >= 2 else None
            got = self.edge(raw, done)
            if raw is not None:
                totals[step] = centre(add(raw, got))
            if done is not None:
                outs[step - 2] = jnp.where(self.place.mid, done, got)
        return outs

    def wide(self, chunks):
        y = self.place.y

        def centre(v):
            return add(v, self.centre(v))

        raws = [add(piece(v, y, 2), self.along_y(piece(v, 1 - y, 2))) for v in chunks]
        outs = self.line(raws, centre)
        return [ordered(y, v, self.along_y(v)) for v in outs]

    def deep(self, chunks):
        upper = self.place.upper

        def centre(v):
            held = add(piece(v, upper, 2), self.centre(piece(v, 1 - upper, 2)))
            held = add(held, self.centre_y(held))
            return ordered(upper, held, self.centre(held))

        return self.line(list(chunks), centre)


def reduce_dp(place, arrays, kind, parts):
    if place.count != 8:
        return [lax.psum(v, "dp") for v in arrays]
    reducer = Reducer(place)
    chunks = [v for a in arrays for v in jnp.split(a, parts)]
    outs = getattr(reducer, kind)(chunks)
    return [jnp.concatenate(outs[i * parts : (i + 1) * parts]) for i in range(len(arrays))]


def local(
    tokens,
    segments,
    ln1_gain,
    ln1_bias,
    qkv_weight,
    qkv_bias,
    out_weight,
    ln2_gain,
    ln2_bias,
    gate_up_weight,
    down_weight,
    cotangent,
):
    place = Place()
    r, c = place.r, place.c
    ids = segments[0]
    length = ids.shape[0]
    factor = HEAD ** (-0.5)
    half = qkv_weight.shape[0]
    units = qkv_weight.shape[2] // 2
    heads = units // HEAD
    hidden = gate_up_weight.shape[2] // 2

    qkv_flat = [qkv_weight[:, k] for k in range(3)]
    qkv_own = jnp.concatenate([piece(w, r, 2, 1) for w in qkv_flat], axis=1)
    qkv_send = jnp.concatenate([piece(w, 1 - r, 2, 1) for w in qkv_flat], axis=1)
    w_qkv = jnp.concatenate([qkv_own, fetch(qkv_send, place, False)], axis=0)

    other = swap(tokens, "row")
    mine = jnp.concatenate([tokens, other], axis=1)
    tokens_all = ordered(c, mine, swap(mine, "col"))
    params = jnp.stack([ln1_gain, ln1_bias, ln2_gain, ln2_bias])
    params = jnp.concatenate([params, swap(params, "row")], axis=1)

    w_out = jnp.concatenate(
        [piece(out_weight, r, 2), fetch(piece(out_weight, 1 - r, 2), place, True)], axis=1
    )
    gate_flat = [gate_up_weight[:, k] for k in range(2)]
    gate_own = jnp.concatenate([piece(w, r, 2, 1) for w in gate_flat], axis=1)
    gate_send = jnp.concatenate([piece(w, 1 - r, 2, 1) for w in gate_flat], axis=1)
    w_gate = jnp.concatenate([gate_own, fetch(gate_send, place, True)], axis=0)
    cot_other = swap(cotangent, "row")
    cot_mine = jnp.concatenate([cotangent, cot_other], axis=1)
    cot_all = ordered(c, cot_mine, swap(cot_mine, "col"))
    w_down = jnp.concatenate(
        [piece(down_weight, r, 2), fetch(piece(down_weight, 1 - r, 2), place, False)], axis=1
    )

    cosines, sines = rotary_tables(ids)
    inputs = tokens_all.astype(F32)
    normed, _, _ = norm_forward(inputs, params[0], params[1])
    act_one = normed.astype(BF)
    joined = dot(act_one, w_qkv).reshape(length, 3, heads, HEAD)
    joined = joined + piece(qkv_bias, r, 2, 1).reshape(3, heads, HEAD)
    queries = rotary(joined[:, 0], cosines, sines).astype(BF)
    keys = rotary(joined[:, 1], cosines, sines).astype(BF)
    values = joined[:, 2].astype(BF)
    attended, logs = attention_forward(queries, keys, values, ids, factor)
    attended = attended.reshape(length, units)
    block = c * 2 + r
    own_inputs = piece(tokens_all, block, 4).astype(F32)
    branch = reduce_blocks(dot(attended, w_out).astype(BF), place)
    hidden_state = own_inputs + branch
    normed, normal_two, inverse_two = norm_forward(hidden_state, params[2], params[3])
    act_two = gather_blocks(normed.astype(BF), place)
    gate_up = dot(act_two, w_gate)
    gate, up = gate_up[:, :hidden], gate_up[:, hidden:]
    inner = (jax.nn.silu(gate) * up).astype(BF)

    def exchanged(own, other):
        return own, swap(other, "row")

    down_grads = exchanged(
        t_dot(inner, cot_all[:, :half]).astype(BF), t_dot(inner, cot_all[:, half:]).astype(BF)
    )
    feed = reduce_blocks(dot(inner, w_down).astype(BF), place)
    result = (hidden_state + feed).astype(BF)
    result = ordered(r, result[:, :half], swap(result[:, half:], "row"))

    grad_inner = dot_t(cot_all, w_down)
    rate = 1.0 / (1.0 + jnp.exp(-gate))
    silu = gate * rate
    grad_gate = (grad_inner * up * (rate * (1.0 + gate * (1.0 - rate)))).astype(BF)
    grad_up = (grad_inner * silu).astype(BF)
    grad_pair = jnp.concatenate([grad_gate, grad_up], axis=1)
    grad_act_two = reduce_blocks(dot_t(grad_pair, w_gate).astype(BF), place)
    gate_grads = [
        exchanged(t_dot(act_two[:, :half], g).astype(BF), t_dot(act_two[:, half:], g).astype(BF))
        for g in (grad_gate, grad_up)
    ]
    grad_norm, ln2_gain_grad, ln2_bias_grad = norm_backward(
        grad_act_two, normal_two, inverse_two, params[2]
    )
    own_cot = piece(cot_all, block, 4).astype(F32)
    grad_hidden = own_cot + grad_norm
    grad_branch = gather_blocks(grad_hidden.astype(BF), place)
    grad_attended = dot_t(grad_branch, w_out).astype(BF).reshape(length, heads, HEAD)
    out_grads = exchanged(
        t_dot(attended, grad_branch[:, :half]).astype(BF),
        t_dot(attended, grad_branch[:, half:]).astype(BF),
    )
    grad_queries, grad_keys, grad_values = attention_backward(
        queries, keys, values, grad_attended, logs, ids, factor
    )
    grad_joined = jnp.stack(
        [rotary(grad_queries, cosines, -sines), rotary(grad_keys, cosines, -sines), grad_values],
        axis=1,
    )
    grad_joined = grad_joined.reshape(length, 3 * units).astype(BF)
    qkv_grads = exchanged(
        t_dot(act_one[:, :half], grad_joined).astype(BF),
        t_dot(act_one[:, half:], grad_joined).astype(BF),
    )
    bias_grad = jnp.sum(grad_joined, axis=0, dtype=F32)
    grad_act_one = reduce_blocks(dot_t(grad_joined, w_qkv).astype(BF), place)
    _, normal_one, inverse_one = norm_forward(own_inputs, params[0], params[1])
    grad_norm, ln1_gain_grad, ln1_bias_grad = norm_backward(
        grad_act_one, normal_one, inverse_one, params[0]
    )
    input_grad = grad_hidden + grad_norm
    input_grad = ordered(r, input_grad[:, :half], swap(input_grad[:, half:], "row"))

    small = jnp.stack([ln1_gain_grad, ln1_bias_grad, ln2_gain_grad, ln2_bias_grad])
    small = small[:, :half] + swap(small[:, half:], "row")
    small = small + swap(small, "col")
    bias_grad = bias_grad.reshape(3, units)
    small = jnp.concatenate([small.reshape(-1), bias_grad.reshape(-1)])
    if place.count == 8:
        for bit in (1, 2, 4):
            small = small + lax.ppermute(small, "dp", dp_perm(bit, 8))
    else:
        small = lax.psum(small, "dp")
    norms = small[: 4 * half].reshape(4, half)
    bias_grad = small[4 * half :].reshape(3, units)
    bias_grad = ordered(r, bias_grad, swap(bias_grad, "row"), 1)

    down_own, down_got = reduce_dp(place, down_grads, "deep", 4)
    gate_own, gate_got, up_own, up_got = reduce_dp(
        place, gate_grads[0] + gate_grads[1], "wide", 2
    )
    out_own, out_got = reduce_dp(place, out_grads, "deep", 2)
    qkv_own, qkv_got = reduce_dp(place, qkv_grads, "deep", 4)

    down_grad = ordered(r, down_own, down_got).astype(F32)
    out_grad = ordered(r, out_own, out_got).astype(F32)
    gate_up_grad = jnp.stack(
        [ordered(r, gate_own, gate_got, 1), ordered(r, up_own, up_got, 1)], axis=1
    ).astype(F32)
    qkv_grad = jnp.concatenate(
        [
            ordered(r, qkv_own.reshape(half, 3, units), qkv_got.reshape(half, 3, units), 2),
        ],
        axis=2,
    ).astype(F32)
    return (
        result,
        input_grad,
        norms[0],
        norms[1],
        qkv_grad,
        bias_grad,
        out_grad,
        norms[2],
        norms[3],
        gate_up_grad,
        down_grad,
    )


def solution(mesh):
    in_specs = (
        P(("dp", "col"), "row"),
        P("dp", None),
        P("row"),
        P("row"),
        P("row", None, "col"),
        P(None, "col"),
        P("col", "row"),
        P("row"),
        P("row"),
        P("row", None, "col"),
        P("col", "row"),
        P(("dp", "col"), "row"),
    )
    out_specs = (
        P(("dp", "col"), "row"),
        P(("dp", "col"), "row"),
        P("row"),
        P("row"),
        P("row", None, "col"),
        P(None, "col"),
        P("col", "row"),
        P("row"),
        P("row"),
        P("row", None, "col"),
        P("col", "row"),
    )
    return jax.shard_map(local, mesh=mesh, in_specs=in_specs, out_specs=out_specs, check_vma=False)
```

time: 1900 us -> 1710 us (0.900)
  waiting for transfers between devices: 1430 us -> 786 us
  starting transfers between devices: 1.28 us -> 314 us
  local copies, waits for them, and re-layouts: 40.3 us -> 182 us
  blocking collectives: 106 us -> 0 us
  other arithmetic: 112 us -> 204 us
    ppermute x0 -> x162, waiting for transfers between devices: none -> 786 us  [the longest x31 235 us: swap(): return lax.ppermute(v, axis, SWAP)]
    psum x1 -> x0, waiting for transfers between devices: 666 us -> none  [local(): lax.psum(gate_up_grad.astype(jnp.bfloat16), 'dp').astype(jnp.float32)]
    reduce_scatter x8 -> x0, waiting for transfers between devices: 407 us -> none  [the longest x2 198 us: head_sum(): return lax.psum_scatter(values, 'row', scatter_dimension=2, tiled=True)]
    all_gather x8 -> x0, waiting for transfers between devices: 352 us -> none  [the longest x2 204 us: hidden_gather(): return lax.all_gather(values, 'row', axis=0, tiled=True)]
    ppermute x0 -> x162, starting transfers between devices: none -> 314 us  [the longest x20 158 us: edge(): return lax.ppermute(jnp.where(mid, outward, inward), 'dp', dp_perm(2, 8))]
    psum x6 -> x0, blocking collectives: 106 us -> none  [the longest x1 62.4 us: local(): lax.psum((ln1_gain_grad, ln1_bias_grad, ln2_gain_grad, ln2_bias_grad), ('...]
    select_n x0 -> x95, other arithmetic: none -> 95 us  [the longest x50 58.7 us: ordered(): first = jnp.where(flag == 0, mine, other)]
    unnamed x111 -> x349, local copies, waits for them, and re-layouts: 27.2 us -> 83.6 us
  transfers between devices with their start and end apart: 17 -> 162, of which waited for: 14 -> 82; matrix products, arithmetic and copies ran while one was open for 6% -> 23% of each run, Pallas kernels for 0% -> 0%
where the time goes in v1:
time: 1710 us; the launch traced here: 1690 us
  waiting for transfers between devices  786 us (46%)
  starting transfers between devices  314 us (18%)
  matrix products  205 us (12%)
  other arithmetic  204 us (12%)
  local copies, waits for them, and re-layouts  182 us (11%)
    ppermute x31, waiting for transfers between devices, swap(): return lax.ppermute(v, axis, SWAP)  235 us
    ppermute x20, waiting for transfers between devices, edge(): return lax.ppermute(jnp.where(mid, outward, inward), 'dp', dp_perm(2, 8))  197 us
    ppermute x20, starting transfers between devices, edge(): return lax.ppermute(jnp.where(mid, outward, inward), 'dp', dp_perm(2, 8))  158 us
    ppermute x16, waiting for transfers between devices, along_y(): return lax.ppermute(v, 'dp', dp_perm(1, 8))  125 us
    ppermute x8, waiting for transfers between devices, fetch(): other = lax.ppermute(held, 'dp', dp_perm(bit, count))  92.2 us
    unnamed x349, local copies, waits for them, and re-layouts  83.6 us
    dot_general x4, matrix products, dot_t(): lax.dot_general(a, b, (((1,), (1,)), ((), ())), preferred_element_type=F32)  65.5 us
    select_n x50, other arithmetic, ordered(): first = jnp.where(flag == 0, mine, other)  58.7 us
  transfers between devices with their start and end apart: 162, of which 82 were waited for; matrix products, arithmetic and copies ran while one was open for 23% of the time, Pallas kernels for 0%

profile of v1, /device:TPU:0, one launch (start us, length us, event | category | flops | bytes accessed | tf_op | source)
XLA Modules:
  0.0 1694.8 jit_solution(9179986256588644139)
XLA Ops:
  20.6 22.8 %fusion.114 = (bf16[1024,1,2816]{2,1,0:T(2,128)(2,1)}, bf16[1024,1,2816]{2,1,0:T(2,128)(2,1)}) fusion(bf16[1024,2,2816]{2,1,0:T(2,128)(2,1)} %param.33), kind=kLoop, calls=%fused_computation.570 | loop fusion | bytes 23068672 | tf_op jit(solution)/shard_map/slice | solution.py:320
  43.4 26.6 %constant_dynamic-slice_fusion.38 = (bf16[1024,1,1408]{2,1,0:T(2,128)(2,1)}, bf16[1024,1,1408]{2,1,0:T(2,128)(2,1)S(1)}, bf16[1024,1,1408]{2,1,0:T(2,128)(2,1)S(1)}, bf16[1024,1,1408]{2,1,0:T(2,128)(2,1)}) fusion(bf16[1024,1,2816]{2,1,0:T(2,128)(2,1)} %get-tuple-element.129, s32[]{:T(128)S(6)} %select_n.876, s32[]{:T(128)S(6)} %select_n.879, ...), kind=kLoop, calls=%fused_computation.514 | loop fusion | bytes 23068680 | tf_op jit(solution)/shard_map/dynamic_slice | solution.py:30
  123.7 26.8 %collective-permute-done.5 = bf16[512,1536]{1,0:T(8,128)(2,1)S(1)} collective-permute-done((bf16[512,1536]{1,0:T(8,128)(2,1)S(1)}, bf16[512,1536]{1,0:T(8,128)(2,1)S(1)}, u32[]{:S(2)}, u32[]{:S(2)}) %collective-permute-start.5) | collective-permute-done | bytes 1572896 | tf_op jit(solution)/shard_map/ppermute | solution.py:78
  197.4 45.4 %collective-permute-done.16 = bf16[352,1024]{1,0:T(8,128)(2,1)} collective-permute-done((bf16[352,1024]{1,0:T(8,128)(2,1)S(1)}, bf16[352,1024]{1,0:T(8,128)(2,1)}, u32[]{:S(2)}, u32[]{:S(2)}) %collective-permute-start.16) | collective-permute-done | bytes 720928 | tf_op jit(solution)/shard_map/ppermute | solution.py:19
  246.6 17.4 %collective-permute-done.22 = bf16[512,1024]{1,0:T(8,128)(2,1)} collective-permute-done((bf16[512,1024]{1,0:T(8,128)(2,1)}, bf16[512,1024]{1,0:T(8,128)(2,1)}, u32[]{:S(2)}, u32[]{:S(2)}) %collective-permute-start.22) | collective-permute-done | bytes 1048608 | tf_op jit(solution)/shard_map/ppermute | solution.py:19
  331.2 33.0 %collective-permute-done.15 = bf16[512,2816]{1,0:T(8,128)(2,1)} collective-permute-done((bf16[512,2816]{1,0:T(8,128)(2,1)}, bf16[512,2816]{1,0:T(8,128)(2,1)}, u32[]{:S(2)}, u32[]{:S(2)}) %collective-permute-start.15) | collective-permute-done | bytes 2883616 | tf_op jit(solution)/shard_map/ppermute | solution.py:78
  371.9 20.2 %fusion.19 = f32[1024,2816]{1,0:T(8,128)} fusion(bf16[512,2048]{1,0:T(8,128)(2,1)} %get-tuple-element.151, bf16[512,2048]{1,0:T(8,128)(2,1)} %get-tuple-element.150, bf16[512,2816]{1,0:T(8,128)(2,1)} %get-tuple-element.145, bf16[512,2816]{1,0:T(8,128)(2,1)} %get-tuple-element.144, bf16[1024,1408]{1,0:T(8,128)(2,1)} %bitcast.138, ...), kind=kOutput, calls=%fused_computation.69 | convolution fusion | flops 11865686016 | bytes 27262976 | tf_op jit(solution)/shard_map/dot_general | solution.py:38
  392.1 17.6 %multiply_convert_fusion.3 = (bf16[1024,1408]{1,0:T(8,128)(2,1)}, bf16[1024,1408]{1,0:T(8,128)(2,1)}, bf16[1024,1408]{1,0:T(8,128)(2,1)}) fusion(f32[1024,2816]{1,0:T(8,128)} %fusion.19, bf16[704,1024]{1,0:T(8,128)(2,1)} %get-tuple-element.183, bf16[704,1024]{1,0:T(8,128)(2,1)S(1)} %copy-done.94, bf16[1408,1024]{1,0:T(8,128)(2,1)} %constant_dynamic-slice_fusion.35, ...), kind=kOutput, calls=%fused_computation.51 | convolution fusion | flops 5952897024 | bytes 30146560 | tf_op jit(solution)/shard_map/dot_general | solution.py:42
  422.2 20.3 %fusion.25 = bf16[1024,2048]{1,0:T(8,128)(2,1)} fusion(bf16[1024,1408]{1,0:T(8,128)(2,1)} %get-tuple-element.123, bf16[1024,1408]{1,0:T(8,128)(2,1)} %get-tuple-element.122, bf16[512,2816]{1,0:T(8,128)(2,1)} %get-tuple-element.145, bf16[512,2816]{1,0:T(8,128)(2,1)} %get-tuple-element.144, bf16[1024,1408]{1,0:T(8,128)(2,1)} %bitcast.139, ...), kind=kOutput, calls=%fused_computation.79 | convolution fusion | flops 11870928896 | bytes 21495808 | tf_op jit(solution)/shard_map/dot_general | solution.py:42
  581.6 26.7 %collective-permute-done.113 = bf16[1024,1408]{1,0:T(8,128)(2,1)S(1)} collective-permute-done((bf16[1024,1408]{1,0:T(8,128)(2,1)}, bf16[1024,1408]{1,0:T(8,128)(2,1)S(1)}, u32[]{:S(2)}, u32[]{:S(2)}) %collective-permute-start.113) | collective-permute-done | bytes 2883616 | tf_op jit(solution)/shard_map/ppermute | solution.py:19
  613.6 78.9 %collective-permute-done.25 = bf16[256,2048]{1,0:T(8,128)(2,1)S(1)} collective-permute-done((bf16[256,2048]{1,0:T(8,128)(2,1)S(1)}, bf16[256,2048]{1,0:T(8,128)(2,1)S(1)}, u32[]{:S(2)}, u32[]{:S(2)}) %collective-permute-start.25) | collective-permute-done | bytes 1048608 | tf_op jit(solution)/shard_map/ppermute | solution.py:19
  694.3 19.9 %collective-permute-done.20 = bf16[256,2048]{1,0:T(8,128)(2,1)S(1)} collective-permute-done((bf16[256,2048]{1,0:T(8,128)(2,1)S(1)}, bf16[256,2048]{1,0:T(8,128)(2,1)S(1)}, u32[]{:S(2)}, u32[]{:S(2)}) %collective-permute-start.20) | collective-permute-done | bytes 1048608 | tf_op jit(solution)/shard_map/ppermute | solution.py:19
  741.6 25.7 %collective-permute-done.95 = bf16[256,1408]{1,0:T(8,128)(2,1)S(1)} collective-permute-done((bf16[256,1408]{1,0:T(8,128)(2,1)S(1)}, bf16[256,1408]{1,0:T(8,128)(2,1)S(1)}, u32[]{:S(2)}, u32[]{:S(2)}) %collective-permute-start.95) | collective-permute-done | bytes 720928 | tf_op jit(solution)/shard_map/ppermute | solution.py:223
  791.9 28.6 %collective-permute-done.141 = bf16[352,1024]{1,0:T(8,128)(2,1)S(1)} collective-permute-done((bf16[352,1024]{1,0:T(8,128)(2,1)S(1)}, bf16[352,1024]{1,0:T(8,128)(2,1)S(1)}, u32[]{:S(2)}, u32[]{:S(2)}) %collective-permute-start.141) | collective-permute-done | bytes 720928 | tf_op jit(solution)/shard_map/ppermute | solution.py:237
  838.6 30.1 %collective-permute-done.97 = bf16[256,1408]{1,0:T(8,128)(2,1)S(1)} collective-permute-done((bf16[256,1408]{1,0:T(8,128)(2,1)S(1)}, bf16[256,1408]{1,0:T(8,128)(2,1)S(1)}, u32[]{:S(2)}, u32[]{:S(2)}) %collective-permute-start.97) | collective-permute-done | bytes 720928 | tf_op jit(solution)/shard_map/ppermute | solution.py:223
  878.1 23.0 %collective-permute-start.110 = (bf16[256,1408]{1,0:T(8,128)(2,1)S(1)}, bf16[256,1408]{1,0:T(8,128)(2,1)S(1)}, u32[]{:S(2)}, u32[]{:S(2)}) collective-permute-start(bf16[256,1408]{1,0:T(8,128)(2,1)S(1)} %broadcast_select_fusion.67), channel_id=1, source_target_pairs={{0,8},{4,12},{8,0},{12,4},{16,24},{20,28},{24,16},{28,20},{1,9},{5... | collective-permute-start | bytes 2162696 | tf_op jit(solution)/shard_map/ppermute | solution.py:237
  1028.2 25.3 %convolution_convert_fusion = bf16[1024,2048]{1,0:T(8,128)(2,1)} fusion(bf16[1024,1536]{0,1:T(8,128)(2,1)S(1)} %bitcast.135, bf16[512,1536]{1,0:T(8,128)(2,1)S(1)} %copy-done.93, bf16[512,1536]{1,0:T(8,128)(2,1)S(1)} %copy-done.92, bf16[1024,512]{1,0:T(8,128)(2,1)S(1)} %copy-done.101, bf16[1024,512]{1,0:T(8,128)(2,1)S(1)} %copy-done.102, ...), kind=kOutput, calls=%fused_computation.78 | convolution fusion | flops 6476005376 | bytes 13631488 | tf_op jit(solution)/shard_map/dot_general | solution.py:42
  1170.8 19.9 %collective-permute-done.76 = bf16[512,1024]{1,0:T(8,128)(2,1)S(1)} collective-permute-done((bf16[512,1024]{1,0:T(8,128)(2,1)S(1)}, bf16[512,1024]{1,0:T(8,128)(2,1)S(1)}, u32[]{:S(2)}, u32[]{:S(2)}) %collective-permute-start.76) | collective-permute-done | bytes 1048608 | tf_op jit(solution)/shard_map/ppermute | solution.py:19
  1270.7 16.7 collective-permute-done.82
  1384.9 38.8 %copy.41 = f32[1024,2,2816]{2,1,0:T(2,128)} copy(f32[1024,2,2816]{2,0,1:T(8,128)} %maximum_convert_fusion) | data formatting | bytes 46137344
  1441.2 24.1 %collective-permute-start.34 = (f32[5632]{0:T(1024)S(1)}, f32[5632]{0:T(1024)S(1)}, u32[]{:S(2)}, u32[]{:S(2)}) collective-permute-start(f32[5632]{0:T(1024)S(1)} %add.637), channel_id=1, source_target_pairs={{0,8},{4,12},{8,0},{12,4},{16,24},{20,28},{24,16},{28,20},{1,9},{5... | collective-permute-start | bytes 67592 | tf_op jit(solution)/shard_map/ppermute | solution.py:412
  1528.3 24.1 %collective-permute-start.58 = (bf16[256,1536]{1,0:T(8,128)(2,1)}, bf16[256,1536]{1,0:T(8,128)(2,1)S(1)}, u32[]{:S(2)}, u32[]{:S(2)}) collective-permute-start(bf16[256,1536]{1,0:T(8,128)(2,1)} %get-tuple-element.156), channel_id=1, source_target_pairs={{0,8},{4,12},{8,0},{12,4},{16,24},{20,28},{24,16},{28,20},{1,9},{5... | collective-permute-start | bytes 2359304 | tf_op jit(solution)/shard_map/ppermute | solution.py:237
  1584.8 22.8 %collective-permute-start.62 = (bf16[256,1536]{1,0:T(8,128)(2,1)S(1)}, bf16[256,1536]{1,0:T(8,128)(2,1)S(1)}, u32[]{:S(2)}, u32[]{:S(2)}) collective-permute-start(bf16[256,1536]{1,0:T(8,128)(2,1)S(1)} %broadcast_select_fusion.33), channel_id=1, source_target_pairs={{0,8},{4,12},{8,0},{12,4},{16,24},{20,28},{24,16},{28,20},{1,9},{5... | collective-permute-start | bytes 2359304 | tf_op jit(solution)/shard_map/ppermute | solution.py:237
  1626.2 27.0 %collective-permute-done.66 = bf16[256,1536]{1,0:T(8,128)(2,1)S(1)} collective-permute-done((bf16[256,1536]{1,0:T(8,128)(2,1)S(1)}, bf16[256,1536]{1,0:T(8,128)(2,1)S(1)}, u32[]{:S(2)}, u32[]{:S(2)}) %collective-permute-start.66) | collective-permute-done | bytes 786464 | tf_op jit(solution)/shard_map/ppermute | solution.py:236
  (999 shorter events, 1028.2 us)
Async XLA Ops:
  2.3 76.0 %collective-permute-start.6 = (bf16[128,1024]{1,0:T(8,128)(2,1)S(1)}, bf16[128,1024]{1,0:T(8,128)(2,1)}, u32[]{:S(2)}, u32[]{:S(2)}) collective-permute-start(bf16[128,1024]{1,0:T(8,128)(2,1)S(1)} %constant_dynamic-slice_fusion.42), channel_id=1, source_target_pairs={{0,2},{2,0},{1,3},{3,1},{4,6},{6,4},{5,7},{7,5},{8,10},{10,8},{9,1... | collective-permute-start | bytes 786440 | tf_op jit(solution)/shard_map/ppermute | solution.py:19
  6.1 82.8 %collective-permute-start.2 = (f32[4,1024]{1,0:T(4,128)S(1)}, f32[4,1024]{1,0:T(4,128)S(1)}, u32[]{:S(2)}, u32[]{:S(2)}) collective-permute-start(f32[4,1024]{1,0:T(4,128)S(1)} %pad_maximum_fusion.68), channel_id=1, source_target_pairs={{0,2},{2,0},{1,3},{3,1},{4,6},{6,4},{5,7},{7,5},{8,10},{10,8},{9,1... | collective-permute-start | bytes 49160 | tf_op jit(solution)/shard_map/ppermute | solution.py:19
  191.8 75.9 %collective-permute-start.9 = (bf16[512,2048]{1,0:T(8,128)(2,1)}, bf16[512,2048]{1,0:T(8,128)(2,1)S(1)}, u32[]{:S(2)}, u32[]{:S(2)}) collective-permute-start(bf16[512,2048]{1,0:T(8,128)(2,1)} %constant_dynamic-slice_fusion.41), channel_id=1, source_target_pairs={{0,1},{1,0},{2,3},{3,2},{4,5},{5,4},{6,7},{7,6},{8,9},{9,8},{10,11... | collective-permute-start | bytes 6291464 | tf_op jit(solution)/shard_map/ppermute | solution.py:19
  478.3 75.7 %collective-permute-start.19 = (bf16[512,2048]{1,0:T(8,128)(2,1)}, bf16[512,2048]{1,0:T(8,128)(2,1)S(1)}, u32[]{:S(2)}, u32[]{:S(2)}) collective-permute-start(bf16[512,2048]{1,0:T(8,128)(2,1)} %constant_dynamic-slice_fusion.33), channel_id=1, source_target_pairs={{0,1},{1,0},{2,3},{3,2},{4,5},{5,4},{6,7},{7,6},{8,9},{9,8},{10,11... | collective-permute-start | bytes 6291464 | tf_op jit(solution)/shard_map/ppermute | solution.py:19
  481.1 99.7 %collective-permute-start.94 = (bf16[1024,1408]{1,0:T(8,128)(2,1)}, bf16[1024,1408]{1,0:T(8,128)(2,1)S(1)}, u32[]{:S(2)}, u32[]{:S(2)}) collective-permute-start(bf16[1024,1408]{1,0:T(8,128)(2,1)} %convolution_convert_fusion.7), channel_id=1, source_target_pairs={{0,2},{2,0},{1,3},{3,1},{4,6},{6,4},{5,7},{7,5},{8,10},{10,8},{9,1... | collective-permute-start | bytes 8650760 | tf_op jit(solution)/shard_map/ppermute | solution.py:19
  528.3 341.7 %collective-permute-start.109 = (bf16[256,1408]{1,0:T(8,128)(2,1)}, bf16[256,1408]{1,0:T(8,128)(2,1)S(1)}, u32[]{:S(2)}, u32[]{:S(2)}) collective-permute-start(bf16[256,1408]{1,0:T(8,128)(2,1)} %constant_dynamic-slice_fusion.10), channel_id=1, source_target_pairs={{0,4},{4,0},{8,12},{12,8},{16,20},{20,16},{24,28},{28,24},{1,5},{5... | collective-permute-start | bytes 2162696 | tf_op jit(solution)/shard_map/ppermute | solution.py:223
  569.5 169.7 %collective-permute-start.140 = (bf16[1408,1024]{1,0:T(8,128)(2,1)}, bf16[1408,1024]{1,0:T(8,128)(2,1)S(1)}, u32[]{:S(2)}, u32[]{:S(2)}) collective-permute-start(bf16[1408,1024]{1,0:T(8,128)(2,1)} %convolution_convert_fusion.3), channel_id=1, source_target_pairs={{0,2},{2,0},{1,3},{3,1},{4,6},{6,4},{5,7},{7,5},{8,10},{10,8},{9,1... | collective-permute-start | bytes 8650760 | tf_op jit(solution)/shard_map/ppermute | solution.py:19
  579.0 143.3 %collective-permute-start.100 = (bf16[256,1408]{1,0:T(8,128)(2,1)S(1)}, bf16[256,1408]{1,0:T(8,128)(2,1)S(1)}, u32[]{:S(2)}, u32[]{:S(2)}) collective-permute-start(bf16[256,1408]{1,0:T(8,128)(2,1)S(1)} %add_convert_fusion.40), channel_id=1, source_target_pairs={{0,1},{1,0},{4,5},{5,4},{24,25},{25,24},{28,29},{29,28},{8,16},{9,... | collective-permute-start | bytes 2162696 | tf_op jit(solution)/shard_map/ppermute | solution.py:226
  608.5 84.0 %collective-permute-start.25 = (bf16[256,2048]{1,0:T(8,128)(2,1)S(1)}, bf16[256,2048]{1,0:T(8,128)(2,1)S(1)}, u32[]{:S(2)}, u32[]{:S(2)}) collective-permute-start(bf16[256,2048]{1,0:T(8,128)(2,1)S(1)} %constant_dynamic-slice_fusion.30), channel_id=1, source_target_pairs={{0,2},{2,0},{1,3},{3,1},{4,6},{6,4},{5,7},{7,5},{8,10},{10,8},{9,1... | collective-permute-start | bytes 3145736 | tf_op jit(solution)/shard_map/ppermute | solution.py:19
  610.2 104.0 %collective-permute-start.20 = (bf16[256,2048]{1,0:T(8,128)(2,1)S(1)}, bf16[256,2048]{1,0:T(8,128)(2,1)S(1)}, u32[]{:S(2)}, u32[]{:S(2)}) collective-permute-start(bf16[256,2048]{1,0:T(8,128)(2,1)S(1)} %constant_dynamic-slice_fusion.32), channel_id=1, source_target_pairs={{0,2},{2,0},{1,3},{3,1},{4,6},{6,4},{5,7},{7,5},{8,10},{10,8},{9,1... | collective-permute-start | bytes 3145736 | tf_op jit(solution)/shard_map/ppermute | solution.py:19
  721.7 151.9 %collective-permute-start.105 = (bf16[256,1408]{1,0:T(8,128)(2,1)S(1)}, bf16[256,1408]{1,0:T(8,128)(2,1)S(1)}, u32[]{:S(2)}, u32[]{:S(2)}) collective-permute-start(bf16[256,1408]{1,0:T(8,128)(2,1)S(1)} %constant_dynamic-slice_fusion.11), channel_id=1, source_target_pairs={{0,4},{4,0},{8,12},{12,8},{16,20},{20,16},{24,28},{28,24},{1,5},{5... | collective-permute-start | bytes 2162696 | tf_op jit(solution)/shard_map/ppermute | solution.py:223
  835.0 247.5 %collective-permute-start.118 = (bf16[256,1408]{1,0:T(8,128)(2,1)}, bf16[256,1408]{1,0:T(8,128)(2,1)}, u32[]{:S(2)}, u32[]{:S(2)}) collective-permute-start(bf16[256,1408]{1,0:T(8,128)(2,1)} %constant_dynamic-slice_fusion.8), channel_id=1, source_target_pairs={{0,4},{4,0},{8,12},{12,8},{16,20},{20,16},{24,28},{28,24},{1,5},{5... | collective-permute-start | bytes 2162696 | tf_op jit(solution)/shard_map/ppermute | solution.py:223
  871.7 214.2 %collective-permute-start.114 = (bf16[256,1408]{1,0:T(8,128)(2,1)}, bf16[256,1408]{1,0:T(8,128)(2,1)}, u32[]{:S(2)}, u32[]{:S(2)}) collective-permute-start(bf16[256,1408]{1,0:T(8,128)(2,1)} %constant_dynamic-slice_fusion.9), channel_id=1, source_target_pairs={{0,4},{4,0},{8,12},{12,8},{16,20},{20,16},{24,28},{28,24},{1,5},{5... | collective-permute-start | bytes 2162696 | tf_op jit(solution)/shard_map/ppermute | solution.py:223
  873.4 94.6 %collective-permute-start.27 = (bf16[512,2048]{1,0:T(8,128)(2,1)S(1)}, bf16[512,2048]{1,0:T(8,128)(2,1)S(1)}, u32[]{:S(2)}, u32[]{:S(2)}) collective-permute-start(bf16[512,2048]{1,0:T(8,128)(2,1)S(1)} %pad_maximum_fusion.19), channel_id=1, source_target_pairs={{0,1},{1,0},{2,3},{3,2},{4,5},{5,4},{6,7},{7,6},{8,9},{9,8},{10,11... | collective-permute-start | bytes 6291464 | tf_op jit(solution)/shard_map/ppermute | solution.py:19
  949.1 133.8 %collective-permute-start.117 = (bf16[256,1408]{1,0:T(8,128)(2,1)}, bf16[256,1408]{1,0:T(8,128)(2,1)}, u32[]{:S(2)}, u32[]{:S(2)}) collective-permute-start(bf16[256,1408]{1,0:T(8,128)(2,1)} %add_convert_fusion.28), channel_id=1, source_target_pairs={{0,1},{1,0},{4,5},{5,4},{24,25},{25,24},{28,29},{29,28},{8,16},{9,... | collective-permute-start | bytes 2162696 | tf_op jit(solution)/shard_map/ppermute | solution.py:226
  963.2 108.5 %collective-permute-start.111 = (bf16[256,1408]{1,0:T(8,128)(2,1)}, bf16[256,1408]{1,0:T(8,128)(2,1)}, u32[]{:S(2)}, u32[]{:S(2)}) collective-permute-start(bf16[256,1408]{1,0:T(8,128)(2,1)} %broadcast_select_fusion.66), channel_id=1, source_target_pairs={{0,4},{4,0},{8,12},{12,8},{16,20},{20,16},{24,28},{28,24},{1,5},{5... | collective-permute-start | bytes 2162696 | tf_op jit(solution)/shard_map/ppermute | solution.py:223
  968.0 105.5 %collective-permute-start.107 = (bf16[256,1408]{1,0:T(8,128)(2,1)}, bf16[256,1408]{1,0:T(8,128)(2,1)}, u32[]{:S(2)}, u32[]{:S(2)}) collective-permute-start(bf16[256,1408]{1,0:T(8,128)(2,1)} %broadcast_select_fusion.68), channel_id=1, source_target_pairs={{0,4},{4,0},{8,12},{12,8},{16,20},{20,16},{24,28},{28,24},{1,5},{5... | collective-permute-start | bytes 2162696 | tf_op jit(solution)/shard_map/ppermute | solution.py:223
  1082.9 211.5 %collective-permute-start.28 = (bf16[512,2048]{1,0:T(8,128)(2,1)}, bf16[512,2048]{1,0:T(8,128)(2,1)}, u32[]{:S(2)}, u32[]{:S(2)}) collective-permute-start(bf16[512,2048]{1,0:T(8,128)(2,1)} %constant_dynamic-slice_fusion.29), channel_id=1, source_target_pairs={{0,1},{1,0},{2,3},{3,2},{4,5},{5,4},{6,7},{7,6},{8,9},{9,8},{10,11... | collective-permute-start | bytes 6291464 | tf_op jit(solution)/shard_map/ppermute | solution.py:19
  1098.3 381.0 %collective-permute-start.49 = (bf16[1024,1536]{1,0:T(8,128)(2,1)}, bf16[1024,1536]{1,0:T(8,128)(2,1)}, u32[]{:S(2)}, u32[]{:S(2)}) collective-permute-start(bf16[1024,1536]{1,0:T(8,128)(2,1)} %convolution_convert_fusion.9), channel_id=1, source_target_pairs={{0,2},{2,0},{1,3},{3,1},{4,6},{6,4},{5,7},{7,5},{8,10},{10,8},{9,1... | collective-permute-start | bytes 9437192 | tf_op jit(solution)/shard_map/ppermute | solution.py:19
  1325.8 97.9 %collective-permute-start.29 = (bf16[256,2048]{1,0:T(8,128)(2,1)}, bf16[256,2048]{1,0:T(8,128)(2,1)}, u32[]{:S(2)}, u32[]{:S(2)}) collective-permute-start(bf16[256,2048]{1,0:T(8,128)(2,1)} %constant_dynamic-slice_fusion.28), channel_id=1, source_target_pairs={{0,2},{2,0},{1,3},{3,1},{4,6},{6,4},{5,7},{7,5},{8,10},{10,8},{9,1... | collective-permute-start | bytes 3145736 | tf_op jit(solution)/shard_map/ppermute | solution.py:19
  1335.2 100.1 %collective-permute-start.90 = (bf16[256,1024]{1,0:T(8,128)(2,1)}, bf16[256,1024]{1,0:T(8,128)(2,1)}, u32[]{:S(2)}, u32[]{:S(2)}) collective-permute-start(bf16[256,1024]{1,0:T(8,128)(2,1)} %pad_maximum_fusion.58), channel_id=1, source_target_pairs={{8,0},{12,4},{16,24},{20,28},{9,1},{13,5},{17,25},{21,29},{10,2},{... | collective-permute-start | bytes 1572872 | tf_op jit(solution)/shard_map/ppermute | solution.py:236
  1349.5 87.7 %collective-permute-start.86 = (bf16[256,1024]{1,0:T(8,128)(2,1)}, bf16[256,1024]{1,0:T(8,128)(2,1)}, u32[]{:S(2)}, u32[]{:S(2)}) collective-permute-start(bf16[256,1024]{1,0:T(8,128)(2,1)} %pad_maximum_fusion.57), channel_id=1, source_target_pairs={{8,0},{12,4},{16,24},{20,28},{9,1},{13,5},{17,25},{21,29},{10,2},{... | collective-permute-start | bytes 1572872 | tf_op jit(solution)/shard_map/ppermute | solution.py:236
  1364.2 132.2 %collective-permute-start.161 = (bf16[352,1024]{1,0:T(8,128)(2,1)}, bf16[352,1024]{1,0:T(8,128)(2,1)}, u32[]{:S(2)}, u32[]{:S(2)}) collective-permute-start(bf16[352,1024]{1,0:T(8,128)(2,1)} %pad_maximum_fusion.52), channel_id=1, source_target_pairs={{8,0},{12,4},{16,24},{20,28},{9,1},{13,5},{17,25},{21,29},{10,2},{... | collective-permute-start | bytes 2162696 | tf_op jit(solution)/shard_map/ppermute | solution.py:236
  1434.5 142.1 %collective-permute-start.30 = (f32[256,1024]{1,0:T(8,128)}, f32[256,1024]{1,0:T(8,128)}, u32[]{:S(2)}, u32[]{:S(2)}) collective-permute-start(f32[256,1024]{1,0:T(8,128)} %slice.451), channel_id=1, source_target_pairs={{0,2},{2,0},{1,3},{3,1},{4,6},{6,4},{5,7},{7,5},{8,10},{10,8},{9,1... | collective-permute-start | bytes 3145736 | tf_op jit(solution)/shard_map/ppermute | solution.py:19
  (308 other events, 5338.5 us)

commit v2 on v1

v2 whole, which is shorter than its diff:
```python
import functools
import math

import jax
import jax.numpy as jnp
from jax import lax
from jax.experimental import pallas as pl
from jax.experimental.pallas import tpu as pltpu
from jax.sharding import PartitionSpec as P

HEAD = 64
ROT = 16
EPSILON = 1e-05
ROPE_BASE = 10000.0
NEGATIVE = -1e30
BF = jnp.bfloat16
F32 = jnp.float32
SWAP = [(0, 1), (1, 0)]


def swap(v, axis):
    return lax.ppermute(v, axis, SWAP)


def ordered(flag, mine, other, axis=0):
    first = jnp.where(flag == 0, mine, other)
    second = jnp.where(flag == 0, other, mine)
    return jnp.concatenate([first, second], axis=axis)


def piece(v, index, count, axis=0):
    size = v.shape[axis] // count
    return lax.dynamic_slice_in_dim(v, index * size, size, axis)


def add(a, b):
    return (a.astype(F32) + b.astype(F32)).astype(BF)


def dot(a, b):
    return jnp.dot(a, b, preferred_element_type=F32)


def dot_t(a, b):
    return lax.dot_general(a, b, (((1,), (1,)), ((), ())), preferred_element_type=F32)


def t_dot(a, b):
    return lax.dot_general(a, b, (((0,), (0,)), ((), ())), preferred_element_type=F32)


class Place:
    def __init__(self):
        self.r = lax.axis_index("row")
        self.c = lax.axis_index("col")
        self.d = lax.axis_index("dp")
        self.count = lax.axis_size("dp")
        self.y = lax.rem(self.d, 2)
        self.zp = lax.rem(self.d // 2, 2)
        self.z = self.d // 2
        self.mid = (self.z == 1) | (self.z == 2)
        self.upper = (self.z >= 2).astype(jnp.int32)


def dp_perm(bit, count):
    return [(i, i ^ bit) for i in range(count)]


def fetch(send, place, y_first):
    count = place.count
    if count % 4:
        return swap(send, "row")
    if y_first:
        index = place.zp * 2 + place.y
        steps = ((1, place.y), (2, place.zp))
    else:
        index = place.y * 2 + place.zp
        steps = ((2, place.zp), (1, place.y))
    held = swap(piece(send, index, 4), "row")
    for bit, flag in steps:
        other = lax.ppermute(held, "dp", dp_perm(bit, count))
        held = ordered(flag, held, other)
    return held


def cross(v):
    half = v.shape[-1] // 2
    return jnp.concatenate([v[..., half:], v[..., :half]], axis=-1)


def gather_blocks(block, place):
    other = cross(swap(block, "row"))
    pair = ordered(place.r, block, other)
    rest = swap(pair, "col")
    return ordered(place.c, pair, rest)


def reduce_blocks(partial, place):
    kept = piece(partial, place.c, 2)
    got = swap(piece(partial, 1 - place.c, 2), "col")
    held = add(kept, got)
    kept = piece(held, place.r, 2)
    got = cross(swap(piece(held, 1 - place.r, 2), "row"))
    return kept.astype(F32) + got.astype(F32)


def norm_forward(values, gain, shift):
    count = values.shape[-1]
    mean = jnp.sum(values, axis=-1, keepdims=True) / count
    spread = jnp.sum(values * values, axis=-1, keepdims=True) / count - mean * mean
    inverse = lax.rsqrt(spread + EPSILON)
    normal = (values - mean) * inverse
    return normal * gain + shift, normal, inverse


def norm_backward(grad, normal, inverse, gain):
    count = grad.shape[-1]
    scaled = grad * gain
    first = jnp.sum(scaled, axis=-1, keepdims=True) / count
    second = jnp.sum(scaled * normal, axis=-1, keepdims=True) / count
    grad_input = inverse * (scaled - first - normal * second)
    return grad_input, jnp.sum(grad * normal, axis=0), jnp.sum(grad, axis=0)


def doc_positions(segment_ids):
    places = jnp.arange(segment_ids.shape[0], dtype=jnp.int32)
    starts = jnp.concatenate([jnp.ones((1,), dtype=bool), segment_ids[1:] != segment_ids[:-1]])
    first_place = lax.cummax(jnp.where(starts, places, jnp.zeros_like(places)), axis=0)
    return places - first_place


def rotary_tables(segment_ids):
    places = doc_positions(segment_ids).astype(F32)
    freq_index = jnp.arange(ROT // 2, dtype=F32)
    inverse = jnp.exp(freq_index * (-2.0 / ROT) * math.log(ROPE_BASE))
    angles = places[:, None] * inverse[None, :]
    return (jnp.cos(angles), jnp.sin(angles))


LONGEST = 512
QB = 256

def windows(length):
    for begin in range(0, length, QB):
        low = max(0, (begin - LONGEST + 1) // QB * QB)
        yield begin, low, begin + QB


def barred(starts, begin, low, end):
    shape = (end - begin, end - low)
    query = begin + lax.broadcasted_iota(jnp.int32, shape, 0)
    key = low + lax.broadcasted_iota(jnp.int32, shape, 1)
    return jnp.where((key <= query) & (key >= starts), 0.0, NEGATIVE)


def turned(v, table):
    width = v.shape[-1]
    return v * table[0] + pltpu.roll(v, width - 8, 1) * table[1] + pltpu.roll(v, 8, 1) * table[2]


def nt(a, b):
    return lax.dot_general(a, b, (((1,), (1,)), ((), ())), preferred_element_type=F32)


def tn(a, b):
    return lax.dot_general(a, b, (((0,), (0,)), ((), ())), preferred_element_type=F32)


def forward_kernel(q_in, k_in, v_in, bias_ref, starts_ref, table_ref, q_ref, k_ref, v_ref, out_ref, raw_ref, log_ref):
    length = q_in.shape[0]
    table = (table_ref[0], table_ref[1], table_ref[2])
    q_ref[...] = (turned(q_in[...] + bias_ref[0, 0:1], table).astype(BF).astype(F32) * HEAD ** (-0.5)).astype(BF)
    k_ref[...] = turned(k_in[...] + bias_ref[0, 1:2], table).astype(BF)
    v_ref[...] = (v_in[...] + bias_ref[0, 2:3]).astype(BF)
    for begin, low, end in windows(length):
        bar = barred(starts_ref[begin:end], begin, low, end)
        outs = []
        for h in range(2):
            lanes = slice(h * HEAD, (h + 1) * HEAD)
            scores = nt(q_ref[begin:end, lanes], k_ref[low:end, lanes]) + bar
            maxima = jnp.max(scores, axis=1, keepdims=True)
            shifted = jnp.exp(scores - maxima).astype(BF)
            wide = jnp.concatenate([v_ref[low:end, lanes], jnp.ones((end - low, HEAD), BF)], axis=1)
            got = jnp.dot(shifted, wide, preferred_element_type=F32)
            totals = got[:, HEAD : HEAD + 1]
            outs.append(got[:, :HEAD] / totals)
            log_ref[0, begin:end, h : h + 1] = maxima + jnp.log(totals)
        out = jnp.concatenate(outs, axis=1)
        raw_ref[begin:end] = out
        out_ref[begin:end] = out.astype(BF)


def backward_kernel(q_ref, k_ref, v_ref, g_ref, raw_ref, log_ref, starts_ref, table_ref, dq_ref, dk_ref, dv_ref, dk_acc, dv_acc):
    length = q_ref.shape[0]
    dk_acc[...] = jnp.zeros_like(dk_acc)
    dv_acc[...] = jnp.zeros_like(dv_acc)
    for begin, low, end in windows(length):
        bar = barred(starts_ref[begin:end], begin, low, end)
        outs, dks, dvs = [], [], []
        for h in range(2):
            lanes = slice(h * HEAD, (h + 1) * HEAD)
            q, k, v, g = q_ref[begin:end, lanes], k_ref[low:end, lanes], v_ref[low:end, lanes], g_ref[begin:end, lanes]
            weights = jnp.exp(nt(q, k) + bar - log_ref[0, begin:end, h : h + 1])
            dvs.append(tn(weights.astype(BF), g))
            inner = jnp.sum(g.astype(F32) * raw_ref[begin:end, lanes], axis=1, keepdims=True)
            grads = (weights * (nt(g, v) - inner)).astype(BF)
            outs.append(jnp.dot(grads, k, preferred_element_type=F32))
            dks.append(tn(grads, q))
        table = (table_ref[0, begin:end], -table_ref[1, begin:end], -table_ref[2, begin:end])
        dq_ref[begin:end] = turned(jnp.concatenate(outs, axis=1) * HEAD ** (-0.5), table).astype(BF)
        dk_acc[low:end] += jnp.concatenate(dks, axis=1)
        dv_acc[low:end] += jnp.concatenate(dvs, axis=1)
    table = (table_ref[0], -table_ref[1], -table_ref[2])
    dk_ref[...] = turned(dk_acc[...], table).astype(BF)
    dv_ref[...] = dv_acc[...].astype(BF)


def tables(cosines, sines):
    length = cosines.shape[0]
    ones = jnp.ones((length, HEAD - 16), F32)
    none = jnp.zeros((length, HEAD - 8), F32)
    one = jnp.concatenate([cosines, cosines, ones], axis=1)
    ahead = jnp.concatenate([-sines, none], axis=1)
    behind = jnp.concatenate([none[:, :8], sines, none[:, 8:]], axis=1)
    return jnp.stack([jnp.concatenate([v, v], axis=1) for v in (one, ahead, behind)])


def attention_forward(joined, bias, starts, table):
    length, pairs = joined.shape[0], bias.shape[0]
    units = pairs * 128
    part = lambda n: pl.BlockSpec((length, 128), lambda p, n=n: (0, n * pairs + p))
    same = pl.BlockSpec((length, 128), lambda p: (0, p))
    half = jax.ShapeDtypeStruct((length, units), BF)
    return pl.pallas_call(
        forward_kernel,
        grid=(pairs,),
        in_specs=[
            part(0), part(1), part(2),
            pl.BlockSpec((1, 3, 128), lambda p: (p, 0, 0)),
            pl.BlockSpec((length, 1), lambda p: (0, 0)),
            pl.BlockSpec((3, length, 128), lambda p: (0, 0, 0)),
        ],
        out_specs=[same] * 5 + [pl.BlockSpec((1, length, 2), lambda p: (p, 0, 0))],
        out_shape=[half] * 4 + [jax.ShapeDtypeStruct((length, units), F32), jax.ShapeDtypeStruct((pairs, length, 2), F32)],
        compiler_params=pltpu.CompilerParams(vmem_limit_bytes=48 * 2**20),
        cost_estimate=pl.CostEstimate(flops=pairs * 2 * length * 640 * 256, bytes_accessed=12 * 2**20, transcendentals=pairs * 2 * length * 640),
    )(joined, joined, joined, bias, starts, table)


def attention_backward(queries, keys, values, grads, raw, logs, starts, table):
    length, units = queries.shape
    pairs = units // 128
    same = pl.BlockSpec((length, 128), lambda p: (0, p))
    half = jax.ShapeDtypeStruct((length, units), BF)
    return pl.pallas_call(
        backward_kernel,
        grid=(pairs,),
        in_specs=[same] * 5
        + [
            pl.BlockSpec((1, length, 2), lambda p: (p, 0, 0)),
            pl.BlockSpec((length, 1), lambda p: (0, 0)),
            pl.BlockSpec((3, length, 128), lambda p: (0, 0, 0)),
        ],
        out_specs=[same] * 3,
        out_shape=[half] * 3,
        scratch_shapes=[pltpu.VMEM((length, 128), F32)] * 2,
        compiler_params=pltpu.CompilerParams(vmem_limit_bytes=48 * 2**20),
        cost_estimate=pl.CostEstimate(flops=pairs * 2 * length * 640 * 640, bytes_accessed=8 * 2**20, transcendentals=pairs * 2 * length * 640),
    )(queries, keys, values, grads, raw, logs, starts, table)


MESH = pl.DeviceIdType.MESH

BR = 512
BC = 256
SLOTS = 6


def gradient_kernel(segments, half, *refs):
    count = len(segments)
    total = sum(s[1] for s in segments)
    sources = refs[: 2 * count]
    out_ref = refs[2 * count]
    out_own, out_got = out_ref.at[0], out_ref.at[1]
    rest = refs[2 * count + 1 :]
    held = rest[: 2 * count]
    (
        load_sem,
        turn,
        part,
        x_src,
        x_dst,
        y_dst,
        acc,
        e_dst,
        low,
        m_dst,
        full,
        f_dst,
        deep,
        n_dst,
        key,
        k_dst,
        whole,
    ) = rest[2 * count : 2 * count + 17]
    sems = rest[2 * count + 17 :]
    names = ("x", "y", "ei", "eo", "m", "g", "fi", "fo", "n", "k", "w")
    send = {k: sems[i] for i, k in enumerate(names)}
    recv = {k: sems[len(names) + i] for i, k in enumerate(names)}
    store_own, store_got = sems[2 * len(names)], sems[2 * len(names) + 1]

    d, r = lax.axis_index("dp"), lax.axis_index("row")
    y, z = lax.rem(d, 2), d // 2
    upper = d // 4
    mid = (z == 1) | (z == 2)
    outer = (z == 0) | (z == 3)
    x_peer = {"row": 1 - r}
    y_peer = {"dp": d + 1 - 2 * y}
    e_peer = {"dp": d + 2 - 4 * lax.rem(z, 2)}
    m_peer = {"dp": d + 2 - 4 * upper}

    loads = []
    for i in range(2 * count):
        loads.append(pltpu.make_async_copy(sources[i], held[i], load_sem.at[i]))
        loads[-1].start()

    barrier = pltpu.get_barrier_semaphore()
    for peer in (x_peer, y_peer, e_peer):
        pl.semaphore_signal(barrier, inc=1, device_id=peer, device_id_type=MESH)

    @pl.when(mid)
    def _():
        pl.semaphore_signal(barrier, inc=1, device_id=m_peer, device_id_type=MESH)
        pl.semaphore_wait(barrier, 4)

    @pl.when(outer)
    def _():
        pl.semaphore_wait(barrier, 3)

    rows = BR // 2

    def halves(index):
        return pl.ds(pl.multiple_of(index * rows, rows), rows)

    def copy(name, u, src, dst, peer):
        s = lax.rem(u, SLOTS)
        return pltpu.make_async_remote_copy(
            src_ref=src, dst_ref=dst, send_sem=send[name].at[s], recv_sem=recv[name].at[s], device_id=peer, device_id_type=MESH
        )

    def slot(u):
        return lax.rem(u, SLOTS)

    def out_half(ref, u, index):
        return ref.at[u, halves(index)]

    def x_copy(u):
        return copy("x", u, x_src.at[slot(u)], x_dst.at[slot(u)], x_peer)

    def y_copy(u):
        return copy("y", u, part.at[slot(u), halves(1 - y)], y_dst.at[slot(u)], y_peer)

    def e_in(u):
        return copy("ei", u, acc.at[slot(u)], e_dst.at[slot(u)], e_peer)

    def e_out(u):
        return copy("eo", u, full.at[slot(u)], e_dst.at[slot(u)], e_peer)

    def m_copy(u):
        return copy("m", u, low.at[slot(u)], m_dst.at[slot(u)], m_peer)

    def g_mid(u):
        return copy("g", u, full.at[slot(u)], out_half(out_own, u, y), y_peer)

    def g_out(u):
        return copy("g", u, e_dst.at[slot(u)], out_half(out_own, u, y), y_peer)

    def f_in(u):
        return copy("fi", u, x_dst.at[slot(u)], f_dst.at[slot(u)], e_peer)

    def f_out(u):
        return copy("fo", u, whole.at[slot(u)], out_got.at[u], e_peer)

    def n_copy(u):
        return copy("n", u, deep.at[slot(u), halves(1 - upper)], n_dst.at[slot(u)], m_peer)

    def k_copy(u):
        return copy("k", u, key.at[slot(u)], k_dst.at[slot(u)], y_peer)

    def w_copy(u):
        place = whole.at[slot(u), halves(upper)]
        return copy("w", u, place, place, m_peer)

    def keep_own(u, src):
        return pltpu.make_async_copy(src, out_half(out_own, u, y), store_own.at[slot(u)])

    def keep_got(u):
        return pltpu.make_async_copy(whole.at[slot(u)], out_got.at[u], store_got.at[slot(u)])

    def stage(u, fn, role=None):
        ok = (u >= 0) & (u < total)
        if role is not None:
            ok = ok & role

        @pl.when(ok)
        def _():
            fn(u)

    def produce(u):
        s = slot(u)
        first = 0
        for i, (kind, blocks) in enumerate(segments):
            lhs, rhs = held[2 * i], held[2 * i + 1]

            @pl.when(u == first)
            def _(i=i):
                loads[2 * i].wait()
                loads[2 * i + 1].wait()

            @pl.when((u >= first) & (u < first + blocks))
            def _(kind=kind, first=first, lhs=lhs, rhs=rhs):
                k = u - first
                if kind == "D":
                    columns = rhs.shape[1] // BC

                    @pl.when(lax.rem(k, columns) == 0)
                    def _():
                        for side in range(2):
                            at = pl.multiple_of(side * half + k // columns * BR, BR)
                            turn[side] = lhs[:, pl.ds(at, BR)].T

                    right = rhs[:, pl.ds(pl.multiple_of(lax.rem(k, columns) * BC, BC), BC)]
                    for side, ref in ((1, x_src), (0, part)):
                        ref[s] = jnp.dot(turn[side], right, preferred_element_type=F32).astype(BF)
                else:
                    size = BR * BC // half
                    left = lhs[:, pl.ds(pl.multiple_of(k * size, size), size)].T
                    for side, ref in ((1, x_src), (0, part)):
                        for q in range(half // BC):
                            right = rhs[:, side * half + q * BC : side * half + (q + 1) * BC]
                            ref[s, q * size : (q + 1) * size] = jnp.dot(
                                left, right, preferred_element_type=F32
                            ).astype(BF)

            first += blocks
        x_copy(u).start()
        y_copy(u).start()

    def t1_a(u):
        s = slot(u)
        y_copy(u).wait_recv()
        acc[s] = part[s, halves(y)] + y_dst[s]
        pl.when(outer)(lambda: e_in(u).start())

    def t1_b(u):
        s = slot(u)
        e_in(u).wait_recv()
        low[s] = acc[s] + e_dst[s]
        m_copy(u).start()

    def t1_c(u):
        s = slot(u)
        m_copy(u).wait_recv()
        full[s] = low[s] + m_dst[s]
        e_out(u).start()
        g_mid(u).start()
        keep_own(u, full.at[s]).start()

    def t1_d(u):
        e_out(u).wait_recv()
        g_out(u).start()
        keep_own(u, e_dst.at[slot(u)]).start()

    def t2_a(u):
        x_copy(u).wait_recv()
        pl.when(outer)(lambda: f_in(u).start())

    def t2_b(u):
        s = slot(u)
        f_in(u).wait_recv()
        deep[s] = x_dst[s] + f_dst[s]
        n_copy(u).start()

    def t2_c(u):
        s = slot(u)
        n_copy(u).wait_recv()
        key[s] = deep[s, halves(upper)] + n_dst[s]
        k_copy(u).start()

    def t2_d(u):
        s = slot(u)
        k_copy(u).wait_recv()
        whole[s, halves(upper)] = key[s] + k_dst[s]
        w_copy(u).start()

    def t2_e(u):
        w_copy(u).wait_recv()
        f_out(u).start()
        keep_got(u).start()

    def body(t, carry):
        stage(t - 2, lambda u: (x_copy(u).wait_send(), y_copy(u).wait_send()))
        stage(t - 3, lambda u: e_in(u).wait_send(), outer)
        stage(t - 3, lambda u: f_in(u).wait_send(), outer)
        stage(t - 4, lambda u: (m_copy(u).wait_send(), n_copy(u).wait_send()), mid)
        stage(t - 5, lambda u: k_copy(u).wait_send(), mid)
        stage(t - 6, lambda u: w_copy(u).wait_send(), mid)
        stage(t - 5, lambda u: (e_out(u).wait_send(), g_mid(u).wait_send(), keep_own(u, full.at[slot(u)]).wait()), mid)
        stage(t - 5, lambda u: (g_out(u).wait_send(), keep_own(u, e_dst.at[slot(u)]).wait()), outer)
        stage(t - 7, lambda u: (f_out(u).wait_send(), keep_got(u).wait()), mid)
        stage(t - 5, lambda u: g_mid(u).wait_recv(), mid)
        stage(t - 6, lambda u: g_out(u).wait_recv(), outer)
        stage(t - 7, lambda u: f_out(u).wait_recv(), outer)
        stage(t - 5, t2_e, mid)
        stage(t - 4, t2_d, mid)
        stage(t - 3, t2_c, mid)
        stage(t - 2, t2_b, mid)
        stage(t - 1, t2_a)
        stage(t - 4, t1_d, outer)
        stage(t - 3, t1_c, mid)
        stage(t - 2, t1_b, mid)
        stage(t - 1, t1_a)
        stage(t, produce)
        return carry

    lax.fori_loop(0, total + 8, body, 0)


def gradient_sums(pairs, half):
    segments, operands = [], []
    for kind, left, right in pairs:
        area = half * right.shape[1] if kind == "D" else left.shape[1] * half
        segments.append((kind, area // (BR * BC)))
        operands += [left, right]
    total = sum(s[1] for s in segments)
    tokens = operands[0].shape[0]
    wide, thin = pltpu.VMEM((SLOTS, BR, BC), BF), pltpu.VMEM((SLOTS, BR // 2, BC), BF)
    dma = pltpu.SemaphoreType.DMA((SLOTS,))
    return pl.pallas_call(
        functools.partial(gradient_kernel, segments, half),
        out_shape=jax.ShapeDtypeStruct((2, total, BR, BC), BF),
        in_specs=[pl.BlockSpec(memory_space=pl.ANY)] * len(operands),
        out_specs=pl.BlockSpec(memory_space=pl.ANY),
        scratch_shapes=[pltpu.VMEM(v.shape, v.dtype) for v in operands]
        + [pltpu.SemaphoreType.DMA((len(operands),)), pltpu.VMEM((2, BR, tokens), BF)]
        + [wide, wide, wide, thin, thin, thin, thin, thin, thin, wide, wide, thin, thin, thin, wide]
        + [dma] * 24,
        compiler_params=pltpu.CompilerParams(
            collective_id=1, has_side_effects=True, vmem_limit_bytes=60 * 2**20
        ),
        cost_estimate=pl.CostEstimate(
            flops=4 * total * BR * BC * tokens, bytes_accessed=4 * total * BR * BC, transcendentals=0
        ),
    )(*operands)


def spread_kernel(side_ref, block_ref, out_ref):
    for i in range(block_ref.shape[1]):
        out_ref[0, i * BR : (i + 1) * BR] = block_ref[0, i].astype(F32)


def spread_pair_kernel(side_ref, gate_ref, up_ref, out_ref):
    for i in range(gate_ref.shape[1]):
        out_ref[i * BR : (i + 1) * BR, 0, :] = gate_ref[0, i].astype(F32)
        out_ref[i * BR : (i + 1) * BR, 1, :] = up_ref[0, i].astype(F32)


def spread_rows_kernel(side_ref, block_ref, out_ref):
    size = out_ref.shape[0]
    for q in range(BR // size):
        out_ref[:, q * BC : (q + 1) * BC] = block_ref[0, 0, q * size : (q + 1) * size].astype(F32)


def spread(body, side, blocks, grid, in_specs, out_spec, out_shape):
    return pl.pallas_call(
        body,
        grid_spec=pltpu.PrefetchScalarGridSpec(
            num_scalar_prefetch=1, grid=grid, in_specs=in_specs, out_specs=out_spec
        ),
        out_shape=jax.ShapeDtypeStruct(out_shape, F32),
        compiler_params=pltpu.CompilerParams(vmem_limit_bytes=48 * 2**20),
    )(side, *([blocks] * len(in_specs)))


def place_of(which, side_ref):
    return which + side_ref[0] - 2 * which * side_ref[0]


def spread_qkv(side, blocks, base, half, units):
    per, kind_blocks = half // BR, units // BC
    return spread(
        spread_kernel,
        side,
        blocks,
        (2, 3 * kind_blocks, per),
        [pl.BlockSpec((1, 1, BR, BC), lambda w, j, i, s: (w, base + i * 3 * kind_blocks + j, 0, 0))],
        pl.BlockSpec(
            (1, BR, BC),
            lambda w, j, i, s: (j // kind_blocks, i, place_of(w, s) * kind_blocks + j % kind_blocks),
        ),
        (3, half, 2 * units),
    ).transpose(1, 0, 2)


def spread_gate_up(side, blocks, base, half, units):
    tiles, columns = units // 128, 2 * units // BC

    def block_of(w, i, f):
        return (w, base + i * columns + f // (BC // 128), 0, f % (BC // 128))

    return spread(
        spread_pair_kernel,
        side,
        blocks,
        (2, half // BR, tiles),
        [
            pl.BlockSpec((1, 1, BR, 128), lambda w, i, f, s: block_of(w, i, f)),
            pl.BlockSpec((1, 1, BR, 128), lambda w, i, f, s: block_of(w, i, tiles + f)),
        ],
        pl.BlockSpec((BR, 2, 128), lambda w, i, f, s: (i, 0, place_of(w, s) * tiles + f)),
        (half, 2, 2 * units),
    )


def spread_rows(side, blocks, base, half, units):
    size = BR * BC // half
    count = units // size
    return spread(
        spread_rows_kernel,
        side,
        blocks,
        (2, count),
        [pl.BlockSpec((1, 1, BR, BC), lambda w, k, s: (w, base + k, 0, 0))],
        pl.BlockSpec((size, half), lambda w, k, s: (place_of(w, s) * count + k, 0)),
        (2 * units, half),
    )


def local(
    tokens,
    segments,
    ln1_gain,
    ln1_bias,
    qkv_weight,
    qkv_bias,
    out_weight,
    ln2_gain,
    ln2_bias,
    gate_up_weight,
    down_weight,
    cotangent,
):
    place = Place()
    r, c = place.r, place.c
    ids = segments[0]
    length = ids.shape[0]
    factor = HEAD ** (-0.5)
    half = qkv_weight.shape[0]
    units = qkv_weight.shape[2] // 2
    heads = units // HEAD
    hidden = gate_up_weight.shape[2] // 2

    other = swap(tokens, "row")
    mine = jnp.concatenate([tokens, other], axis=1)
    tokens_all = ordered(c, mine, swap(mine, "col"))
    params = jnp.stack([ln1_gain, ln1_bias, ln2_gain, ln2_bias])
    params = jnp.concatenate([params, swap(params, "row")], axis=1)

    qkv_flat = [qkv_weight[:, k] for k in range(3)]
    qkv_own = jnp.concatenate([piece(w, r, 2, 1) for w in qkv_flat], axis=1)
    qkv_send = jnp.concatenate([piece(w, 1 - r, 2, 1) for w in qkv_flat], axis=1)
    w_qkv = jnp.concatenate([qkv_own, fetch(qkv_send, place, False)], axis=0)
    w_out = jnp.concatenate(
        [piece(out_weight, r, 2), fetch(piece(out_weight, 1 - r, 2), place, True)], axis=1
    )
    w_gate = jnp.concatenate(
        [
            piece(gate_up_weight, r, 2, 2),
            fetch(piece(gate_up_weight, 1 - r, 2, 2), place, True),
        ],
        axis=0,
    )
    cot_other = swap(cotangent, "row")
    cot_mine = jnp.concatenate([cotangent, cot_other], axis=1)
    cot_all = ordered(c, cot_mine, swap(cot_mine, "col"))
    w_down = jnp.concatenate(
        [piece(down_weight, r, 2), fetch(piece(down_weight, 1 - r, 2), place, False)], axis=1
    )

    cosines, sines = rotary_tables(ids)
    table = tables(cosines, sines)
    inputs = tokens_all.astype(F32)
    normed, _, _ = norm_forward(inputs, params[0], params[1])
    act_one = normed.astype(BF)
    joined = dot(act_one, w_qkv)
    starts = (jnp.arange(length, dtype=jnp.int32) - doc_positions(ids))[:, None]
    bias = piece(qkv_bias, r, 2, 1).reshape(3, units // 128, 128).transpose(1, 0, 2)
    queries, keys, values, attended, raw, logs = attention_forward(joined, bias, starts, table)
    block = c * 2 + r
    own_inputs = piece(tokens_all, block, 4).astype(F32)
    branch = reduce_blocks(dot(attended, w_out).astype(BF), place)
    hidden_state = own_inputs + branch
    normed, normal_two, inverse_two = norm_forward(hidden_state, params[2], params[3])
    act_two = gather_blocks(normed.astype(BF), place)
    gate_up = jnp.einsum("sd,dkf->ksf", act_two, w_gate, preferred_element_type=F32)
    gate, up = gate_up[0], gate_up[1]
    inner = (jax.nn.silu(gate) * up).astype(BF)

    feed = reduce_blocks(dot(inner, w_down).astype(BF), place)
    result = (hidden_state + feed).astype(BF)
    result = ordered(r, result[:, :half], swap(result[:, half:], "row"))

    grad_inner = dot_t(cot_all, w_down)
    rate = 1.0 / (1.0 + jnp.exp(-gate))
    silu = gate * rate
    grad_gate = (grad_inner * up * (rate * (1.0 + gate * (1.0 - rate)))).astype(BF)
    grad_up = (grad_inner * silu).astype(BF)
    grad_two = jnp.stack([grad_gate, grad_up])
    grad_pair = jnp.concatenate([grad_gate, grad_up], axis=1)
    grad_act_two = reduce_blocks(
        jnp.einsum("ksf,dkf->sd", grad_two, w_gate, preferred_element_type=F32).astype(BF), place
    )
    grad_norm, ln2_gain_grad, ln2_bias_grad = norm_backward(
        grad_act_two, normal_two, inverse_two, params[2]
    )
    own_cot = piece(cot_all, block, 4).astype(F32)
    grad_hidden = own_cot + grad_norm
    grad_branch = gather_blocks(grad_hidden.astype(BF), place)
    grad_attended = dot_t(grad_branch, w_out).astype(BF)
    grad_joined = attention_backward(
        queries, keys, values, grad_attended, raw, logs, starts, table
    )
    grad_joined = jnp.concatenate(grad_joined, axis=1)
    bias_grad = jnp.sum(grad_joined, axis=0, dtype=F32)
    grad_act_one = reduce_blocks(dot_t(grad_joined, w_qkv).astype(BF), place)
    _, normal_one, inverse_one = norm_forward(own_inputs, params[0], params[1])
    grad_norm, ln1_gain_grad, ln1_bias_grad = norm_backward(
        grad_act_one, normal_one, inverse_one, params[0]
    )
    input_grad = grad_hidden + grad_norm
    input_grad = ordered(r, input_grad[:, :half], swap(input_grad[:, half:], "row"))

    small = jnp.stack([ln1_gain_grad, ln1_bias_grad, ln2_gain_grad, ln2_bias_grad])
    small = small[:, :half] + swap(small[:, half:], "row")
    small = small + swap(small, "col")
    bias_grad = bias_grad.reshape(3, units)
    small = jnp.concatenate([small.reshape(-1), bias_grad.reshape(-1)])
    if place.count == 8:
        for bit in (1, 2, 4):
            small = small + lax.ppermute(small, "dp", dp_perm(bit, 8))
    else:
        small = lax.psum(small, "dp")
    norms = small[: 4 * half].reshape(4, half)
    bias_grad = small[4 * half :].reshape(3, units)
    bias_grad = ordered(r, bias_grad, swap(bias_grad, "row"), 1)

    pairs = (
        ("D", act_two, grad_pair),
        ("D", act_one, grad_joined),
        ("U", attended, grad_branch),
        ("U", inner, cot_all),
    )
    if place.count == 8:
        sums = gradient_sums(pairs, half)
        side = r.reshape(1)
        qkv_base = half * 2 * hidden // (BR * BC)
        out_base = qkv_base + half * 3 * units // (BR * BC)
        down_base = out_base + half * units // (BR * BC)
        gate_up_grad = spread_gate_up(side, sums, 0, half, hidden)
        qkv_grad = spread_qkv(side, sums, qkv_base, half, units)
        out_grad = spread_rows(side, sums, out_base, half, units)
        down_grad = spread_rows(side, sums, down_base, half, hidden)
    else:
        sums = []
        for kind, left, right in pairs:
            both = t_dot(left, right).astype(BF)
            axis = 0 if kind == "D" else 1
            own, sent = jnp.split(both, 2, axis)
            sums.append([lax.psum(v, "dp").astype(F32) for v in (own, swap(sent, "row"))])
        gate_up_grad = ordered(r, *[v.reshape(half, 2, hidden) for v in sums[0]], 2)
        qkv_grad = ordered(r, *[v.reshape(half, 3, units) for v in sums[1]], 2)
        out_grad = ordered(r, *sums[2])
        down_grad = ordered(r, *sums[3])
    return (
        result,
        input_grad,
        norms[0],
        norms[1],
        qkv_grad,
        bias_grad,
        out_grad,
        norms[2],
        norms[3],
        gate_up_grad,
        down_grad,
    )


def solution(mesh):
    in_specs = (
        P(("dp", "col"), "row"),
        P("dp", None),
        P("row"),
        P("row"),
        P("row", None, "col"),
        P(None, "col"),
        P("col", "row"),
        P("row"),
        P("row"),
        P("row", None, "col"),
        P("col", "row"),
        P(("dp", "col"), "row"),
    )
    out_specs = (
        P(("dp", "col"), "row"),
        P(("dp", "col"), "row"),
        P("row"),
        P("row"),
        P("row", None, "col"),
        P(None, "col"),
        P("col", "row"),
        P("row"),
        P("row"),
        P("row", None, "col"),
        P("col", "row"),
    )
    return jax.shard_map(local, mesh=mesh, in_specs=in_specs, out_specs=out_specs, check_vma=False)
```

time: 1710 us -> 1180 us (0.69)
  Pallas kernels: 0 us -> 593 us
  waiting for transfers between devices: 786 us -> 272 us
  starting transfers between devices: 314 us -> 36 us
  other arithmetic: 204 us -> 76.5 us
  local copies, waits for them, and re-layouts: 182 us -> 83.7 us
  matrix products: 205 us -> 107 us
    pallas_call x0 -> x7, Pallas kernels: none -> 593 us  [the longest x1 465 us: gradient_sums(): pl.pallas_call(functools.partial(gradient_kernel, segments, half), out_sh...]
    ppermute x120 -> x0, waiting for transfers between devices: 457 us -> none  [the longest x20 197 us: edge(): return lax.ppermute(jnp.where(mid, outward, inward), 'dp', dp_perm(2, 8))]
    ppermute x120 -> x0, starting transfers between devices: 250 us -> none  [the longest x20 158 us: edge(): return lax.ppermute(jnp.where(mid, outward, inward), 'dp', dp_perm(2, 8))]
    ppermute x31 -> x26, waiting for transfers between devices: 235 us -> 181 us  [swap(): return lax.ppermute(v, axis, SWAP)]
    dot_general x22 -> x2, matrix products: 91.6 us -> 38.6 us  [the longest x1 20 us: local(): jnp.einsum('sd,dkf->ksf', act_two, w_gate, preferred_element_type=F32)]
    unnamed x349 -> x149, local copies, waits for them, and re-layouts: 83.6 us -> 33.4 us
    convert_element_type x6 -> x0, other arithmetic: 37 us -> none  [the longest x2 12.5 us: attention_backward(): grad_scores = (weights * (grad_weights - jnp.sum(weights * grad_weights,...]
    select_n x45 -> x0, other arithmetic: 36.3 us -> none  [the longest x28 21.2 us: line(): outs[step - 2] = jnp.where(self.place.mid, done, got)]
  transfers between devices with their start and end apart: 162 -> 37, of which waited for: 82 -> 22; matrix products, arithmetic and copies ran while one was open for 23% -> 12% of each run, Pallas kernels for 0% -> 46%
where the time goes in v2:
time: 1180 us; the launch traced here: 1170 us
  Pallas kernels  593 us (50%)
  waiting for transfers between devices  272 us (23%)
  matrix products  107 us (9%)
  local copies, waits for them, and re-layouts  83.7 us (7%)
  other arithmetic  76.5 us (6%)
  starting transfers between devices  36 us (3%)
    pallas_call x1, Pallas kernels, gradient_sums(): pl.pallas_call(functools.partial(gradient_kernel, segments, half), out_sh...  465 us
    ppermute x26, waiting for transfers between devices, swap(): return lax.ppermute(v, axis, SWAP)  181 us
    ppermute x8, waiting for transfers between devices, fetch(): other = lax.ppermute(held, 'dp', dp_perm(bit, count))  87.8 us
    pallas_call x4, Pallas kernels, spread(): pl.pallas_call(body, grid_spec=pltpu.PrefetchScalarGridSpec(num_scalar_pr...  70.1 us
    dot_general x3, matrix products, dot_t(): lax.dot_general(a, b, (((1,), (1,)), ((), ())), preferred_element_type=F32)  36.2 us
    unnamed x149, local copies, waits for them, and re-layouts  33.4 us
    dot_general x3, matrix products, dot(): return jnp.dot(a, b, preferred_element_type=F32)  32.4 us
    pallas_call x1, Pallas kernels, attention_forward(): pl.pallas_call(forward_kernel, grid=(pairs,), in_specs=[part(0), part(1),...  31.5 us
  transfers between devices with their start and end apart: 37, of which 22 were waited for; matrix products, arithmetic and copies ran while one was open for 12% of the time, Pallas kernels for 46%

profile of v2, /device:TPU:0, one launch (start us, length us, event | category | flops | bytes accessed | tf_op | source)
XLA Modules:
  0.0 1170.7 jit_solution(12220769009237889436)
XLA Ops:
  57.6 14.6 %collective-permute-done.4 = bf16[256,1536]{1,0:T(8,128)(2,1)S(1)} collective-permute-done((bf16[256,1536]{1,0:T(8,128)(2,1)}, bf16[256,1536]{1,0:T(8,128)(2,1)S(1)}, u32[]{:S(2)}, u32[]{:S(2)}) %collective-permute-start.4) | collective-permute-done | bytes 786464 | tf_op jit(solution)/shard_map/ppermute | solution.py:81
  80.5 27.7 %collective-permute-done.5 = bf16[512,1536]{1,0:T(8,128)(2,1)S(1)} collective-permute-done((bf16[512,1536]{1,0:T(8,128)(2,1)S(1)}, bf16[512,1536]{1,0:T(8,128)(2,1)S(1)}, u32[]{:S(2)}, u32[]{:S(2)}) %collective-permute-start.5) | collective-permute-done | bytes 1572896 | tf_op jit(solution)/shard_map/ppermute | solution.py:81
  110.4 20.8 %fusion.44.q_in.k_in.v_in = f32[1024,1536]{1,0:T(8,128)} fusion(bf16[1024,2048]{1,0:T(8,128)(2,1)S(1)} %fusion.3.refs_2_, bf16[512,1536]{1,0:T(8,128)(2,1)S(1)} %get-tuple-element.68, bf16[512,1536]{1,0:T(8,128)(2,1)S(1)} %get-tuple-element.67, bf16[1024,512]{1,0:T(8,128)(2,1)S(1)} %copy-done.47, bf16[1024,512]{1,0:T(8,128)(2,1)S(1)} %copy-done.48, ...), kind=kOutput, calls=%fused_computation.195 | convolution fusion | flops 6473908224 | bytes 16777216 | tf_op jit(solution)/shard_map/dot_general | solution.py:41
  131.2 31.5 %shard_map.203 = (bf16[1024,512]{1,0:T(8,128)(2,1)S(1)}, bf16[1024,512]{1,0:T(8,128)(2,1)S(1)}, bf16[1024,512]{1,0:T(8,128)(2,1)S(1)}, bf16[1024,512]{1,0:T(8,12...) custom-call(f32[1024,1536]{1,0:T(8,128)} %fusion.44.q_in.k_in.v_in, f32[1024,1536]{1,0:T(8,128)} %fusion.44.q_in.k_in.v_in, ...), custom_call_target="tpu_custom_call" | custom-call | flops 1342177280 | bytes 12582912 | tf_op jit(solution)/shard_map/pallas_call | solution.py:234
  184.3 28.7 %collective-permute-done.11 = bf16[256,2,1408]{0,2,1:T(8,128)(2,1)} collective-permute-done((bf16[256,2,1408]{0,2,1:T(8,128)(2,1)}, bf16[256,2,1408]{0,2,1:T(8,128)(2,1)}, u32[]{:S(2)}, u32[]{:S(2)}) %collective-permute-start.11) | collective-permute-done | bytes 1441824 | tf_op jit(solution)/shard_map/ppermute | solution.py:22
  215.6 34.8 %collective-permute-done.16 = bf16[352,1024]{1,0:T(8,128)(2,1)S(1)} collective-permute-done((bf16[352,1024]{1,0:T(8,128)(2,1)}, bf16[352,1024]{1,0:T(8,128)(2,1)S(1)}, u32[]{:S(2)}, u32[]{:S(2)}) %collective-permute-start.16) | collective-permute-done | bytes 720928 | tf_op jit(solution)/shard_map/ppermute | solution.py:22
  259.2 9.1 collective-permute-done.17
  275.6 7.4 collective-permute-done.10
  295.4 14.8 %copy.40 = bf16[1024,2,1408]{0,2,1:T(8,128)(2,1)} copy(bf16[1024,2,1408]{2,1,0:T(2,128)(2,1)} %constant_dynamic-slice_fusion.9) | data formatting | bytes 11534336
  325.8 28.5 %collective-permute-done.13 = bf16[512,2,1408]{0,2,1:T(8,128)(2,1)} collective-permute-done((bf16[512,2,1408]{0,2,1:T(8,128)(2,1)}, bf16[512,2,1408]{0,2,1:T(8,128)(2,1)}, u32[]{:S(2)}, u32[]{:S(2)}) %collective-permute-start.13) | collective-permute-done | bytes 2883616 | tf_op jit(solution)/shard_map/ppermute | solution.py:81
  361.8 20.0 %convolution_bitcast_fusion = f32[2,1024,1408]{2,1,0:T(8,128)} fusion(bf16[512,2,1408]{0,2,1:T(8,128)(2,1)} %get-tuple-element.56, bf16[512,2,1408]{0,2,1:T(8,128)(2,1)} %get-tuple-element.55, bf16[1024,2,1408]{0,2,1:T(8,128)(2,1)} %copy.40, bf16[512,2048]{1,0:T(8,128)(2,1)} %get-tuple-element.62, bf16[512,2048]{1,0:T(8,128)(2,1)} %get-tuple-element.61), kind=kOutput, calls=%fused_computation.10 | convolution fusion | flops 11854151680 | bytes 27262976 | tf_op jit(solution)/shard_map/sd,dkf->ksf/dot_general | solution.py:705
  381.8 16.9 %multiply_convert_fusion.1 = (bf16[1024,1408]{1,0:T(8,128)(2,1)}, bf16[1024,1408]{1,0:T(8,128)(2,1)}, bf16[1024,1408]{1,0:T(8,128)(2,1)}) fusion(f32[2,1024,1408]{2,1,0:T(8,128)} %convolution_bitcast_fusion, bf16[704,1024]{1,0:T(8,128)(2,1)} %get-tuple-element.70, bf16[704,1024]{1,0:T(8,128)(2,1)} %get-tuple-element.69, ...), kind=kOutput, calls=%fused_computation.22 | convolution fusion | flops 5952897024 | bytes 30146560 | tf_op jit(solution)/shard_map/dot_general | solution.py:45
  398.7 18.6 %bitcast_convert_fusion = bf16[1024,2048]{1,0:T(8,128)(2,1)} fusion(bf16[512,2,1408]{0,2,1:T(8,128)(2,1)} %get-tuple-element.56, bf16[512,2,1408]{0,2,1:T(8,128)(2,1)} %get-tuple-element.55, bf16[1024,2,1408]{0,2,1:T(8,128)(2,1)} %copy.40, bf16[1,1024,1408]{2,1,0:T(8,128)(2,1)} %bitcast.81, bf16[1,1024,1408]{2,1,0:T(8,128)(2,1)} %bitcast.80), kind=kOutput, calls=%fused_computation.9 | convolution fusion | flops 11850743808 | bytes 21495808 | tf_op jit(solution)/shard_map/ksf,dkf->sd/dot_general | solution.py:721
  419.7 9.3 convolution_convert_fusion.1
  435.1 23.0 %collective-permute-done.25 = bf16[256,2048]{1,0:T(8,128)(2,1)S(1)} collective-permute-done((bf16[256,2048]{1,0:T(8,128)(2,1)S(1)}, bf16[256,2048]{1,0:T(8,128)(2,1)S(1)}, u32[]{:S(2)}, u32[]{:S(2)}) %collective-permute-start.25) | collective-permute-done | bytes 1048608 | tf_op jit(solution)/shard_map/ppermute | solution.py:22
  459.4 20.4 %collective-permute-done.20 = bf16[256,2048]{1,0:T(8,128)(2,1)S(1)} collective-permute-done((bf16[256,2048]{1,0:T(8,128)(2,1)S(1)}, bf16[256,2048]{1,0:T(8,128)(2,1)S(1)}, u32[]{:S(2)}, u32[]{:S(2)}) %collective-permute-start.20) | collective-permute-done | bytes 1048608 | tf_op jit(solution)/shard_map/ppermute | solution.py:22
  482.5 24.0 %collective-permute-done.26 = bf16[256,2048]{1,0:T(8,128)(2,1)S(1)} collective-permute-done((bf16[256,2048]{1,0:T(8,128)(2,1)S(1)}, bf16[256,2048]{1,0:T(8,128)(2,1)S(1)}, u32[]{:S(2)}, u32[]{:S(2)}) %collective-permute-start.26) | collective-permute-done | bytes 1048608 | tf_op jit(solution)/shard_map/ppermute | solution.py:22
  516.1 26.6 %shard_map.204 = (bf16[1024,512]{1,0:T(8,128)(2,1)S(1)}, bf16[1024,512]{1,0:T(8,128)(2,1)S(1)}, bf16[1024,512]{1,0:T(8,128)(2,1)S(1)}) custom-call(bf16[1024,512]{1,0:T(8,128)(2,1)S(1)} %get-tuple-element.21.q_ref, bf16[1024,512]{1,0:T(8,128)(2,1)S(1)} %get-tuple-element.22.k_ref, bf16[1024,512]{1,0:T(8,128)(2,1)} %copy-done.3, ...), custom_call_target="tpu_custom_call" | custom-call | flops 3355443200 | bytes 8388608 | tf_op jit(solution)/shard_map/pallas_call | solution.py:255
  547.0 15.9 %convolution_convert_fusion = bf16[1024,2048]{1,0:T(8,128)(2,1)} fusion(bf16[1024,1536]{1,0:T(8,128)(2,1)} %constant_dynamic-update-slice_fusion.4.refs_3_, bf16[512,1536]{1,0:T(8,128)(2,1)S(1)} %copy-done.44, bf16[512,1536]{1,0:T(8,128)(2,1)S(1)} %copy-done.42, bf16[1024,512]{1,0:T(8,128)(2,1)} %get-tuple-element.82, ...), kind=kOutput, calls=%fused_computation.39 | convolution fusion | flops 6476005376 | bytes 13631488 | tf_op jit(solution)/shard_map/dot_general | solution.py:45
  591.1 18.2 %collective-permute-done.29 = bf16[256,2048]{1,0:T(8,128)(2,1)S(1)} collective-permute-done((bf16[256,2048]{1,0:T(8,128)(2,1)S(1)}, bf16[256,2048]{1,0:T(8,128)(2,1)S(1)}, u32[]{:S(2)}, u32[]{:S(2)}) %collective-permute-start.29) | collective-permute-done | bytes 1048608 | tf_op jit(solution)/shard_map/ppermute | solution.py:22
  626.8 465.2 %shard_map.205.block_ref.gate_ref.up_ref = bf16[2,49,512,256]{3,2,1,0:T(8,128)(2,1)} custom-call(bf16[1024,2048]{1,0:T(8,128)(2,1)} %pad_maximum_fusion.7.refs_0_, bf16[1024,2816]{1,0:T(8,128)(2,1)} %pad_maximum_fusion.2.refs_1_, bf16[1024,2048]{1,0:T(8,128)(2,1)} %copy-done.32, bf16[1024,1536]{1,0:T(8,128)(2,1)} %constant_dynamic-update-slice_fusion.4.refs_3_, ...), custom_call_target="tpu_custom_call" | custom-call | flops 26306674688 | bytes 25690112 | tf_op jit(solution)/shard_map/pallas_call | solution.py:539
  1098.0 14.4 %shard_map.209 = f32[2816,1024]{1,0:T(8,128)} custom-call(s32[1]{0:T(128)} %bitcast.33.side_ref, bf16[2,49,512,256]{3,2,1,0:T(8,128)(2,1)} %shard_map.205.block_ref.gate_ref.up_ref), custom_call_target="tpu_custom_call" | custom-call | tf_op jit(solution)/shard_map/pallas_call | solution.py:575
  1112.4 15.6 %shard_map.206 = f32[3,1024,1024]{2,1,0:T(8,128)} custom-call(s32[1]{0:T(128)} %bitcast.33.side_ref, bf16[2,49,512,256]{3,2,1,0:T(8,128)(2,1)} %shard_map.205.block_ref.gate_ref.up_ref), custom_call_target="tpu_custom_call" | custom-call | tf_op jit(solution)/shard_map/pallas_call | solution.py:575
  1128.0 34.1 %shard_map.208 = f32[1024,2,2816]{2,1,0:T(2,128)} custom-call(s32[1]{0:T(128)} %bitcast.33.side_ref, bf16[2,49,512,256]{3,2,1,0:T(8,128)(2,1)} %shard_map.205.block_ref.gate_ref.up_ref, bf16[2,49,512,256]{3,2,1,0:T(8,128)(2,1)} %shard_map.205.block_ref.gate_ref.up_ref), custom_call_target="tpu_custom_call" | custom-call | tf_op jit(solution)/shard_map/pallas_call | solution.py:575
  (329 shorter events, 228.2 us)
Async XLA Ops:
  1.6 51.9 %collective-permute-start.2 = (f32[4,1024]{1,0:T(4,128)S(1)}, f32[4,1024]{1,0:T(4,128)S(1)}, u32[]{:S(2)}, u32[]{:S(2)}) collective-permute-start(f32[4,1024]{1,0:T(4,128)S(1)} %pad_maximum_fusion.27), channel_id=1, source_target_pairs={{0,2},{2,0},{1,3},{3,1},{4,6},{6,4},{5,7},{7,5},{8,10},{10,8},{9,1... | collective-permute-start | bytes 49160 | tf_op jit(solution)/shard_map/ppermute | solution.py:22
  4.6 30.2 %collective-permute-start.6 = (bf16[128,1024]{1,0:T(8,128)(2,1)S(1)}, bf16[128,1024]{1,0:T(8,128)(2,1)}, u32[]{:S(2)}, u32[]{:S(2)}) collective-permute-start(bf16[128,1024]{1,0:T(8,128)(2,1)S(1)} %constant_dynamic-slice_fusion.12), channel_id=1, source_target_pairs={{0,2},{2,0},{1,3},{3,1},{4,6},{6,4},{5,7},{7,5},{8,10},{10,8},{9,1... | collective-permute-start | bytes 786440 | tf_op jit(solution)/shard_map/ppermute | solution.py:22
  5.4 31.2 %collective-permute-start = (bf16[512,1024]{1,0:T(8,128)(2,1)}, bf16[512,1024]{1,0:T(8,128)(2,1)}, u32[]{:S(2)}, u32[]{:S(2)}) collective-permute-start(bf16[512,1024]{1,0:T(8,128)(2,1)} %param.12), channel_id=1, source_target_pairs={{0,2},{2,0},{1,3},{3,1},{4,6},{6,4},{5,7},{7,5},{8,10},{10,8},{9,1... | collective-permute-start | bytes 3145736 | tf_op jit(solution)/shard_map/ppermute | solution.py:22
  18.2 33.8 %collective-permute-start.3 = (bf16[256,1536]{1,0:T(8,128)(2,1)}, bf16[256,1536]{1,0:T(8,128)(2,1)}, u32[]{:S(2)}, u32[]{:S(2)}) collective-permute-start(bf16[256,1536]{1,0:T(8,128)(2,1)} %fusion.33), channel_id=1, source_target_pairs={{0,2},{2,0},{1,3},{3,1},{4,6},{6,4},{5,7},{7,5},{8,10},{10,8},{9,1... | collective-permute-start | bytes 2359304 | tf_op jit(solution)/shard_map/ppermute | solution.py:22
  37.9 37.3 %collective-permute-start.1 = (bf16[512,2048]{1,0:T(8,128)(2,1)S(1)}, bf16[512,2048]{1,0:T(8,128)(2,1)S(1)}, u32[]{:S(2)}, u32[]{:S(2)}) collective-permute-start(bf16[512,2048]{1,0:T(8,128)(2,1)S(1)} %constant_dynamic-update-slice_fusion), channel_id=1, source_target_pairs={{0,1},{1,0},{2,3},{3,2},{4,5},{5,4},{6,7},{7,6},{8,9},{9,8},{10,11... | collective-permute-start | bytes 6291464 | tf_op jit(solution)/shard_map/ppermute | solution.py:22
  51.9 20.3 %collective-permute-start.4 = (bf16[256,1536]{1,0:T(8,128)(2,1)}, bf16[256,1536]{1,0:T(8,128)(2,1)S(1)}, u32[]{:S(2)}, u32[]{:S(2)}) collective-permute-start(bf16[256,1536]{1,0:T(8,128)(2,1)} %collective-permute-done.3), channel_id=1, source_target_pairs={{0,8},{4,12},{8,0},{12,4},{16,24},{20,28},{24,16},{28,20},{1,9},{5... | collective-permute-start | bytes 2359304 | tf_op jit(solution)/shard_map/ppermute | solution.py:81
  73.6 34.5 %collective-permute-start.5 = (bf16[512,1536]{1,0:T(8,128)(2,1)S(1)}, bf16[512,1536]{1,0:T(8,128)(2,1)S(1)}, u32[]{:S(2)}, u32[]{:S(2)}) collective-permute-start(bf16[512,1536]{1,0:T(8,128)(2,1)S(1)} %pad_maximum_fusion.15), channel_id=1, source_target_pairs={{0,4},{4,0},{8,12},{12,8},{16,20},{20,16},{24,28},{28,24},{1,5},{5... | collective-permute-start | bytes 4718600 | tf_op jit(solution)/shard_map/ppermute | solution.py:81
  167.8 86.5 %collective-permute-start.9 = (bf16[512,2048]{1,0:T(8,128)(2,1)}, bf16[512,2048]{1,0:T(8,128)(2,1)}, u32[]{:S(2)}, u32[]{:S(2)}) collective-permute-start(bf16[512,2048]{1,0:T(8,128)(2,1)} %constant_dynamic-slice_fusion.11), channel_id=1, source_target_pairs={{0,1},{1,0},{2,3},{3,2},{4,5},{5,4},{6,7},{7,6},{8,9},{9,8},{10,11... | collective-permute-start | bytes 6291464 | tf_op jit(solution)/shard_map/ppermute | solution.py:22
  178.3 34.8 %collective-permute-start.11 = (bf16[256,2,1408]{0,2,1:T(8,128)(2,1)}, bf16[256,2,1408]{0,2,1:T(8,128)(2,1)}, u32[]{:S(2)}, u32[]{:S(2)}) collective-permute-start(bf16[256,2,1408]{0,2,1:T(8,128)(2,1)} %copy.41), channel_id=1, source_target_pairs={{0,2},{2,0},{1,3},{3,1},{4,6},{6,4},{5,7},{7,5},{8,10},{10,8},{9,1... | collective-permute-start | bytes 4325384 | tf_op jit(solution)/shard_map/ppermute | solution.py:22
  180.0 72.0 %collective-permute-start.22 = (bf16[512,1024]{1,0:T(8,128)(2,1)}, bf16[512,1024]{1,0:T(8,128)(2,1)}, u32[]{:S(2)}, u32[]{:S(2)}) collective-permute-start(bf16[512,1024]{1,0:T(8,128)(2,1)} %param.23), channel_id=1, source_target_pairs={{0,2},{2,0},{1,3},{3,1},{4,6},{6,4},{5,7},{7,5},{8,10},{10,8},{9,1... | collective-permute-start | bytes 3145736 | tf_op jit(solution)/shard_map/ppermute | solution.py:22
  182.6 67.8 %collective-permute-start.16 = (bf16[352,1024]{1,0:T(8,128)(2,1)}, bf16[352,1024]{1,0:T(8,128)(2,1)S(1)}, u32[]{:S(2)}, u32[]{:S(2)}) collective-permute-start(bf16[352,1024]{1,0:T(8,128)(2,1)} %constant_dynamic-slice_fusion.6), channel_id=1, source_target_pairs={{0,2},{2,0},{1,3},{3,1},{4,6},{6,4},{5,7},{7,5},{8,10},{10,8},{9,1... | collective-permute-start | bytes 2162696 | tf_op jit(solution)/shard_map/ppermute | solution.py:22
  213.0 59.3 %collective-permute-start.12 = (bf16[256,2,1408]{0,2,1:T(8,128)(2,1)}, bf16[256,2,1408]{0,2,1:T(8,128)(2,1)}, u32[]{:S(2)}, u32[]{:S(2)}) collective-permute-start(bf16[256,2,1408]{0,2,1:T(8,128)(2,1)} %collective-permute-done.11), channel_id=1, source_target_pairs={{0,4},{4,0},{8,12},{12,8},{16,20},{20,16},{24,28},{28,24},{1,5},{5... | collective-permute-start | bytes 4325384 | tf_op jit(solution)/shard_map/ppermute | solution.py:81
  254.3 67.4 %collective-permute-start.23 = (bf16[512,2048]{1,0:T(8,128)(2,1)}, bf16[512,2048]{1,0:T(8,128)(2,1)}, u32[]{:S(2)}, u32[]{:S(2)}) collective-permute-start(bf16[512,2048]{1,0:T(8,128)(2,1)} %constant_dynamic-update-slice_fusion.2), channel_id=1, source_target_pairs={{0,1},{1,0},{2,3},{3,2},{4,5},{5,4},{6,7},{7,6},{8,9},{9,8},{10,11... | collective-permute-start | bytes 6291464 | tf_op jit(solution)/shard_map/ppermute | solution.py:22
  257.4 25.6 %collective-permute-start.10 = (bf16[256,2048]{1,0:T(8,128)(2,1)S(1)}, bf16[256,2048]{1,0:T(8,128)(2,1)S(1)}, u32[]{:S(2)}, u32[]{:S(2)}) collective-permute-start(bf16[256,2048]{1,0:T(8,128)(2,1)S(1)} %constant_dynamic-slice_fusion.10), channel_id=1, source_target_pairs={{0,2},{2,0},{1,3},{3,1},{4,6},{6,4},{5,7},{7,5},{8,10},{10,8},{9,1... | collective-permute-start | bytes 3145736 | tf_op jit(solution)/shard_map/ppermute | solution.py:22
  270.8 47.1 %collective-permute-start.18 = (bf16[704,1024]{1,0:T(8,128)(2,1)}, bf16[704,1024]{1,0:T(8,128)(2,1)}, u32[]{:S(2)}, u32[]{:S(2)}) collective-permute-start(bf16[704,1024]{1,0:T(8,128)(2,1)} %pad_maximum_fusion.17), channel_id=1, source_target_pairs={{0,4},{4,0},{8,12},{12,8},{16,20},{20,16},{24,28},{28,24},{1,5},{5... | collective-permute-start | bytes 4325384 | tf_op jit(solution)/shard_map/ppermute | solution.py:81
  286.5 25.2 %collective-permute-start.14 = (bf16[256,2048]{1,0:T(8,128)(2,1)}, bf16[256,2048]{1,0:T(8,128)(2,1)}, u32[]{:S(2)}, u32[]{:S(2)}) collective-permute-start(bf16[256,2048]{1,0:T(8,128)(2,1)} %add_convert_fusion.5), channel_id=1, source_target_pairs={{0,2},{2,0},{1,3},{3,1},{4,6},{6,4},{5,7},{7,5},{8,10},{10,8},{9,1... | collective-permute-start | bytes 3145736 | tf_op jit(solution)/shard_map/ppermute | solution.py:22
  290.0 64.2 %collective-permute-start.13 = (bf16[512,2,1408]{0,2,1:T(8,128)(2,1)}, bf16[512,2,1408]{0,2,1:T(8,128)(2,1)}, u32[]{:S(2)}, u32[]{:S(2)}) collective-permute-start(bf16[512,2,1408]{0,2,1:T(8,128)(2,1)} %pad_maximum_fusion.11), channel_id=1, source_target_pairs={{0,8},{4,12},{8,0},{12,4},{16,24},{20,28},{24,16},{28,20},{1,9},{5... | collective-permute-start | bytes 8650760 | tf_op jit(solution)/shard_map/ppermute | solution.py:81
  314.0 44.5 %collective-permute-start.15 = (bf16[512,2048]{1,0:T(8,128)(2,1)S(1)}, bf16[512,2048]{1,0:T(8,128)(2,1)S(1)}, u32[]{:S(2)}, u32[]{:S(2)}) collective-permute-start(bf16[512,2048]{1,0:T(8,128)(2,1)S(1)} %pad_maximum_fusion.12), channel_id=1, source_target_pairs={{0,1},{1,0},{2,3},{3,2},{4,5},{5,4},{6,7},{7,6},{8,9},{9,8},{10,11... | collective-permute-start | bytes 6291464 | tf_op jit(solution)/shard_map/ppermute | solution.py:22
  432.1 26.1 %collective-permute-start.25 = (bf16[256,2048]{1,0:T(8,128)(2,1)S(1)}, bf16[256,2048]{1,0:T(8,128)(2,1)S(1)}, u32[]{:S(2)}, u32[]{:S(2)}) collective-permute-start(bf16[256,2048]{1,0:T(8,128)(2,1)S(1)} %constant_dynamic-slice_fusion.2), channel_id=1, source_target_pairs={{0,2},{2,0},{1,3},{3,1},{4,6},{6,4},{5,7},{7,5},{8,10},{10,8},{9,1... | collective-permute-start | bytes 3145736 | tf_op jit(solution)/shard_map/ppermute | solution.py:22
  434.4 45.4 %collective-permute-start.20 = (bf16[256,2048]{1,0:T(8,128)(2,1)S(1)}, bf16[256,2048]{1,0:T(8,128)(2,1)S(1)}, u32[]{:S(2)}, u32[]{:S(2)}) collective-permute-start(bf16[256,2048]{1,0:T(8,128)(2,1)S(1)} %constant_dynamic-slice_fusion.4), channel_id=1, source_target_pairs={{0,2},{2,0},{1,3},{3,1},{4,6},{6,4},{5,7},{7,5},{8,10},{10,8},{9,1... | collective-permute-start | bytes 3145736 | tf_op jit(solution)/shard_map/ppermute | solution.py:22
  482.1 24.4 %collective-permute-start.26 = (bf16[256,2048]{1,0:T(8,128)(2,1)S(1)}, bf16[256,2048]{1,0:T(8,128)(2,1)S(1)}, u32[]{:S(2)}, u32[]{:S(2)}) collective-permute-start(bf16[256,2048]{1,0:T(8,128)(2,1)S(1)} %get-tuple-element.43), channel_id=1, source_target_pairs={{0,2},{2,0},{1,3},{3,1},{4,6},{6,4},{5,7},{7,5},{8,10},{10,8},{9,1... | collective-permute-start | bytes 3145736 | tf_op jit(solution)/shard_map/ppermute | solution.py:22
  575.7 33.6 %collective-permute-start.29 = (bf16[256,2048]{1,0:T(8,128)(2,1)S(1)}, bf16[256,2048]{1,0:T(8,128)(2,1)S(1)}, u32[]{:S(2)}, u32[]{:S(2)}) collective-permute-start(bf16[256,2048]{1,0:T(8,128)(2,1)S(1)} %constant_dynamic-slice_fusion), channel_id=1, source_target_pairs={{0,2},{2,0},{1,3},{3,1},{4,6},{6,4},{5,7},{7,5},{8,10},{10,8},{9,1... | collective-permute-start | bytes 3145736 | tf_op jit(solution)/shard_map/ppermute | solution.py:22
  623.4 543.1 %collective-permute-start.30 = (f32[256,1024]{1,0:T(8,128)}, f32[256,1024]{1,0:T(8,128)}, u32[]{:S(2)}, u32[]{:S(2)}) collective-permute-start(f32[256,1024]{1,0:T(8,128)} %slice.201), channel_id=1, source_target_pairs={{0,2},{2,0},{1,3},{3,1},{4,6},{6,4},{5,7},{7,5},{8,10},{10,8},{9,1... | collective-permute-start | bytes 3145736 | tf_op jit(solution)/shard_map/ppermute | solution.py:22
  624.1 538.0 %collective-permute-start.35 = (f32[5632]{0:T(1024)S(1)}, f32[5632]{0:T(1024)S(1)}, u32[]{:S(2)}, u32[]{:S(2)}) collective-permute-start(f32[5632]{0:T(1024)S(1)} %add.230), channel_id=1, source_target_pairs={{0,16},{4,20},{8,24},{12,28},{16,0},{20,4},{24,8},{28,12},{1,17},{... | collective-permute-start | bytes 67592 | tf_op jit(solution)/shard_map/ppermute | solution.py:750
  (84 other events, 1010.6 us)

commit v3 on v2

--- a/solution.py
+++ b/solution.py
@@ -16,6 +16,7 @@
 BF = jnp.bfloat16
 F32 = jnp.float32
 SWAP = [(0, 1), (1, 0)]
+MESH = pl.DeviceIdType.MESH
 
 
 def swap(v, axis):
@@ -66,23 +67,6 @@
     return [(i, i ^ bit) for i in range(count)]
 
 
-def fetch(send, place, y_first):
-    count = place.count
-    if count % 4:
-        return swap(send, "row")
-    if y_first:
-        index = place.zp * 2 + place.y
-        steps = ((1, place.y), (2, place.zp))
-    else:
-        index = place.y * 2 + place.zp
-        steps = ((2, place.zp), (1, place.y))
-    held = swap(piece(send, index, 4), "row")
-    for bit, flag in steps:
-        other = lax.ppermute(held, "dp", dp_perm(bit, count))
-        held = ordered(flag, held, other)
-    return held
-
-
 def cross(v):
     half = v.shape[-1] // 2
     return jnp.concatenate([v[..., half:], v[..., :half]], axis=-1)
@@ -164,30 +148,6 @@
 
 def tn(a, b):
     return lax.dot_general(a, b, (((0,), (0,)), ((), ())), preferred_element_type=F32)
-
-
-def forward_kernel(q_in, k_in, v_in, bias_ref, starts_ref, table_ref, q_ref, k_ref, v_ref, out_ref, raw_ref, log_ref):
-    length = q_in.shape[0]
-    table = (table_ref[0], table_ref[1], table_ref[2])
-    q_ref[...] = (turned(q_in[...] + bias_ref[0, 0:1], table).astype(BF).astype(F32) * HEAD ** (-0.5)).astype(BF)
-    k_ref[...] = turned(k_in[...] + bias_ref[0, 1:2], table).astype(BF)
-    v_ref[...] = (v_in[...] + bias_ref[0, 2:3]).astype(BF)
-    for begin, low, end in windows(length):
-        bar = barred(starts_ref[begin:end], begin, low, end)
-        outs = []
-        for h in range(2):
-            lanes = slice(h * HEAD, (h + 1) * HEAD)
-            scores = nt(q_ref[begin:end, lanes], k_ref[low:end, lanes]) + bar
-            maxima = jnp.max(scores, axis=1, keepdims=True)
-            shifted = jnp.exp(scores - maxima).astype(BF)
-            wide = jnp.concatenate([v_ref[low:end, lanes], jnp.ones((end - low, HEAD), BF)], axis=1)
-            got = jnp.dot(shifted, wide, preferred_element_type=F32)
-            totals = got[:, HEAD : HEAD + 1]
-            outs.append(got[:, :HEAD] / totals)
-            log_ref[0, begin:end, h : h + 1] = maxima + jnp.log(totals)
-        out = jnp.concatenate(outs, axis=1)
-        raw_ref[begin:end] = out
-        out_ref[begin:end] = out.astype(BF)
 
 
 def backward_kernel(q_ref, k_ref, v_ref, g_ref, raw_ref, log_ref, starts_ref, table_ref, dq_ref, dk_ref, dv_ref, dk_acc, dv_acc):
@@ -225,28 +185,6 @@
     return jnp.stack([jnp.concatenate([v, v], axis=1) for v in (one, ahead, behind)])
 
 
-def attention_forward(joined, bias, starts, table):
-    length, pairs = joined.shape[0], bias.shape[0]
-    units = pairs * 128
-    part = lambda n: pl.BlockSpec((length, 128), lambda p, n=n: (0, n * pairs + p))
-    same = pl.BlockSpec((length, 128), lambda p: (0, p))
-    half = jax.ShapeDtypeStruct((length, units), BF)
-    return pl.pallas_call(
-        forward_kernel,
-        grid=(pairs,),
-        in_specs=[
-            part(0), part(1), part(2),
-            pl.BlockSpec((1, 3, 128), lambda p: (p, 0, 0)),
-            pl.BlockSpec((length, 1), lambda p: (0, 0)),
-            pl.BlockSpec((3, length, 128), lambda p: (0, 0, 0)),
-        ],
-        out_specs=[same] * 5 + [pl.BlockSpec((1, length, 2), lambda p: (p, 0, 0))],
-        out_shape=[half] * 4 + [jax.ShapeDtypeStruct((length, units), F32), jax.ShapeDtypeStruct((pairs, length, 2), F32)],
-        compiler_params=pltpu.CompilerParams(vmem_limit_bytes=48 * 2**20),
-        cost_estimate=pl.CostEstimate(flops=pairs * 2 * length * 640 * 256, bytes_accessed=12 * 2**20, transcendentals=pairs * 2 * length * 640),
-    )(joined, joined, joined, bias, starts, table)
-
-
 def attention_backward(queries, keys, values, grads, raw, logs, starts, table):
     length, units = queries.shape
     pairs = units // 128
@@ -269,14 +207,12 @@
     )(queries, keys, values, grads, raw, logs, starts, table)
 
 
-MESH = pl.DeviceIdType.MESH
-
 BR = 512
 BC = 256
 SLOTS = 6
 
 
-def gradient_kernel(segments, half, *refs):
+def gradient_kernel(segments, bases, half, *refs):
     count = len(segments)
     total = sum(s[1] for s in segments)
     sources = refs[: 2 * count]
@@ -351,8 +287,15 @@
     def slot(u):
         return lax.rem(u, SLOTS)
 
+    def spot(u):
+        place, first = u, 0
+        for (_, blocks), base in zip(segments, bases):
+            place = jnp.where(u >= first, u + (base - first), place)
+            first += blocks
+        return place
+
     def out_half(ref, u, index):
-        return ref.at[u, halves(index)]
+        return ref.at[spot(u), halves(index)]
 
     def x_copy(u):
         return copy("x", u, x_src.at[slot(u)], x_dst.at[slot(u)], x_peer)
@@ -379,7 +322,7 @@
         return copy("fi", u, x_dst.at[slot(u)], f_dst.at[slot(u)], e_peer)
 
     def f_out(u):
-        return copy("fo", u, whole.at[slot(u)], out_got.at[u], e_peer)
+        return copy("fo", u, whole.at[slot(u)], out_got.at[spot(u)], e_peer)
 
     def n_copy(u):
         return copy("n", u, deep.at[slot(u), halves(1 - upper)], n_dst.at[slot(u)], m_peer)
@@ -395,7 +338,7 @@
         return pltpu.make_async_copy(src, out_half(out_own, u, y), store_own.at[slot(u)])
 
     def keep_got(u):
-        return pltpu.make_async_copy(whole.at[slot(u)], out_got.at[u], store_got.at[slot(u)])
+        return pltpu.make_async_copy(whole.at[slot(u)], out_got.at[spot(u)], store_got.at[slot(u)])
 
     def stage(u, fn, role=None):
         ok = (u >= 0) & (u < total)
@@ -534,11 +477,15 @@
         operands += [left, right]
     total = sum(s[1] for s in segments)
     tokens = operands[0].shape[0]
+    bases, end = [], 0
+    for _, blocks in segments:
+        bases.append(-(-end // blocks) * blocks)
+        end = bases[-1] + blocks
     wide, thin = pltpu.VMEM((SLOTS, BR, BC), BF), pltpu.VMEM((SLOTS, BR // 2, BC), BF)
     dma = pltpu.SemaphoreType.DMA((SLOTS,))
-    return pl.pallas_call(
-        functools.partial(gradient_kernel, segments, half),
-        out_shape=jax.ShapeDtypeStruct((2, total, BR, BC), BF),
+    sums = pl.pallas_call(
+        functools.partial(gradient_kernel, segments, bases, half),
+        out_shape=jax.ShapeDtypeStruct((2, end, BR, BC), BF),
         in_specs=[pl.BlockSpec(memory_space=pl.ANY)] * len(operands),
         out_specs=pl.BlockSpec(memory_space=pl.ANY),
         scratch_shapes=[pltpu.VMEM(v.shape, v.dtype) for v in operands]
@@ -552,72 +499,70 @@
             flops=4 * total * BR * BC * tokens, bytes_accessed=4 * total * BR * BC, transcendentals=0
         ),
     )(*operands)
-
-
-def spread_kernel(side_ref, block_ref, out_ref):
-    for i in range(block_ref.shape[1]):
-        out_ref[0, i * BR : (i + 1) * BR] = block_ref[0, i].astype(F32)
-
-
-def spread_pair_kernel(side_ref, gate_ref, up_ref, out_ref):
-    for i in range(gate_ref.shape[1]):
-        out_ref[i * BR : (i + 1) * BR, 0, :] = gate_ref[0, i].astype(F32)
-        out_ref[i * BR : (i + 1) * BR, 1, :] = up_ref[0, i].astype(F32)
+    return sums, bases
+
+
+def spread_qkv_kernel(side_ref, block_ref, out_ref):
+    per = out_ref.shape[2] // BC
+    for j in range(block_ref.shape[1]):
+        at = j % per * BC
+        out_ref[j // per, :, at : at + BC] = block_ref[0, j].astype(F32)
+
+
+def spread_pair_kernel(side_ref, block_ref, out_ref):
+    units = out_ref.shape[2]
+    for j in range(block_ref.shape[1]):
+        for at in range(0, BC, 128):
+            unit = j * BC + at
+            out_ref[:, unit // units, unit % units : unit % units + 128] = block_ref[
+                0, j, :, at : at + 128
+            ].astype(F32)
 
 
 def spread_rows_kernel(side_ref, block_ref, out_ref):
-    size = out_ref.shape[0]
-    for q in range(BR // size):
-        out_ref[:, q * BC : (q + 1) * BC] = block_ref[0, 0, q * size : (q + 1) * size].astype(F32)
-
-
-def spread(body, side, blocks, grid, in_specs, out_spec, out_shape):
+    size = block_ref.shape[2]
+    for k in range(block_ref.shape[1]):
+        out_ref[k * size : (k + 1) * size] = block_ref[0, k].astype(F32)
+
+
+def spread(body, side, blocks, steps, in_spec, out_spec, out_shape):
     return pl.pallas_call(
         body,
         grid_spec=pltpu.PrefetchScalarGridSpec(
-            num_scalar_prefetch=1, grid=grid, in_specs=in_specs, out_specs=out_spec
+            num_scalar_prefetch=1, grid=(2, steps), in_specs=[in_spec], out_specs=out_spec
         ),
         out_shape=jax.ShapeDtypeStruct(out_shape, F32),
         compiler_params=pltpu.CompilerParams(vmem_limit_bytes=48 * 2**20),
-    )(side, *([blocks] * len(in_specs)))
+    )(side, blocks)
 
 
 def place_of(which, side_ref):
     return which + side_ref[0] - 2 * which * side_ref[0]
 
 
-def spread_qkv(side, blocks, base, half, units):
-    per, kind_blocks = half // BR, units // BC
-    return spread(
-        spread_kernel,
-        side,
-        blocks,
-        (2, 3 * kind_blocks, per),
-        [pl.BlockSpec((1, 1, BR, BC), lambda w, j, i, s: (w, base + i * 3 * kind_blocks + j, 0, 0))],
-        pl.BlockSpec(
-            (1, BR, BC),
-            lambda w, j, i, s: (j // kind_blocks, i, place_of(w, s) * kind_blocks + j % kind_blocks),
-        ),
-        (3, half, 2 * units),
-    ).transpose(1, 0, 2)
-
-
-def spread_gate_up(side, blocks, base, half, units):
-    tiles, columns = units // 128, 2 * units // BC
-
-    def block_of(w, i, f):
-        return (w, base + i * columns + f // (BC // 128), 0, f % (BC // 128))
-
+def spread_columns(side, blocks, base, half, units, kinds, rows):
+    columns, per = kinds * units // BC, BR // rows
+    first = base // columns
+    in_spec = pl.BlockSpec(
+        (1, columns, rows, BC), lambda w, i, s: (w, first + i // per, i % per, 0)
+    )
+    if kinds == 3:
+        return spread(
+            spread_qkv_kernel,
+            side,
+            blocks,
+            half // rows,
+            in_spec,
+            pl.BlockSpec((3, rows, units), lambda w, i, s: (0, i, place_of(w, s))),
+            (3, half, 2 * units),
+        ).transpose(1, 0, 2)
     return spread(
         spread_pair_kernel,
         side,
         blocks,
-        (2, half // BR, tiles),
-        [
-            pl.BlockSpec((1, 1, BR, 128), lambda w, i, f, s: block_of(w, i, f)),
-            pl.BlockSpec((1, 1, BR, 128), lambda w, i, f, s: block_of(w, i, tiles + f)),
-        ],
-        pl.BlockSpec((BR, 2, 128), lambda w, i, f, s: (i, 0, place_of(w, s) * tiles + f)),
+        half // rows,
+        in_spec,
+        pl.BlockSpec((rows, 2, units), lambda w, i, s: (i, 0, place_of(w, s))),
         (half, 2, 2 * units),
     )
 
@@ -629,11 +574,449 @@
         spread_rows_kernel,
         side,
         blocks,
-        (2, count),
-        [pl.BlockSpec((1, 1, BR, BC), lambda w, k, s: (w, base + k, 0, 0))],
-        pl.BlockSpec((size, half), lambda w, k, s: (place_of(w, s) * count + k, 0)),
+        half // BC,
+        pl.BlockSpec((1, count, size, BC), lambda w, q, s: (w, base // count, q, 0)),
+        pl.BlockSpec((units, BC), lambda w, q, s: (place_of(w, s), q)),
         (2 * units, half),
     )
+
+
+def front_kernel(
+    tokens,
+    starts_ref,
+    table_ref,
+    params_ref,
+    bias_ref,
+    qkv_w,
+    out_w,
+    gate_w,
+    down_w,
+    cotangent,
+    act_one,
+    q_out,
+    k_out,
+    v_out,
+    att_out,
+    raw_out,
+    log_out,
+    hid_out,
+    act_two,
+    gate_out,
+    up_out,
+    inner_out,
+    wq_out,
+    wo_out,
+    wg_out,
+    wd_out,
+    cot_out,
+    own_out,
+    tok,
+    act,
+    wq,
+    wo,
+    wg,
+    gate_far,
+    gate_own,
+    qs,
+    ks,
+    vs,
+    att,
+    raw,
+    logs,
+    core_in,
+    row_src,
+    row_in,
+    own_in,
+    hid,
+    tile,
+    send_sem,
+    recv_sem,
+    load_sem,
+    store_sem,
+):
+    r, c, d = lax.axis_index("row"), lax.axis_index("col"), lax.axis_index("dp")
+    y, zp = lax.rem(d, 2), lax.rem(d // 2, 2)
+    length, width = tok.shape
+    half = width // 2
+    part, block = length // 2, length // 4
+    units, hidden = qs.shape[1], wg.shape[2]
+    sub = zp * 2 + y
+    dy, dz = 1 - 2 * y, 2 - 4 * zp
+    row_peer, col_peer = {"row": 1 - r}, {"col": 1 - c}
+    near = ({"dp": d + dy}, {"dp": d + dz}, {"dp": d + dy + dz})
+
+    barrier = pltpu.get_barrier_semaphore()
+    for peer in (row_peer, col_peer) + near:
+        pl.semaphore_signal(barrier, inc=1, device_id=peer, device_id_type=MESH)
+
+    stores = []
+
+    def span(start, size):
+        return pl.ds(pl.multiple_of(start, size), size)
+
+    def load(n, src, dst):
+        copy = pltpu.make_async_copy(src, dst, load_sem.at[n])
+        copy.start()
+        return copy
+
+    def store(src, dst):
+        copy = pltpu.make_async_copy(src, dst, store_sem.at[len(stores)])
+        copy.start()
+        stores.append(copy)
+        return copy
+
+    def remote(n, src, dst, peer):
+        return pltpu.make_async_remote_copy(
+            src_ref=src,
+            dst_ref=dst,
+            send_sem=send_sem.at[n],
+            recv_sem=recv_sem.at[n],
+            device_id=peer,
+            device_id_type=MESH,
+        )
+
+    mine, theirs = span(r * units, units), span((1 - r) * units, units)
+    own_rows, far_rows = span(c * part, part), span((1 - c) * part, part)
+    lo, hi = pl.ds(0, half), pl.ds(half, half)
+    quarter = half // 4
+    down_quarter = hidden // 4
+
+    load_tok = load(0, tokens, tok.at[own_rows, lo])
+    load_q = load(1, qkv_w.at[:, :, mine], wq.at[:, lo])
+    load_o = load(2, out_w.at[mine], wo.at[:, lo])
+    gate_cols = span(r * hidden, hidden)
+
+    def load_gate(i):
+        return load(3 + i % 2, gate_w.at[pl.ds(i * quarter, quarter), :, gate_cols], gate_own.at[i % 2])
+
+    load_d = load(5, down_w.at[span(r * hidden, hidden)], wd_out.at[:, lo])
+    load_c = load(6, cotangent, cot_out.at[own_rows, lo])
+    gates = [load_gate(0), load_gate(1)]
+
+    rows_sub = span(sub * quarter, quarter)
+    rows_far = span(half + sub * quarter, quarter)
+    q_x = remote(0, qkv_w.at[:, rows_sub, theirs], wq.at[:, rows_far], row_peer)
+    q_n = [remote(1 + k, wq.at[:, rows_far], wq.at[:, rows_far], p) for k, p in enumerate(near)]
+    tok_x = remote(4, tokens, tok.at[own_rows, hi], row_peer)
+    tok_c = remote(5, tokens, tok.at[own_rows, lo], col_peer)
+    tok_f = remote(6, tok.at[own_rows, hi], tok.at[own_rows, hi], col_peer)
+    out_rows = units // 4
+    out_sub = span(sub * out_rows, out_rows)
+    o_x = remote(
+        7, out_w.at[span((1 - r) * units + sub * out_rows, out_rows)], wo.at[out_sub, hi], row_peer
+    )
+    o_n = [remote(8 + k, wo.at[out_sub, hi], wo.at[out_sub, hi], p) for k, p in enumerate(near)]
+    g_x = remote(
+        11, gate_w.at[rows_sub, :, span((1 - r) * hidden, hidden)], gate_far.at[sub], row_peer
+    )
+    g_n = [remote(12 + k, gate_far.at[sub], gate_far.at[sub], p) for k, p in enumerate(near)]
+    down_sub = span(sub * down_quarter, down_quarter)
+    d_x = remote(
+        15,
+        down_w.at[span((1 - r) * hidden + sub * down_quarter, down_quarter)],
+        wd_out.at[down_sub, hi],
+        row_peer,
+    )
+    d_n = [
+        remote(16 + k, wd_out.at[down_sub, hi], wd_out.at[down_sub, hi], p)
+        for k, p in enumerate(near)
+    ]
+    c_x = remote(19, cotangent, cot_out.at[own_rows, hi], row_peer)
+    c_c = remote(20, cotangent, cot_out.at[own_rows, lo], col_peer)
+    c_f = remote(21, cot_out.at[own_rows, hi], cot_out.at[own_rows, hi], col_peer)
+    rs_c = remote(22, act.at[far_rows], core_in, col_peer)
+    rs_x = remote(23, row_src, row_in, row_peer)
+    own_block = span(c * part + r * block, block)
+    x_block = span(c * part + (1 - r) * block, block)
+    ag_x = [
+        remote(24, tok.at[own_block, lo], tok.at[own_block, hi], row_peer),
+        remote(25, tok.at[own_block, hi], tok.at[own_block, lo], row_peer),
+    ]
+    ag_c = remote(26, tok.at[own_block], tok.at[own_block], col_peer)
+    ag_f = remote(27, tok.at[x_block], tok.at[x_block], col_peer)
+
+    def start(copies):
+        for copy in copies:
+            copy.start()
+
+    def arrived(copies):
+        for copy in copies:
+            copy.wait_recv()
+
+    def part_gate(ref, at):
+        wg[0, at] = ref[:, 0, :]
+        wg[1, at] = ref[:, 1, :]
+
+    pl.semaphore_wait(barrier, 5)
+    q_x.start()
+    tok_c.start()
+    c_c.start()
+    for i in range(4):
+        if i == 2:
+            q_x.wait_recv()
+            start(q_n)
+            tok_x.start()
+        gates[i].wait()
+        part_gate(gate_own.at[i % 2], pl.ds(i * quarter, quarter))
+        if i + 2 < 4:
+            gates.append(load_gate(i + 2))
+    tok_x.wait_recv()
+    tok_f.start()
+    o_x.start()
+    g_x.start()
+
+    load_tok.wait()
+    tok_c.wait_recv()
+
+    def normed(v, at):
+        mean = jnp.sum(v, axis=1, keepdims=True) / width
+        spread_of = jnp.sum(v * v, axis=1, keepdims=True) / width - mean * mean
+        v = (v - mean) * lax.rsqrt(spread_of + EPSILON)
+        return (v * params_ref[at : at + 1] + params_ref[at + 1 : at + 2]).astype(BF)
+
+    norm_rows = 64
+
+    def norm_one(base):
+        def body(i, carry):
+            at = span(base + i * norm_rows, norm_rows)
+            act[at] = normed(tok[at].astype(F32), 0)
+            return carry
+
+        lax.fori_loop(0, part // norm_rows, body, 0)
+
+    norm_one(c * part)
+    own_in[...] = tok[own_block]
+    tok_f.wait_recv()
+    norm_one((1 - c) * part)
+    store(act, act_one)
+    store(own_in, own_out)
+
+    load_q.wait()
+    arrived(q_n)
+    o_x.wait_recv()
+    start(o_n)
+    store(wq, wq_out)
+    chunk = 256
+
+    def project(i, carry):
+        at = span(i * chunk, chunk)
+        rows = act[at]
+        for kind, ref in enumerate((qs, ks, vs)):
+            out = jnp.dot(rows, wq[kind], preferred_element_type=F32) + bias_ref[kind : kind + 1]
+            if kind == 2:
+                ref[at] = out.astype(BF)
+                continue
+            table = (table_ref[0, at], table_ref[1, at], table_ref[2, at])
+            for g in range(units // 128):
+                lanes = slice(g * 128, (g + 1) * 128)
+                v = turned(out[:, lanes], table).astype(BF)
+                if kind == 0:
+                    v = (v.astype(F32) * HEAD ** (-0.5)).astype(BF)
+                ref[at, lanes] = v
+        return carry
+
+    lax.fori_loop(0, length // chunk, project, 0)
+    for ref, out in ((qs, q_out), (ks, k_out), (vs, v_out)):
+        store(ref, out)
+
+    pairs = units // 128
+
+    def attend(p, carry):
+        @pl.when(p == pairs // 2)
+        def _():
+            g_x.wait_recv()
+            start(g_n)
+            d_x.start()
+
+        lane0 = p * 128
+        q2 = qs[:, span(lane0, 128)]
+        k2 = ks[:, span(lane0, 128)]
+        v2 = vs[:, span(lane0, 128)]
+        for begin, low, end in windows(length):
+            bar = barred(starts_ref[begin:end], begin, low, end)
+            outs = []
+            for h in range(2):
+                lanes = slice(h * HEAD, (h + 1) * HEAD)
+                scores = nt(q2[begin:end, lanes], k2[low:end, lanes]) + bar
+                maxima = jnp.max(scores, axis=1, keepdims=True)
+                shifted = jnp.exp(scores - maxima).astype(BF)
+                wide = jnp.concatenate([v2[low:end, lanes], jnp.ones((end - low, HEAD), BF)], axis=1)
+                got = jnp.dot(shifted, wide, preferred_element_type=F32)
+                totals = got[:, HEAD : HEAD + 1]
+                outs.append(got[:, :HEAD] / totals)
+                logs[p, begin:end, h : h + 1] = maxima + jnp.log(totals)
+            out = jnp.concatenate(outs, axis=1)
+            raw[begin:end, span(lane0, 128)] = out
+            att[begin:end, span(lane0, 128)] = out.astype(BF)
+        return carry
+
+    lax.fori_loop(0, pairs, attend, 0)
+    store(att, att_out)
+    store(raw, raw_out)
+    store(logs, log_out)
+
+    load_o.wait()
+    arrived(o_n)
+    store(wo, wo_out)
+    stores[0].wait()
+    tok_f.wait_send()
+
+    def branch(base):
+        def body(i, carry):
+            at = span(base + i * chunk, chunk)
+            act[at] = jnp.dot(att[at], wo[...], preferred_element_type=F32).astype(BF)
+            return carry
+
+        lax.fori_loop(0, part // chunk, body, 0)
+
+    branch((1 - c) * part)
+    rs_c.start()
+    branch(c * part)
+    rs_c.wait_recv()
+    row_src[...] = act[x_block] + core_in[span((1 - r) * block, block)]
+    rs_x.start()
+    part_gate(gate_far.at[sub], span(half + sub * quarter, quarter))
+    subs = (zp * 2 + 1 - y, (1 - zp) * 2 + y, (1 - zp) * 2 + 1 - y)
+    rs_x.wait_recv()
+    hid_rows = 64
+
+    def norm_two(i, carry):
+        at = span(i * hid_rows, hid_rows)
+        kept = act[span(c * part + r * block + i * hid_rows, hid_rows)].astype(F32)
+        kept = kept + core_in[span(r * block + i * hid_rows, hid_rows)].astype(F32)
+        got = row_in[at].astype(F32)
+        kept = kept + jnp.concatenate([got[:, half:], got[:, :half]], axis=1)
+        kept = own_in[at].astype(F32) + kept
+        hid[at] = kept
+        tok[span(c * part + r * block + i * hid_rows, hid_rows)] = normed(kept, 2)
+        return carry
+
+    lax.fori_loop(0, block // hid_rows, norm_two, 0)
+    start(ag_x)
+    ag_c.start()
+    store(hid, hid_out)
+    d_x.wait_recv()
+    start(d_n)
+    c_x.start()
+    for k in range(3):
+        g_n[k].wait_recv()
+        part_gate(gate_far.at[subs[k]], span(half + subs[k] * quarter, quarter))
+    store(wg, wg_out)
+
+    stores_of = []
+    columns = [(at, min(512, hidden - at)) for at in range(0, hidden, 512)]
+    for b in range(4):
+        cc = c if b % 2 == 0 else 1 - c
+        rr = r if b < 2 else 1 - r
+        at = span(cc * part + rr * block, block)
+        if b == 1:
+            ag_c.wait_recv()
+        elif b == 2:
+            arrived(ag_x)
+            ag_f.start()
+        elif b == 3:
+            ag_f.wait_recv()
+        s = b % 2
+        for copy in stores_of[3 * (b - 2) : 3 * (b - 1)] if b >= 2 else ():
+            copy.wait()
+        rows = tok[at]
+        for first, size in columns:
+            cols = slice(first, first + size)
+            gate = jnp.dot(rows, wg[0, :, cols], preferred_element_type=F32)
+            up = jnp.dot(rows, wg[1, :, cols], preferred_element_type=F32)
+            tile[s, 0, :, cols] = gate.astype(BF)
+            tile[s, 1, :, cols] = up.astype(BF)
+            tile[s, 2, :, cols] = (gate / (1.0 + jnp.exp(-gate)) * up).astype(BF)
+        for k, out in enumerate((gate_out, up_out, inner_out)):
+            copy = pltpu.make_async_copy(tile.at[s, k], out.at[at], load_sem.at[7 + 3 * s + k])
+            copy.start()
+            stores_of.append(copy)
+    store(tok, act_two)
+    c_x.wait_recv()
+    load_c.wait()
+    c_f.start()
+    for copy in stores_of[6:] + stores[1:] + [load_d]:
+        copy.wait()
+    arrived(d_n)
+    c_c.wait_recv()
+    c_f.wait_recv()
+    for copy in [q_x, tok_x, tok_c, o_x, g_x, d_x, c_x, c_c, c_f, rs_c, rs_x, ag_c, ag_f] + (
+        q_n + o_n + g_n + d_n + ag_x
+    ):
+        copy.wait_send()
+
+
+def front(tokens, starts, table, params, bias, qkv_w, out_w, gate_w, down_w, cotangent):
+    part, half = tokens.shape
+    length, width, block = 2 * part, 2 * half, part // 2
+    units, hidden = out_w.shape[0] // 2, down_w.shape[0] // 2
+    any_spec, vmem_spec = pl.BlockSpec(memory_space=pl.ANY), pl.BlockSpec(memory_space=pltpu.VMEM)
+    pairs = units // 128
+
+    def bf(*shape):
+        return jax.ShapeDtypeStruct(shape, BF)
+
+    def f32(*shape):
+        return jax.ShapeDtypeStruct(shape, F32)
+
+    outs = [
+        bf(length, width),
+        bf(length, units),
+        bf(length, units),
+        bf(length, units),
+        bf(length, units),
+        f32(length, units),
+        f32(pairs, length, 2),
+        f32(block, width),
+        bf(length, width),
+        bf(length, hidden),
+        bf(length, hidden),
+        bf(length, hidden),
+        bf(3, width, units),
+        bf(units, width),
+        bf(2, width, hidden),
+        bf(hidden, width),
+        bf(length, width),
+        bf(block, width),
+    ]
+    scratch = [
+        bf(length, width),
+        bf(length, width),
+        bf(3, width, units),
+        bf(units, width),
+        bf(2, width, hidden),
+        bf(4, half // 4, 2, hidden),
+        bf(2, half // 4, 2, hidden),
+        bf(length, units),
+        bf(length, units),
+        bf(length, units),
+        bf(length, units),
+        f32(length, units),
+        f32(pairs, length, 2),
+        bf(part, width),
+        bf(block, width),
+        bf(block, width),
+        bf(block, width),
+        f32(block, width),
+        bf(2, 3, block, hidden),
+    ]
+    dma = pltpu.SemaphoreType.DMA
+    return pl.pallas_call(
+        front_kernel,
+        out_shape=outs,
+        in_specs=[any_spec] + [vmem_spec] * 4 + [any_spec] * 5,
+        out_specs=[any_spec] * len(outs),
+        scratch_shapes=[pltpu.VMEM(v.shape, v.dtype) for v in scratch]
+        + [dma((28,)), dma((28,)), dma((13,)), dma((16,))],
+        compiler_params=pltpu.CompilerParams(
+            collective_id=2, has_side_effects=True, vmem_limit_bytes=62 * 2**20
+        ),
+        cost_estimate=pl.CostEstimate(
+            flops=2 * length * width * (4 * units + 2 * hidden),
+            bytes_accessed=100 * 2**20,
+            transcendentals=length * 2048,
+        ),
+    )(tokens, starts, table, params, bias, qkv_w, out_w, gate_w, down_w, cotangent)
 
 
 def local(
@@ -660,51 +1043,47 @@
     heads = units // HEAD
     hidden = gate_up_weight.shape[2] // 2
 
-    other = swap(tokens, "row")
-    mine = jnp.concatenate([tokens, other], axis=1)
-    tokens_all = ordered(c, mine, swap(mine, "col"))
     params = jnp.stack([ln1_gain, ln1_bias, ln2_gain, ln2_bias])
     params = jnp.concatenate([params, swap(params, "row")], axis=1)
-
-    qkv_flat = [qkv_weight[:, k] for k in range(3)]
-    qkv_own = jnp.concatenate([piece(w, r, 2, 1) for w in qkv_flat], axis=1)
-    qkv_send = jnp.concatenate([piece(w, 1 - r, 2, 1) for w in qkv_flat], axis=1)
-    w_qkv = jnp.concatenate([qkv_own, fetch(qkv_send, place, False)], axis=0)
-    w_out = jnp.concatenate(
-        [piece(out_weight, r, 2), fetch(piece(out_weight, 1 - r, 2), place, True)], axis=1
-    )
-    w_gate = jnp.concatenate(
-        [
-            piece(gate_up_weight, r, 2, 2),
-            fetch(piece(gate_up_weight, 1 - r, 2, 2), place, True),
-        ],
-        axis=0,
-    )
-    cot_other = swap(cotangent, "row")
-    cot_mine = jnp.concatenate([cotangent, cot_other], axis=1)
-    cot_all = ordered(c, cot_mine, swap(cot_mine, "col"))
-    w_down = jnp.concatenate(
-        [piece(down_weight, r, 2), fetch(piece(down_weight, 1 - r, 2), place, False)], axis=1
-    )
-
     cosines, sines = rotary_tables(ids)
     table = tables(cosines, sines)
-    inputs = tokens_all.astype(F32)
-    normed, _, _ = norm_forward(inputs, params[0], params[1])
-    act_one = normed.astype(BF)
-    joined = dot(act_one, w_qkv)
     starts = (jnp.arange(length, dtype=jnp.int32) - doc_positions(ids))[:, None]
-    bias = piece(qkv_bias, r, 2, 1).reshape(3, units // 128, 128).transpose(1, 0, 2)
-    queries, keys, values, attended, raw, logs = attention_forward(joined, bias, starts, table)
+    bias = piece(qkv_bias, r, 2, 1)
+    (
+        act_one,
+        queries,
+        keys,
+        values,
+        attended,
+        raw,
+        logs,
+        hidden_state,
+        act_two,
+        gate,
+        up,
+        inner,
+        w_qkv,
+        w_out,
+        w_gate,
+        w_down,
+        cot_all,
+        own_inputs,
+    ) = front(
+        tokens,
+        starts,
+        table,
+        params,
+        bias,
+        qkv_weight.transpose(1, 0, 2),
+        out_weight,
+        gate_up_weight,
+        down_weight,
+        cotangent,
+    )
     block = c * 2 + r
-    own_inputs = piece(tokens_all, block, 4).astype(F32)
-    branch = reduce_blocks(dot(attended, w_out).astype(BF), place)
-    hidden_state = own_inputs + branch
-    normed, normal_two, inverse_two = norm_forward(hidden_state, params[2], params[3])
-    act_two = gather_blocks(normed.astype(BF), place)
-    gate_up = jnp.einsum("sd,dkf->ksf", act_two, w_gate, preferred_element_type=F32)
-    gate, up = gate_up[0], gate_up[1]
-    inner = (jax.nn.silu(gate) * up).astype(BF)
+    own_inputs = own_inputs.astype(F32)
+    _, normal_two, inverse_two = norm_forward(hidden_state, params[2], params[3])
+    gate, up = gate.astype(F32), up.astype(F32)
 
     feed = reduce_blocks(dot(inner, w_down).astype(BF), place)
     result = (hidden_state + feed).astype(BF)
@@ -718,7 +1097,7 @@
     grad_two = jnp.stack([grad_gate, grad_up])
     grad_pair = jnp.concatenate([grad_gate, grad_up], axis=1)
     grad_act_two = reduce_blocks(
-        jnp.einsum("ksf,dkf->sd", grad_two, w_gate, preferred_element_type=F32).astype(BF), place
+        jnp.einsum("ksf,kdf->sd", grad_two, w_gate, preferred_element_type=F32).astype(BF), place
     )
     grad_norm, ln2_gain_grad, ln2_bias_grad = norm_backward(
         grad_act_two, normal_two, inverse_two, params[2]
@@ -732,7 +1111,10 @@
     )
     grad_joined = jnp.concatenate(grad_joined, axis=1)
     bias_grad = jnp.sum(grad_joined, axis=0, dtype=F32)
-    grad_act_one = reduce_blocks(dot_t(grad_joined, w_qkv).astype(BF), place)
+    grad_kinds = grad_joined.reshape(length, 3, units)
+    grad_act_one = reduce_blocks(
+        jnp.einsum("sku,kdu->sd", grad_kinds, w_qkv, preferred_element_type=F32).astype(BF), place
+    )
     _, normal_one, inverse_one = norm_forward(own_inputs, params[0], params[1])
     grad_norm, ln1_gain_grad, ln1_bias_grad = norm_backward(
         grad_act_one, normal_one, inverse_one, params[0]
@@ -761,15 +1143,12 @@
         ("U", inner, cot_all),
     )
     if place.count == 8:
-        sums = gradient_sums(pairs, half)
+        sums, bases = gradient_sums(pairs, half)
         side = r.reshape(1)
-        qkv_base = half * 2 * hidden // (BR * BC)
-        out_base = qkv_base + half * 3 * units // (BR * BC)
-        down_base = out_base + half * units // (BR * BC)
-        gate_up_grad = spread_gate_up(side, sums, 0, half, hidden)
-        qkv_grad = spread_qkv(side, sums, qkv_base, half, units)
-        out_grad = spread_rows(side, sums, out_base, half, units)
-        down_grad = spread_rows(side, sums, down_base, half, hidden)
+        gate_up_grad = spread_columns(side, sums, bases[0], half, hidden, 2, 256)
+        qkv_grad = spread_columns(side, sums, bases[1], half, units, 3, 256)
+        out_grad = spread_rows(side, sums, bases[2], half, units)
+        down_grad = spread_rows(side, sums, bases[3], half, hidden)
     else:
         sums = []
         for kind, left, right in pairs:

time: 1180 us -> 946 us (0.80)
  waiting for transfers between devices: 272 us -> 109 us
  Pallas kernels: 593 us -> 708 us
  local copies, waits for them, and re-layouts: 83.7 us -> 18.9 us
  matrix products: 107 us -> 50.5 us
  other arithmetic: 76.5 us -> 38.3 us
  starting transfers between devices: 36 us -> 14.9 us
    pallas_call x2, Pallas kernels: 497 us -> 639 us  [the longest x1 462 us: gradient_sums(): pl.pallas_call(functools.partial(gradient_kernel, segments, bases, half),...]
    ppermute x8 -> x0, waiting for transfers between devices: 87.8 us -> none  [fetch(): other = lax.ppermute(held, 'dp', dp_perm(bit, count))]
    ppermute x26 -> x14, waiting for transfers between devices: 181 us -> 104 us  [swap(): return lax.ppermute(v, axis, SWAP)]
    unnamed x149 -> x63, local copies, waits for them, and re-layouts: 33.4 us -> 4.82 us
    pallas_call x4, Pallas kernels: 70.1 us -> 41.8 us  [spread(): pl.pallas_call(body, grid_spec=pltpu.PrefetchScalarGridSpec(num_scalar_pr...]
    dot_general x3 -> x1, matrix products: 32.4 us -> 9.07 us  [dot(): return jnp.dot(a, b, preferred_element_type=F32)]
    dynamic_slice x16 -> x7, local copies, waits for them, and re-layouts: 28.2 us -> 5.77 us  [piece(): return lax.dynamic_slice_in_dim(v, index * size, size, axis)]
    select_n x17 -> x5, other arithmetic: 25.9 us -> 3.61 us  [ordered(): first = jnp.where(flag == 0, mine, other)]
  transfers between devices with their start and end apart: 37 -> 17, of which waited for: 22 -> 11; matrix products, arithmetic and copies ran while one was open for 12% -> 4% of each run, Pallas kernels for 46% -> 54%
where the time goes in v3:
time: 946 us; the launch traced here: 941 us
  Pallas kernels  708 us (75%)
  waiting for transfers between devices  109 us (12%)
  matrix products  50.5 us (5%)
  other arithmetic  38.3 us (4%)
  local copies, waits for them, and re-layouts  18.9 us (2%)
  starting transfers between devices  14.9 us (2%)
    pallas_call x1, Pallas kernels, gradient_sums(): pl.pallas_call(functools.partial(gradient_kernel, segments, bases, half),...  462 us
    pallas_call x1, Pallas kernels, front(): pl.pallas_call(front_kernel, out_shape=outs, in_specs=[any_spec] + [vmem_...  177 us
    ppermute x14, waiting for transfers between devices, swap(): return lax.ppermute(v, axis, SWAP)  104 us
    pallas_call x4, Pallas kernels, spread(): pl.pallas_call(body, grid_spec=pltpu.PrefetchScalarGridSpec(num_scalar_pr...  41.8 us
    pallas_call x1, Pallas kernels, attention_backward(): pl.pallas_call(backward_kernel, grid=(pairs,), in_specs=[same] * 5 + [pl....  26.6 us
  transfers between devices with their start and end apart: 17, of which 11 were waited for; matrix products, arithmetic and copies ran while one was open for 4% of the time, Pallas kernels for 54%

profile of v3, /device:TPU:0, one launch (start us, length us, event | category | flops | bytes accessed | tf_op | source)
XLA Modules:
  0.0 940.5 jit_solution(18169772444780672272)
XLA Ops:
  1.4 3.0 collective-permute-start
  14.6 176.8 %shard_map.203 = (bf16[1024,2048]{1,0:T(8,128)(2,1)}, bf16[1024,512]{1,0:T(8,128)(2,1)}, bf16[1024,512]{1,0:T(8,128)(2,1)}, bf16[1024,512]{1,0:T(8,128)(2,1)}, b...) custom-call(bf16[512,1024]{1,0:T(8,128)(2,1)} %tokens.1, ...), custom_call_target="tpu_custom_call" | custom-call | flops 20401094656 | bytes 104857600 | tf_op jit(solution)/shard_map/pallas_call | solution.py:1004
  191.4 10.9 %fusion.42 = f32[1024,1408]{1,0:T(8,128)S(1)} fusion(bf16[1024,2048]{1,0:T(8,128)(2,1)} %get-tuple-element.35.refs_7_, bf16[1408,2048]{1,0:T(8,128)(2,1)} %get-tuple-element.34), kind=kOutput, calls=%fused_computation.118 | convolution fusion | flops 5905580032 | bytes 15728640 | tf_op jit(solution)/shard_map/dot_general | solution.py:46
  202.4 3.0 fusion.6
  205.4 17.0 %bitcast_convert_fusion.1 = bf16[1024,2048]{1,0:T(8,128)(2,1)S(1)} fusion(bf16[2,2048,1408]{2,1,0:T(8,128)(2,1)} %get-tuple-element.38, bf16[1,1024,1408]{2,1,0:T(8,128)(2,1)S(1)} %bitcast.48, bf16[1,1024,1408]{2,1,0:T(8,128)(2,1)S(1)} %bitcast.47), kind=kOutput, calls=%fused_computation.4 | convolution fusion | flops 11816140800 | bytes 21495808 | tf_op jit(solution)/shard_map/ksf,kdf->sd/dot_general | solution.py:1100
  226.4 9.1 convolution_convert_fusion
  238.1 3.2 add_convert_fusion.1
  245.1 22.4 %collective-permute-done.5 = bf16[256,2048]{1,0:T(8,128)(2,1)S(1)} collective-permute-done((bf16[256,2048]{1,0:T(8,128)(2,1)S(1)}, bf16[256,2048]{1,0:T(8,128)(2,1)S(1)}, u32[]{:S(2)}, u32[]{:S(2)}) %collective-permute-start.5) | collective-permute-done | bytes 1048608 | tf_op jit(solution)/shard_map/ppermute | solution.py:23
  268.7 20.9 %collective-permute-done.2 = bf16[256,2048]{1,0:T(8,128)(2,1)S(1)} collective-permute-done((bf16[256,2048]{1,0:T(8,128)(2,1)S(1)}, bf16[256,2048]{1,0:T(8,128)(2,1)S(1)}, u32[]{:S(2)}, u32[]{:S(2)}) %collective-permute-start.2) | collective-permute-done | bytes 1048608 | tf_op jit(solution)/shard_map/ppermute | solution.py:23
  289.6 3.8 fusion.35
  294.4 23.9 %collective-permute-done.6 = bf16[256,2048]{1,0:T(8,128)(2,1)S(1)} collective-permute-done((bf16[256,2048]{1,0:T(8,128)(2,1)S(1)}, bf16[256,2048]{1,0:T(8,128)(2,1)S(1)}, u32[]{:S(2)}, u32[]{:S(2)}) %collective-permute-start.6) | collective-permute-done | bytes 1048608 | tf_op jit(solution)/shard_map/ppermute | solution.py:23
  320.3 4.5 collective-permute-done.7
  327.7 3.3 convolution_convert_fusion.1.g_ref
  331.0 26.6 %shard_map.204 = (bf16[1024,512]{1,0:T(8,128)(2,1)S(1)}, bf16[1024,512]{1,0:T(8,128)(2,1)S(1)}, bf16[1024,512]{1,0:T(8,128)(2,1)S(1)}) custom-call(bf16[1024,512]{1,0:T(8,128)(2,1)S(1)} %copy-done.3, bf16[1024,512]{1,0:T(8,128)(2,1)S(1)} %copy-done.4, bf16[1024,512]{1,0:T(8,128)(2,1)} %get-tuple-element.42.v_ref, ...), custom_call_target="tpu_custom_call" | custom-call | flops 3355443200 | bytes 8388608 | tf_op jit(solution)/shard_map/pallas_call | solution.py:193
  357.9 3.3 copy.29
  361.2 10.2 %bitcast_convert_fusion = bf16[1024,2048]{1,0:T(8,128)(2,1)S(1)} fusion(bf16[1024,3,512]{0,2,1:T(8,128)(2,1)} %bitcast.49, bf16[3,2048,512]{2,1,0:T(8,128)(2,1)} %get-tuple-element.49), kind=kOutput, calls=%fused_computation.3 | convolution fusion | flops 6444548096 | bytes 13631488 | tf_op jit(solution)/shard_map/sku,kdu->sd/dot_general | solution.py:1116
  382.0 9.8 %collective-permute-done.3 = bf16[256,1024]{1,0:T(8,128)(2,1)S(1)} collective-permute-done((bf16[256,1024]{1,0:T(8,128)(2,1)S(1)}, bf16[256,1024]{1,0:T(8,128)(2,1)S(1)}, u32[]{:S(2)}, u32[]{:S(2)}) %collective-permute-start.3) | collective-permute-done | bytes 524320 | tf_op jit(solution)/shard_map/ppermute | solution.py:23
  395.3 18.2 %collective-permute-done.9 = bf16[256,2048]{1,0:T(8,128)(2,1)S(1)} collective-permute-done((bf16[256,2048]{1,0:T(8,128)(2,1)S(1)}, bf16[256,2048]{1,0:T(8,128)(2,1)S(1)}, u32[]{:S(2)}, u32[]{:S(2)}) %collective-permute-start.9) | collective-permute-done | bytes 1048608 | tf_op jit(solution)/shard_map/ppermute | solution.py:23
  419.8 3.8 collective-permute-done.13
  430.1 462.4 %shard_map.205.block_ref = bf16[2,55,512,256]{3,2,1,0:T(8,128)(2,1)} custom-call(bf16[1024,2048]{1,0:T(8,128)(2,1)} %get-tuple-element.50.refs_0_, bf16[1024,2816]{1,0:T(8,128)(2,1)} %pad_maximum_fusion.refs_1_, bf16[1024,2048]{1,0:T(8,128)(2,1)} %get-tuple-element.51.refs_2_, bf16[1024,1536]{1,0:T(8,128)(2,1)} %copy-done.6, ...), custom_call_target="tpu_custom_call" | custom-call | flops 26306674688 | bytes 25690112 | tf_op jit(solution)/shard_map/pallas_call | solution.py:486
  892.5 6.0 shard_map.207
  898.5 8.5 shard_map.209
  907.0 8.9 shard_map.206
  915.9 18.4 %shard_map.208 = f32[1024,2,2816]{2,1,0:T(2,128)} custom-call(s32[1]{0:T(128)} %bitcast.22.side_ref, bf16[2,55,512,256]{3,2,1,0:T(8,128)(2,1)} %shard_map.205.block_ref), custom_call_target="tpu_custom_call" | custom-call | tf_op jit(solution)/shard_map/pallas_call | solution.py:529
  (160 shorter events, 61.2 us)
Async XLA Ops:
  0.6 12.7 %copy-start = (f32[3,1024]{1,0:T(4,128)S(1)}, f32[3,1024]{1,0:T(4,128)}, u32[]{:S(2)}) copy-start(f32[3,1024]{1,0:T(4,128)} %param.17) | copy-start | bytes 36868
  1.4 12.5 %collective-permute-start = (f32[4,1024]{1,0:T(4,128)S(1)}, f32[4,1024]{1,0:T(4,128)S(1)}, u32[]{:S(2)}, u32[]{:S(2)}) collective-permute-start(f32[4,1024]{1,0:T(4,128)S(1)} %pad_maximum_fusion.12), channel_id=1, source_target_pairs={{0,2},{2,0},{1,3},{3,1},{4,6},{6,4},{5,7},{7,5},{8,10},{10,8},{9,1... | collective-permute-start | bytes 49160 | tf_op jit(solution)/shard_map/ppermute | solution.py:23
  205.4 17.1 %copy-start.7 = (bf16[1024,1408]{1,0:T(8,128)(2,1)}, bf16[1024,1408]{1,0:T(8,128)(2,1)S(1)}, u32[]{:S(2)}) copy-start(bf16[1024,1408]{1,0:T(8,128)(2,1)S(1)} %get-tuple-element.69) | copy-start | bytes 8650756
  205.4 17.1 %copy-start.9 = (bf16[1024,1408]{1,0:T(8,128)(2,1)}, bf16[1024,1408]{1,0:T(8,128)(2,1)S(1)}, u32[]{:S(2)}) copy-start(bf16[1024,1408]{1,0:T(8,128)(2,1)S(1)} %get-tuple-element.70) | copy-start | bytes 8650756
  225.5 12.6 %collective-permute-start.4 = (bf16[512,2048]{1,0:T(8,128)(2,1)}, bf16[512,2048]{1,0:T(8,128)(2,1)}, u32[]{:S(2)}, u32[]{:S(2)}) collective-permute-start(bf16[512,2048]{1,0:T(8,128)(2,1)} %constant_dynamic-slice_fusion.3), channel_id=1, source_target_pairs={{0,1},{1,0},{2,3},{3,2},{4,5},{5,4},{6,7},{7,6},{8,9},{9,8},{10,11... | collective-permute-start | bytes 6291464 | tf_op jit(solution)/shard_map/ppermute | solution.py:23
  238.1 5.1 collective-permute-start.1
  241.4 26.0 %collective-permute-start.5 = (bf16[256,2048]{1,0:T(8,128)(2,1)S(1)}, bf16[256,2048]{1,0:T(8,128)(2,1)S(1)}, u32[]{:S(2)}, u32[]{:S(2)}) collective-permute-start(bf16[256,2048]{1,0:T(8,128)(2,1)S(1)} %constant_dynamic-slice_fusion.2), channel_id=1, source_target_pairs={{0,2},{2,0},{1,3},{3,1},{4,6},{6,4},{5,7},{7,5},{8,10},{10,8},{9,1... | collective-permute-start | bytes 3145736 | tf_op jit(solution)/shard_map/ppermute | solution.py:23
  244.1 45.4 %collective-permute-start.2 = (bf16[256,2048]{1,0:T(8,128)(2,1)S(1)}, bf16[256,2048]{1,0:T(8,128)(2,1)S(1)}, u32[]{:S(2)}, u32[]{:S(2)}) collective-permute-start(bf16[256,2048]{1,0:T(8,128)(2,1)S(1)} %constant_dynamic-slice_fusion.4), channel_id=1, source_target_pairs={{0,2},{2,0},{1,3},{3,1},{4,6},{6,4},{5,7},{7,5},{8,10},{10,8},{9,1... | collective-permute-start | bytes 3145736 | tf_op jit(solution)/shard_map/ppermute | solution.py:23
  293.4 24.8 %collective-permute-start.6 = (bf16[256,2048]{1,0:T(8,128)(2,1)S(1)}, bf16[256,2048]{1,0:T(8,128)(2,1)S(1)}, u32[]{:S(2)}, u32[]{:S(2)}) collective-permute-start(bf16[256,2048]{1,0:T(8,128)(2,1)S(1)} %get-tuple-element.65), channel_id=1, source_target_pairs={{0,2},{2,0},{1,3},{3,1},{4,6},{6,4},{5,7},{7,5},{8,10},{10,8},{9,1... | collective-permute-start | bytes 3145736 | tf_op jit(solution)/shard_map/ppermute | solution.py:23
  320.3 4.5 collective-permute-start.7
  357.9 57.8 %copy-start.6 = (bf16[1024,1536]{1,0:T(8,128)(2,1)}, bf16[1024,1536]{1,0:T(8,128)(2,1)S(1)}, u32[]{:S(2)}) copy-start(bf16[1024,1536]{1,0:T(8,128)(2,1)S(1)} %constant_dynamic-update-slice_fusion.refs_3_) | copy-start | bytes 9437188
  361.2 11.9 %copy-start.10 = (bf16[1024,1408]{1,0:T(8,128)(2,1)S(1)}, bf16[1024,1408]{1,0:T(8,128)(2,1)}, u32[]{:S(2)}) copy-start(bf16[1024,1408]{1,0:T(8,128)(2,1)} %copy-done.9) | copy-start | bytes 8650756
  373.0 4.9 collective-permute-start.8
  376.9 14.8 %collective-permute-start.3 = (bf16[256,1024]{1,0:T(8,128)(2,1)S(1)}, bf16[256,1024]{1,0:T(8,128)(2,1)S(1)}, u32[]{:S(2)}, u32[]{:S(2)}) collective-permute-start(bf16[256,1024]{1,0:T(8,128)(2,1)S(1)} %slice.137), channel_id=1, source_target_pairs={{0,2},{2,0},{1,3},{3,1},{4,6},{6,4},{5,7},{7,5},{8,10},{10,8},{9,1... | collective-permute-start | bytes 1572872 | tf_op jit(solution)/shard_map/ppermute | solution.py:23
  380.4 33.0 %collective-permute-start.9 = (bf16[256,2048]{1,0:T(8,128)(2,1)S(1)}, bf16[256,2048]{1,0:T(8,128)(2,1)S(1)}, u32[]{:S(2)}, u32[]{:S(2)}) collective-permute-start(bf16[256,2048]{1,0:T(8,128)(2,1)S(1)} %constant_dynamic-slice_fusion), channel_id=1, source_target_pairs={{0,2},{2,0},{1,3},{3,1},{4,6},{6,4},{5,7},{7,5},{8,10},{10,8},{9,1... | collective-permute-start | bytes 3145736 | tf_op jit(solution)/shard_map/ppermute | solution.py:23
  382.0 11.0 %copy-start.14 = (bf16[512,2048]{1,0:T(8,128)(2,1)S(1)}, bf16[512,2048]{1,0:T(8,128)(2,1)}, u32[]{:S(2)}) copy-start(bf16[512,2048]{1,0:T(8,128)(2,1)} %copy-done.13) | copy-start | bytes 6291460
  382.0 11.0 %copy-start.16 = (bf16[512,2048]{1,0:T(8,128)(2,1)S(1)}, bf16[512,2048]{1,0:T(8,128)(2,1)}, u32[]{:S(2)}) copy-start(bf16[512,2048]{1,0:T(8,128)(2,1)} %copy-done.15) | copy-start | bytes 6291460
  414.7 3.8 collective-permute-start.11
  418.5 1.2 collective-permute-start.12
  419.8 3.9 collective-permute-start.13
  423.7 3.8 collective-permute-start.14
  426.2 512.5 %collective-permute-start.10 = (f32[256,1024]{1,0:T(8,128)}, f32[256,1024]{1,0:T(8,128)S(1)}, u32[]{:S(2)}, u32[]{:S(2)}) collective-permute-start(f32[256,1024]{1,0:T(8,128)} %slice.147), channel_id=1, source_target_pairs={{0,2},{2,0},{1,3},{3,1},{4,6},{6,4},{5,7},{7,5},{8,10},{10,8},{9,1... | collective-permute-start | bytes 3145736 | tf_op jit(solution)/shard_map/ppermute | solution.py:23
  427.5 506.8 %collective-permute-start.15 = (f32[5632]{0:T(1024)S(1)}, f32[5632]{0:T(1024)S(1)}, u32[]{:S(2)}, u32[]{:S(2)}) collective-permute-start(f32[5632]{0:T(1024)S(1)} %add.117), channel_id=1, source_target_pairs={{0,16},{4,20},{8,24},{12,28},{16,0},{20,4},{24,8},{28,12},{1,17},{... | collective-permute-start | bytes 67592 | tf_op jit(solution)/shard_map/ppermute | solution.py:1132
  934.3 3.7 collective-permute-start.16
  (23 other events, 91.5 us)

commit v4 on v3

--- a/solution.py
+++ b/solution.py
@@ -150,7 +150,7 @@
     return lax.dot_general(a, b, (((0,), (0,)), ((), ())), preferred_element_type=F32)
 
 
-def backward_kernel(q_ref, k_ref, v_ref, g_ref, raw_ref, log_ref, starts_ref, table_ref, dq_ref, dk_ref, dv_ref, dk_acc, dv_acc):
+def backward_kernel(q_ref, k_ref, v_ref, g_ref, att_ref, log_ref, starts_ref, table_ref, dq_ref, dk_ref, dv_ref, dk_acc, dv_acc):
     length = q_ref.shape[0]
     dk_acc[...] = jnp.zeros_like(dk_acc)
     dv_acc[...] = jnp.zeros_like(dv_acc)
@@ -162,7 +162,7 @@
             q, k, v, g = q_ref[begin:end, lanes], k_ref[low:end, lanes], v_ref[low:end, lanes], g_ref[begin:end, lanes]
             weights = jnp.exp(nt(q, k) + bar - log_ref[0, begin:end, h : h + 1])
             dvs.append(tn(weights.astype(BF), g))
-            inner = jnp.sum(g.astype(F32) * raw_ref[begin:end, lanes], axis=1, keepdims=True)
+            inner = jnp.sum(g.astype(F32) * att_ref[begin:end, lanes].astype(F32), axis=1, keepdims=True)
             grads = (weights * (nt(g, v) - inner)).astype(BF)
             outs.append(jnp.dot(grads, k, preferred_element_type=F32))
             dks.append(tn(grads, q))
@@ -185,7 +185,7 @@
     return jnp.stack([jnp.concatenate([v, v], axis=1) for v in (one, ahead, behind)])
 
 
-def attention_backward(queries, keys, values, grads, raw, logs, starts, table):
+def attention_backward(queries, keys, values, grads, attended, logs, starts, table):
     length, units = queries.shape
     pairs = units // 128
     same = pl.BlockSpec((length, 128), lambda p: (0, p))
@@ -204,94 +204,228 @@
         scratch_shapes=[pltpu.VMEM((length, 128), F32)] * 2,
         compiler_params=pltpu.CompilerParams(vmem_limit_bytes=48 * 2**20),
         cost_estimate=pl.CostEstimate(flops=pairs * 2 * length * 640 * 640, bytes_accessed=8 * 2**20, transcendentals=pairs * 2 * length * 640),
-    )(queries, keys, values, grads, raw, logs, starts, table)
+    )(queries, keys, values, grads, attended, logs, starts, table)
 
 
 BR = 512
 BC = 256
-SLOTS = 6
-
-
-def gradient_kernel(segments, bases, half, *refs):
-    count = len(segments)
-    total = sum(s[1] for s in segments)
-    sources = refs[: 2 * count]
-    out_ref = refs[2 * count]
+SLOTS = 5
+SEMAPHORES = 8
+
+
+def back_kernel(
+    bases,
+    inner,
+    cotangent,
+    gate,
+    up,
+    act_two,
+    attended,
+    queries,
+    keys,
+    values,
+    logs,
+    starts_ref,
+    table_ref,
+    act_one,
+    hidden_state,
+    own_inputs,
+    params_ref,
+    w_down,
+    w_gate,
+    w_out,
+    w_qkv,
+    out_ref,
+    res_own,
+    res_got,
+    grad_own,
+    grad_got,
+    norm_sums,
+    bias_sums,
+    turn,
+    turn_in,
+    joint,
+    branch,
+    pair,
+    att,
+    att_grad,
+    heads,
+    head_logs,
+    key_sums,
+    value_sums,
+    down_rows,
+    gate_in,
+    down_columns,
+    wide_w,
+    w_o,
+    sent,
+    kept,
+    core_in,
+    row_src,
+    row_in,
+    acc_rows,
+    grad_rows,
+    hid,
+    own,
+    result,
+    part,
+    x_src,
+    x_dst,
+    y_dst,
+    acc,
+    e_dst,
+    low,
+    m_dst,
+    full,
+    f_dst,
+    deep,
+    n_dst,
+    key,
+    k_dst,
+    whole,
+    load_sem,
+    once_sem,
+    piece_sem,
+    gather_sem,
+    *sems,
+):
     out_own, out_got = out_ref.at[0], out_ref.at[1]
-    rest = refs[2 * count + 1 :]
-    held = rest[: 2 * count]
-    (
-        load_sem,
-        turn,
-        part,
-        x_src,
-        x_dst,
-        y_dst,
-        acc,
-        e_dst,
-        low,
-        m_dst,
-        full,
-        f_dst,
-        deep,
-        n_dst,
-        key,
-        k_dst,
-        whole,
-    ) = rest[2 * count : 2 * count + 17]
-    sems = rest[2 * count + 17 :]
     names = ("x", "y", "ei", "eo", "m", "g", "fi", "fo", "n", "k", "w")
     send = {k: sems[i] for i, k in enumerate(names)}
     recv = {k: sems[len(names) + i] for i, k in enumerate(names)}
     store_own, store_got = sems[2 * len(names)], sems[2 * len(names) + 1]
 
-    d, r = lax.axis_index("dp"), lax.axis_index("row")
+    length, width = branch.shape
+    half, part_rows, block = width // 2, length // 2, length // 4
+    hidden, units = pair.shape[1] // 2, att.shape[1]
+    pairs = units // 128
+    size = BR * BC // half
+    segments = (hidden // size, half * 2 * hidden // (BR * BC), units // size, half * 3 * units // (BR * BC))
+    total = sum(segments)
+    firsts = [sum(segments[:i]) for i in range(4)]
+
+    d, r, c = lax.axis_index("dp"), lax.axis_index("row"), lax.axis_index("col")
     y, z = lax.rem(d, 2), d // 2
     upper = d // 4
     mid = (z == 1) | (z == 2)
     outer = (z == 0) | (z == 3)
-    x_peer = {"row": 1 - r}
+    x_peer, c_peer = {"row": 1 - r}, {"col": 1 - c}
     y_peer = {"dp": d + 1 - 2 * y}
     e_peer = {"dp": d + 2 - 4 * lax.rem(z, 2)}
     m_peer = {"dp": d + 2 - 4 * upper}
 
-    loads = []
-    for i in range(2 * count):
-        loads.append(pltpu.make_async_copy(sources[i], held[i], load_sem.at[i]))
-        loads[-1].start()
+    def span(start, count):
+        return pl.ds(pl.multiple_of(start, count), count)
+
+    def local_copy(n, src, dst):
+        return pltpu.make_async_copy(src, dst, load_sem.at[n])
 
     barrier = pltpu.get_barrier_semaphore()
-    for peer in (x_peer, y_peer, e_peer):
+    for peer in (x_peer, y_peer, e_peer, c_peer):
         pl.semaphore_signal(barrier, inc=1, device_id=peer, device_id_type=MESH)
 
     @pl.when(mid)
     def _():
         pl.semaphore_signal(barrier, inc=1, device_id=m_peer, device_id_type=MESH)
-        pl.semaphore_wait(barrier, 4)
+
+    own_block = span(c * part_rows + r * block, block)
+    x_block = span(c * part_rows + (1 - r) * block, block)
+    lo, hi = pl.ds(0, half), pl.ds(half, half)
+    load_inner = local_copy(0, inner, joint.at[:, pl.ds(0, hidden)])
+    load_cot = local_copy(1, cotangent, branch)
+    load_hid = local_copy(2, hidden_state, hid)
+    load_own = local_copy(3, cotangent.at[own_block], own)
+    load_att = local_copy(4, attended, att)
+    load_wo = local_copy(5, w_out, w_o)
+    load_inputs = local_copy(6, own_inputs, own)
+
+    def down_rows_load(i):
+        s = lax.rem(i, 2)
+        at = span(i * 128, 128)
+        return (
+            pltpu.make_async_copy(w_down.at[at], down_rows.at[s], once_sem.at[s]),
+            pltpu.make_async_copy(gate.at[:, at], gate_in.at[s, 0], once_sem.at[2 + s]),
+            pltpu.make_async_copy(up.at[:, at], gate_in.at[s, 1], once_sem.at[4 + s]),
+        )
+
+    def order(i):
+        return lax.rem(i, 2) * (half // BC) + i // 2
+
+    def down_columns_load(i):
+        s = lax.rem(i, 2)
+        return (pltpu.make_async_copy(w_down.at[:, span(order(i) * BC, BC)], down_columns.at[s], once_sem.at[6 + s]),)
+
+    def gate_load(i):
+        s = lax.rem(i, 2)
+        return (pltpu.make_async_copy(w_gate.at[:, span(order(i) * BC, BC)], wide_w.at[s], once_sem.at[8 + s]),)
+
+    def qkv_load(i):
+        s = lax.rem(i, 2)
+        rows = span(order(i) * BC, BC)
+        return tuple(
+            pltpu.make_async_copy(
+                w_qkv.at[k, rows], wide_w.at[s, k // 2, :, pl.ds(k % 2 * units, units)], once_sem.at[10 + 2 * k + s]
+            )
+            for k in range(3)
+        )
+
+    def heads_load(p):
+        s = lax.rem(p, 2)
+        lanes = span(p * 128, 128)
+        return tuple(
+            pltpu.make_async_copy(ref.at[:, lanes], heads.at[s, k], once_sem.at[16 + 2 * k + s])
+            for k, ref in enumerate((queries, keys, values))
+        ) + (pltpu.make_async_copy(logs.at[p], head_logs.at[s], once_sem.at[22 + s]),)
+
+    def turn_load(source, i):
+        return tuple(
+            local_copy(7 + side, source.at[:, span(side * half + i * BR, BR)], turn_in.at[side]) for side in range(2)
+        )
+
+    def start(copies):
+        for copy in copies:
+            copy.start()
+
+    def wait(copies):
+        for copy in copies:
+            copy.wait()
+
+    start((load_inner, load_cot, load_hid, load_own, load_att, load_wo))
+    start(down_rows_load(0))
+    start(down_columns_load(0))
+    start(turn_load(act_two, 0))
+
+    @pl.when(mid)
+    def _():
+        pl.semaphore_wait(barrier, 5)
 
     @pl.when(outer)
     def _():
-        pl.semaphore_wait(barrier, 3)
+        pl.semaphore_wait(barrier, 4)
 
     rows = BR // 2
 
     def halves(index):
-        return pl.ds(pl.multiple_of(index * rows, rows), rows)
-
-    def copy(name, u, src, dst, peer):
-        s = lax.rem(u, SLOTS)
-        return pltpu.make_async_remote_copy(
-            src_ref=src, dst_ref=dst, send_sem=send[name].at[s], recv_sem=recv[name].at[s], device_id=peer, device_id_type=MESH
-        )
+        return span(index * rows, rows)
 
     def slot(u):
         return lax.rem(u, SLOTS)
 
+    def copy(name, u, src, dst, peer):
+        s = lax.rem(u, SEMAPHORES)
+        return pltpu.make_async_remote_copy(
+            src_ref=src,
+            dst_ref=dst,
+            send_sem=send[name].at[s],
+            recv_sem=recv[name].at[s],
+            device_id=peer,
+            device_id_type=MESH,
+        )
+
     def spot(u):
-        place, first = u, 0
-        for (_, blocks), base in zip(segments, bases):
+        place = u
+        for first, base in zip(firsts, bases):
             place = jnp.where(u >= first, u + (base - first), place)
-            first += blocks
         return place
 
     def out_half(ref, u, index):
@@ -349,43 +483,47 @@
         def _():
             fn(u)
 
+    def within(t, first, count, fn):
+        @pl.when((t >= first) & (t < first + count))
+        def _():
+            fn(t - first)
+
+    def unit_block(k, s, lhs, rhs):
+        left = lhs[:, span(k * size, size)].T
+        for side, ref in ((1, x_src), (0, part)):
+            for q in range(half // BC):
+                right = rhs[:, side * half + q * BC : side * half + (q + 1) * BC]
+                ref[s, q * size : (q + 1) * size] = jnp.dot(left, right, preferred_element_type=F32).astype(BF)
+
+    def feature_block(k, s, rhs, source, following):
+        columns = rhs.shape[1] // BC
+
+        for i in range(half // BR):
+
+            @pl.when(k == i * columns)
+            def _(i=i):
+                wait(turn_load(source, i))
+                for side in range(2):
+                    turn[side] = turn_in[side].T
+                following_load = following if i + 1 == half // BR else (source, i + 1)
+                if following_load is not None:
+                    start(turn_load(*following_load))
+
+        right = rhs[:, span(lax.rem(k, columns) * BC, BC)]
+        for side, ref in ((1, x_src), (0, part)):
+            ref[s] = jnp.dot(turn[side], right, preferred_element_type=F32).astype(BF)
+
     def produce(u):
         s = slot(u)
-        first = 0
-        for i, (kind, blocks) in enumerate(segments):
-            lhs, rhs = held[2 * i], held[2 * i + 1]
-
-            @pl.when(u == first)
-            def _(i=i):
-                loads[2 * i].wait()
-                loads[2 * i + 1].wait()
-
-            @pl.when((u >= first) & (u < first + blocks))
-            def _(kind=kind, first=first, lhs=lhs, rhs=rhs):
-                k = u - first
-                if kind == "D":
-                    columns = rhs.shape[1] // BC
-
-                    @pl.when(lax.rem(k, columns) == 0)
-                    def _():
-                        for side in range(2):
-                            at = pl.multiple_of(side * half + k // columns * BR, BR)
-                            turn[side] = lhs[:, pl.ds(at, BR)].T
-
-                    right = rhs[:, pl.ds(pl.multiple_of(lax.rem(k, columns) * BC, BC), BC)]
-                    for side, ref in ((1, x_src), (0, part)):
-                        ref[s] = jnp.dot(turn[side], right, preferred_element_type=F32).astype(BF)
-                else:
-                    size = BR * BC // half
-                    left = lhs[:, pl.ds(pl.multiple_of(k * size, size), size)].T
-                    for side, ref in ((1, x_src), (0, part)):
-                        for q in range(half // BC):
-                            right = rhs[:, side * half + q * BC : side * half + (q + 1) * BC]
-                            ref[s, q * size : (q + 1) * size] = jnp.dot(
-                                left, right, preferred_element_type=F32
-                            ).astype(BF)
-
-            first += blocks
+
+        @pl.when(u == 0)
+        def _():
+            wait((load_inner, load_cot))
+
+        within(u, firsts[0], segments[0], lambda k: unit_block(k, s, joint, branch))
+        within(u, firsts[1], segments[1], lambda k: feature_block(k, s, pair, act_two, (act_one, 0)))
+        within(u, firsts[2], segments[2], lambda k: unit_block(k, s, att, branch))
+        within(u, firsts[3], segments[3], lambda k: feature_block(k, s, joint, act_one, None))
         x_copy(u).start()
         y_copy(u).start()
 
@@ -441,16 +579,329 @@
         f_out(u).start()
         keep_got(u).start()
 
+    pieces = width // BC
+    own_part, far_part = c * part_rows, (1 - c) * part_rows
+
+    def core_copy(n):
+        s = lax.rem(n, 3)
+        return pltpu.make_async_remote_copy(
+            src_ref=sent.at[s],
+            dst_ref=core_in.at[s],
+            send_sem=piece_sem.at[s],
+            recv_sem=piece_sem.at[3 + s],
+            device_id=c_peer,
+            device_id_type=MESH,
+        )
+
+    def row_copy(n):
+        s = lax.rem(n, 4)
+        return pltpu.make_async_remote_copy(
+            src_ref=row_src.at[s],
+            dst_ref=row_in.at[s],
+            send_sem=piece_sem.at[6 + s],
+            recv_sem=piece_sem.at[10 + s],
+            device_id=x_peer,
+            device_id_type=MESH,
+        )
+
+    def sum_piece(n, product):
+        s = lax.rem(n, 3)
+        sent[s] = product(span(far_part, part_rows)).astype(BF)
+        core_copy(n).start()
+        kept[s] = product(span(own_part, part_rows)).astype(BF)
+
+    def sum_core(n, i):
+        s, q = lax.rem(n, 3), lax.rem(n, 4)
+        core_copy(n).wait_recv()
+        core_copy(n).wait_send()
+        far, near = span((1 - r) * block, block), span(r * block, block)
+        row_src[q] = kept[s, far] + core_in[s, far]
+        row_copy(n).start()
+        acc_rows[:, span(order(i) * BC, BC)] = kept[s, near].astype(F32) + core_in[s, near].astype(F32)
+
+    def sum_row(n, i):
+        q = lax.rem(n, 4)
+        row_copy(n).wait_recv()
+        row_copy(n).wait_send()
+        partner = lax.rem(order(i) + half // BC, pieces)
+        cols = span(partner * BC, BC)
+        acc_rows[:, cols] = acc_rows[:, cols] + row_in[q].astype(F32)
+
+    def summed(t, first, base, product, load, wait_for=None):
+        within(t, first + 3, pieces, lambda i: sum_row(base + i, i))
+        within(t, first + 1, pieces, lambda i: sum_core(base + i, i))
+
+        def task(i):
+            if wait_for is not None:
+                pl.when(i == 0)(lambda: wait(wait_for))
+            pl.when(i + 1 < pieces)(lambda: start(load(i + 1)))
+            wait(load(i))
+            sum_piece(base + i, lambda at: product(lax.rem(i, 2), at))
+
+        within(t, first, pieces, task)
+
+    def feed_product(s, at):
+        return jnp.dot(joint[at, :hidden], down_columns[s], preferred_element_type=F32)
+
+    def act_two_product(s, at):
+        return nt(pair[at, :hidden], wide_w[s, 0]) + nt(pair[at, hidden:], wide_w[s, 1])
+
+    def act_one_product(s, at):
+        out = nt(joint[at, :units], wide_w[s, 0, :, :units])
+        out = out + nt(joint[at, units : 2 * units], wide_w[s, 0, :, units : 2 * units])
+        return out + nt(joint[at, 2 * units :], wide_w[s, 1, :, :units])
+
+    def gate_task(i):
+        s = lax.rem(i, 2)
+
+        @pl.when(i + 1 < hidden // 128)
+        def _():
+            start(down_rows_load(i + 1))
+
+        wait(down_rows_load(i))
+
+        def some(j, carry):
+            at = span(j * 256, 256)
+            grad = nt(branch[at], down_rows[s])
+            g, u = gate_in[s, 0, at].astype(F32), gate_in[s, 1, at].astype(F32)
+            rate = 1.0 / (1.0 + jnp.exp(-g))
+            pair[at, span(i * 128, 128)] = (grad * u * (rate * (1.0 + g * (1.0 - rate)))).astype(BF)
+            pair[at, span(hidden + i * 128, 128)] = (grad * (g * rate)).astype(BF)
+            return carry
+
+        lax.fori_loop(0, length // 256, some, 0)
+
+    def result_copy():
+        return pltpu.make_async_remote_copy(
+            src_ref=result.at[:, hi],
+            dst_ref=res_got,
+            send_sem=gather_sem.at[0],
+            recv_sem=gather_sem.at[1],
+            device_id=x_peer,
+            device_id_type=MESH,
+        )
+
+    store_result = local_copy(9, result.at[:, lo], res_own)
+
+    def result_task(i):
+        load_hid.wait()
+        load_own.wait()
+        result[...] = (hid[...] + acc_rows[...]).astype(BF)
+        result_copy().start()
+        store_result.start()
+
+    chunk = 64
+    chunks = block // chunk
+
+    def norm_rows(values, at, grads, gain):
+        mean = jnp.sum(values, axis=1, keepdims=True) / width
+        spread_of = jnp.sum(values * values, axis=1, keepdims=True) / width - mean * mean
+        inverse = lax.rsqrt(spread_of + EPSILON)
+        normal = (values - mean) * inverse
+        scaled = grads * gain
+        terms = grads * normal
+        first = jnp.sum(scaled, axis=1, keepdims=True) / width
+        second = jnp.sum(terms * gain, axis=1, keepdims=True) / width
+        return inverse * (scaled - first - normal * second), terms
+
+    def gather_copies(i):
+        at = span(c * part_rows + r * block + i * chunk, chunk)
+
+        def one(n, src, dst, peer):
+            return pltpu.make_async_remote_copy(
+                src_ref=src,
+                dst_ref=dst,
+                send_sem=gather_sem.at[2 + 2 * (n * chunks + i)],
+                recv_sem=gather_sem.at[3 + 2 * (n * chunks + i)],
+                device_id=peer,
+                device_id_type=MESH,
+            )
+
+        got = span(c * part_rows + (1 - r) * block + i * chunk, chunk)
+        return (
+            one(0, branch.at[at, lo], branch.at[at, hi], x_peer),
+            one(1, branch.at[at, hi], branch.at[at, lo], x_peer),
+            one(2, branch.at[at], branch.at[at], c_peer),
+            one(3, branch.at[got], branch.at[got], c_peer),
+        )
+
+    def norm_two_task(i):
+        at = span(i * chunk, chunk)
+        grads = acc_rows[at]
+        grad, terms = norm_rows(hid[at], at, grads, params_ref[2:3])
+        norm_sums[2:3] = norm_sums[2:3] + jnp.sum(terms, axis=0, keepdims=True)
+        norm_sums[3:4] = norm_sums[3:4] + jnp.sum(grads, axis=0, keepdims=True)
+        grad = own[at].astype(F32) + grad
+        grad_rows[at] = grad
+        branch[span(c * part_rows + r * block + i * chunk, chunk)] = grad.astype(BF)
+        start(gather_copies(i)[:3])
+
+    def forward_task(i):
+        copies = gather_copies(i)
+        copies[0].wait_recv()
+        copies[1].wait_recv()
+        copies[3].start()
+
+    def gathered_task(i):
+        copies = gather_copies(i)
+        copies[2].wait_recv()
+        copies[3].wait_recv()
+        for one in copies:
+            one.wait_send()
+
+    def att_grad_task(i):
+        at = span(i * part_rows, part_rows)
+        att_grad[at] = nt(branch[at], w_o[...]).astype(BF)
+
+    def attention_task(i):
+        p, second = i // 2, lax.rem(i, 2)
+        s = lax.rem(p, 2)
+        lanes0 = span(p * 128, 128)
+
+        @pl.when(second == 0)
+        def _():
+            pl.when(p + 1 < pairs)(lambda: start(heads_load(p + 1)))
+            wait(heads_load(p))
+            key_sums[...] = jnp.zeros_like(key_sums)
+            value_sums[...] = jnp.zeros_like(value_sums)
+
+        def window(begin, low, end):
+            bar = barred(starts_ref[begin:end], begin, low, end)
+            q2, k2, v2 = heads[s, 0, begin:end], heads[s, 1, low:end], heads[s, 2, low:end]
+            g2, a2 = att_grad[begin:end, lanes0], att[begin:end, lanes0]
+            outs, dks, dvs = [], [], []
+            for h in range(2):
+                lanes = slice(h * HEAD, (h + 1) * HEAD)
+                q, k, v, g = q2[:, lanes], k2[:, lanes], v2[:, lanes], g2[:, lanes]
+                weights = jnp.exp(nt(q, k) + bar - head_logs[s, begin:end, h : h + 1])
+                dvs.append(tn(weights.astype(BF), g))
+                inside = jnp.sum(g.astype(F32) * a2[:, lanes].astype(F32), axis=1, keepdims=True)
+                grads = (weights * (nt(g, v) - inside)).astype(BF)
+                outs.append(jnp.dot(grads, k, preferred_element_type=F32))
+                dks.append(tn(grads, q))
+            table = (table_ref[0, begin:end], -table_ref[1, begin:end], -table_ref[2, begin:end])
+            dq = turned(jnp.concatenate(outs, axis=1) * HEAD ** (-0.5), table).astype(BF)
+            joint[begin:end, lanes0] = dq
+            bias_sums[0:1, lanes0] = bias_sums[0:1, lanes0] + jnp.sum(dq.astype(F32), axis=0, keepdims=True)
+            key_sums[low:end] += jnp.concatenate(dks, axis=1)
+            value_sums[low:end] += jnp.concatenate(dvs, axis=1)
+
+        spans = list(windows(length))
+        middle = len(spans) // 2
+
+        @pl.when(second == 0)
+        def _():
+            for one in spans[:middle]:
+                window(*one)
+
+        @pl.when(second == 1)
+        def _():
+            for one in spans[middle:]:
+                window(*one)
+            table = (table_ref[0], -table_ref[1], -table_ref[2])
+            dk = turned(key_sums[...], table).astype(BF)
+            dv = value_sums[...].astype(BF)
+            for k, v in ((1, dk), (2, dv)):
+                joint[:, span(k * units + p * 128, 128)] = v
+                bias_sums[k : k + 1, lanes0] = jnp.sum(v.astype(F32), axis=0, keepdims=True)
+
+    def grad_copies(i):
+        at = span(i * chunk, chunk)
+        n = 2 + 8 * chunks + 2 * i
+        return (
+            pltpu.make_async_remote_copy(
+                src_ref=grad_rows.at[at, hi],
+                dst_ref=grad_got.at[at],
+                send_sem=gather_sem.at[n],
+                recv_sem=gather_sem.at[n + 1],
+                device_id=x_peer,
+                device_id_type=MESH,
+            ),
+            local_copy(10 + i, grad_rows.at[at, lo], grad_own.at[at]),
+        )
+
+    def norm_one_task(i):
+        pl.when(i == 0)(lambda: load_inputs.wait())
+        at = span(i * chunk, chunk)
+        grads = acc_rows[at]
+        grad, terms = norm_rows(own[at].astype(F32), at, grads, params_ref[0:1])
+        norm_sums[0:1] = norm_sums[0:1] + jnp.sum(terms, axis=0, keepdims=True)
+        norm_sums[1:2] = norm_sums[1:2] + jnp.sum(grads, axis=0, keepdims=True)
+        grad_rows[at] = grad_rows[at] + grad
+        start(grad_copies(i))
+
+    norm_sums[...] = jnp.zeros_like(norm_sums)
+    bias_sums[...] = jnp.zeros_like(bias_sums)
+    gates = hidden // 128
+    at_two = max(gates, pieces + 3)
+    at_norm = at_two + pieces + 3
+    at_att = at_norm + chunks // 2 + 3
+    at_heads = at_att + 2
+    at_one = at_heads + 2 * pairs
+    at_last = at_one + pieces + 3
+
+    def tasks(t):
+        within(t, 0, gates, gate_task)
+        summed(t, 0, 0, feed_product, down_columns_load)
+        within(t, at_two, 1, result_task)
+        pl.when(t == at_two - 1)(lambda: start(gate_load(0)))
+        summed(t, at_two, pieces, act_two_product, gate_load)
+
+        def two(task):
+            def both(i):
+                task(2 * i)
+                task(2 * i + 1)
+
+            return both
+
+        within(t, at_norm + 3, chunks // 2, two(gathered_task))
+        within(t, at_norm + 2, chunks // 2, two(forward_task))
+        within(t, at_norm, chunks // 2, two(norm_two_task))
+
+        @pl.when(t == at_att)
+        def _():
+            load_wo.wait()
+            load_att.wait()
+            load_inputs.start()
+            start(heads_load(0))
+
+        within(t, at_att, 2, att_grad_task)
+        within(t, at_heads, 2 * pairs, attention_task)
+        pl.when(t == at_one - 1)(lambda: start(qkv_load(0)))
+        summed(t, at_one, 2 * pieces, act_one_product, qkv_load)
+        within(t, at_last, chunks // 2, two(norm_one_task))
+
     def body(t, carry):
-        stage(t - 2, lambda u: (x_copy(u).wait_send(), y_copy(u).wait_send()))
+        def free_all(u):
+            x_copy(u).wait_send()
+            y_copy(u).wait_send()
+
+        def free_mid(u):
+            m_copy(u).wait_send()
+            n_copy(u).wait_send()
+
+        def free_out(u):
+            e_out(u).wait_send()
+            g_mid(u).wait_send()
+            keep_own(u, full.at[slot(u)]).wait()
+
+        def free_far(u):
+            g_out(u).wait_send()
+            keep_own(u, e_dst.at[slot(u)]).wait()
+
+        def free_got(u):
+            f_out(u).wait_send()
+            keep_got(u).wait()
+
+        stage(t - 2, free_all)
         stage(t - 3, lambda u: e_in(u).wait_send(), outer)
         stage(t - 3, lambda u: f_in(u).wait_send(), outer)
-        stage(t - 4, lambda u: (m_copy(u).wait_send(), n_copy(u).wait_send()), mid)
+        stage(t - 4, free_mid, mid)
         stage(t - 5, lambda u: k_copy(u).wait_send(), mid)
         stage(t - 6, lambda u: w_copy(u).wait_send(), mid)
-        stage(t - 5, lambda u: (e_out(u).wait_send(), g_mid(u).wait_send(), keep_own(u, full.at[slot(u)]).wait()), mid)
-        stage(t - 5, lambda u: (g_out(u).wait_send(), keep_own(u, e_dst.at[slot(u)]).wait()), outer)
-        stage(t - 7, lambda u: (f_out(u).wait_send(), keep_got(u).wait()), mid)
+        stage(t - 5, free_out, mid)
+        stage(t - 5, free_far, outer)
+        stage(t - 7, free_got, mid)
         stage(t - 5, lambda u: g_mid(u).wait_recv(), mid)
         stage(t - 6, lambda u: g_out(u).wait_recv(), outer)
         stage(t - 7, lambda u: f_out(u).wait_recv(), outer)
@@ -464,42 +915,146 @@
         stage(t - 2, t1_b, mid)
         stage(t - 1, t1_a)
         stage(t, produce)
+        tasks(t)
         return carry
 
-    lax.fori_loop(0, total + 8, body, 0)
-
-
-def gradient_sums(pairs, half):
-    segments, operands = [], []
-    for kind, left, right in pairs:
-        area = half * right.shape[1] if kind == "D" else left.shape[1] * half
-        segments.append((kind, area // (BR * BC)))
-        operands += [left, right]
-    total = sum(s[1] for s in segments)
-    tokens = operands[0].shape[0]
+    lax.fori_loop(0, max(total + 8, at_last + chunks // 2), body, 0)
+    result_copy().wait()
+    store_result.wait()
+    for i in range(chunks):
+        wait(grad_copies(i))
+
+
+def back(
+    inner,
+    cotangent,
+    gate,
+    up,
+    act_two,
+    attended,
+    queries,
+    keys,
+    values,
+    logs,
+    starts,
+    table,
+    act_one,
+    hidden_state,
+    own_inputs,
+    params,
+    w_down,
+    w_gate,
+    w_out,
+    w_qkv,
+):
+    length, width = cotangent.shape
+    hidden, units = inner.shape[1], attended.shape[1]
+    half, part_rows, block = width // 2, length // 2, length // 4
+    area, chunks = BR * BC, block // 64
+    counts = [hidden * half // area, half * 2 * hidden // area, units * half // area, half * 3 * units // area]
     bases, end = [], 0
-    for _, blocks in segments:
+    for blocks in counts:
         bases.append(-(-end // blocks) * blocks)
         end = bases[-1] + blocks
-    wide, thin = pltpu.VMEM((SLOTS, BR, BC), BF), pltpu.VMEM((SLOTS, BR // 2, BC), BF)
-    dma = pltpu.SemaphoreType.DMA((SLOTS,))
-    sums = pl.pallas_call(
-        functools.partial(gradient_kernel, segments, bases, half),
-        out_shape=jax.ShapeDtypeStruct((2, end, BR, BC), BF),
-        in_specs=[pl.BlockSpec(memory_space=pl.ANY)] * len(operands),
-        out_specs=pl.BlockSpec(memory_space=pl.ANY),
-        scratch_shapes=[pltpu.VMEM(v.shape, v.dtype) for v in operands]
-        + [pltpu.SemaphoreType.DMA((len(operands),)), pltpu.VMEM((2, BR, tokens), BF)]
-        + [wide, wide, wide, thin, thin, thin, thin, thin, thin, wide, wide, thin, thin, thin, wide]
-        + [dma] * 24,
+
+    def bf(*shape):
+        return jax.ShapeDtypeStruct(shape, BF)
+
+    def f32(*shape):
+        return jax.ShapeDtypeStruct(shape, F32)
+
+    outs = [
+        bf(2, end, BR, BC),
+        bf(block, half),
+        bf(block, half),
+        f32(block, half),
+        f32(block, half),
+        f32(8, width),
+        f32(8, units),
+    ]
+    any_spec, vmem_spec = pl.BlockSpec(memory_space=pl.ANY), pl.BlockSpec(memory_space=pltpu.VMEM)
+    wide, thin = bf(SLOTS, BR, BC), bf(SLOTS, BR // 2, BC)
+    scratch = [
+        bf(2, BR, length),
+        bf(2, length, BR),
+        bf(length, max(hidden, 3 * units)),
+        bf(length, width),
+        bf(length, 2 * hidden),
+        bf(length, units),
+        bf(length, units),
+        bf(2, 3, length, 128),
+        f32(2, length, 2),
+        f32(length, 128),
+        f32(length, 128),
+        bf(2, 128, width),
+        bf(2, 2, length, 128),
+        bf(2, hidden, BC),
+        bf(2, 2, BC, max(hidden, 2 * units)),
+        bf(units, width),
+        bf(3, part_rows, BC),
+        bf(3, part_rows, BC),
+        bf(3, part_rows, BC),
+        bf(4, block, BC),
+        bf(4, block, BC),
+        f32(block, width),
+        f32(block, width),
+        f32(block, width),
+        bf(block, width),
+        bf(block, width),
+        wide,
+        wide,
+        wide,
+        thin,
+        thin,
+        thin,
+        thin,
+        thin,
+        thin,
+        wide,
+        wide,
+        thin,
+        thin,
+        thin,
+        wide,
+    ]
+    dma = pltpu.SemaphoreType.DMA
+    flops = 2 * length * width * (8 * units + 6 * hidden) + 2 * length * 640 * 5 * units
+    outs = pl.pallas_call(
+        functools.partial(back_kernel, bases),
+        out_shape=outs,
+        in_specs=[any_spec] * 10 + [vmem_spec] * 2 + [any_spec] * 3 + [vmem_spec] + [any_spec] * 4,
+        out_specs=[any_spec] * 5 + [vmem_spec] * 2,
+        scratch_shapes=[pltpu.VMEM(v.shape, v.dtype) for v in scratch]
+        + [dma((10 + chunks,)), dma((24,)), dma((14,)), dma((2 + 10 * chunks,))]
+        + [dma((SEMAPHORES,))] * 22
+        + [dma((SLOTS,))] * 2,
         compiler_params=pltpu.CompilerParams(
-            collective_id=1, has_side_effects=True, vmem_limit_bytes=60 * 2**20
+            collective_id=1, has_side_effects=True, vmem_limit_bytes=63 * 2**20
         ),
-        cost_estimate=pl.CostEstimate(
-            flops=4 * total * BR * BC * tokens, bytes_accessed=4 * total * BR * BC, transcendentals=0
-        ),
-    )(*operands)
-    return sums, bases
+        cost_estimate=pl.CostEstimate(flops=flops, bytes_accessed=200 * 2**20, transcendentals=length * 8192),
+    )(
+        inner,
+        cotangent,
+        gate,
+        up,
+        act_two,
+        attended,
+        queries,
+        keys,
+        values,
+        logs,
+        starts,
+        table,
+        act_one,
+        hidden_state,
+        own_inputs,
+        params,
+        w_down,
+        w_gate,
+        w_out,
+        w_qkv,
+    )
+    return outs[0], bases, *outs[1:]
 
 
 def spread_qkv_kernel(side_ref, block_ref, out_ref):
@@ -597,7 +1152,6 @@
     k_out,
     v_out,
     att_out,
-    raw_out,
     log_out,
     hid_out,
     act_two,
@@ -621,7 +1175,6 @@
     ks,
     vs,
     att,
-    raw,
     logs,
     core_in,
     row_src,
@@ -678,7 +1231,7 @@
     mine, theirs = span(r * units, units), span((1 - r) * units, units)
     own_rows, far_rows = span(c * part, part), span((1 - c) * part, part)
     lo, hi = pl.ds(0, half), pl.ds(half, half)
-    quarter = half // 4
+    quarter, eighth = half // 4, half // 8
     down_quarter = hidden // 4
 
     load_tok = load(0, tokens, tok.at[own_rows, lo])
@@ -687,7 +1240,7 @@
     gate_cols = span(r * hidden, hidden)
 
     def load_gate(i):
-        return load(3 + i % 2, gate_w.at[pl.ds(i * quarter, quarter), :, gate_cols], gate_own.at[i % 2])
+        return load(3 + i % 2, gate_w.at[pl.ds(i * eighth, eighth), :, gate_cols], gate_own.at[i % 2])
 
     load_d = load(5, down_w.at[span(r * hidden, hidden)], wd_out.at[:, lo])
     load_c = load(6, cotangent, cot_out.at[own_rows, lo])
@@ -751,14 +1304,14 @@
     q_x.start()
     tok_c.start()
     c_c.start()
-    for i in range(4):
-        if i == 2:
+    for i in range(8):
+        if i == 4:
             q_x.wait_recv()
             start(q_n)
             tok_x.start()
         gates[i].wait()
-        part_gate(gate_own.at[i % 2], pl.ds(i * quarter, quarter))
-        if i + 2 < 4:
+        part_gate(gate_own.at[i % 2], pl.ds(i * eighth, eighth))
+        if i + 2 < 8:
             gates.append(load_gate(i + 2))
     tok_x.wait_recv()
     tok_f.start()
@@ -846,13 +1399,11 @@
                 outs.append(got[:, :HEAD] / totals)
                 logs[p, begin:end, h : h + 1] = maxima + jnp.log(totals)
             out = jnp.concatenate(outs, axis=1)
-            raw[begin:end, span(lane0, 128)] = out
             att[begin:end, span(lane0, 128)] = out.astype(BF)
         return carry
 
     lax.fori_loop(0, pairs, attend, 0)
     store(att, att_out)
-    store(raw, raw_out)
     store(logs, log_out)
 
     load_o.wait()
@@ -965,7 +1516,6 @@
         bf(length, units),
         bf(length, units),
         bf(length, units),
-        f32(length, units),
         f32(pairs, length, 2),
         f32(block, width),
         bf(length, width),
@@ -986,12 +1536,11 @@
         bf(units, width),
         bf(2, width, hidden),
         bf(4, half // 4, 2, hidden),
-        bf(2, half // 4, 2, hidden),
+        bf(2, half // 8, 2, hidden),
         bf(length, units),
         bf(length, units),
         bf(length, units),
         bf(length, units),
-        f32(length, units),
         f32(pairs, length, 2),
         bf(part, width),
         bf(block, width),
@@ -1055,7 +1604,6 @@
         keys,
         values,
         attended,
-        raw,
         logs,
         hidden_state,
         act_two,
@@ -1080,47 +1628,97 @@
         down_weight,
         cotangent,
     )
-    block = c * 2 + r
-    own_inputs = own_inputs.astype(F32)
-    _, normal_two, inverse_two = norm_forward(hidden_state, params[2], params[3])
-    gate, up = gate.astype(F32), up.astype(F32)
-
-    feed = reduce_blocks(dot(inner, w_down).astype(BF), place)
-    result = (hidden_state + feed).astype(BF)
-    result = ordered(r, result[:, :half], swap(result[:, half:], "row"))
-
-    grad_inner = dot_t(cot_all, w_down)
-    rate = 1.0 / (1.0 + jnp.exp(-gate))
-    silu = gate * rate
-    grad_gate = (grad_inner * up * (rate * (1.0 + gate * (1.0 - rate)))).astype(BF)
-    grad_up = (grad_inner * silu).astype(BF)
-    grad_two = jnp.stack([grad_gate, grad_up])
-    grad_pair = jnp.concatenate([grad_gate, grad_up], axis=1)
-    grad_act_two = reduce_blocks(
-        jnp.einsum("ksf,kdf->sd", grad_two, w_gate, preferred_element_type=F32).astype(BF), place
-    )
-    grad_norm, ln2_gain_grad, ln2_bias_grad = norm_backward(
-        grad_act_two, normal_two, inverse_two, params[2]
-    )
-    own_cot = piece(cot_all, block, 4).astype(F32)
-    grad_hidden = own_cot + grad_norm
-    grad_branch = gather_blocks(grad_hidden.astype(BF), place)
-    grad_attended = dot_t(grad_branch, w_out).astype(BF)
-    grad_joined = attention_backward(
-        queries, keys, values, grad_attended, raw, logs, starts, table
-    )
-    grad_joined = jnp.concatenate(grad_joined, axis=1)
-    bias_grad = jnp.sum(grad_joined, axis=0, dtype=F32)
-    grad_kinds = grad_joined.reshape(length, 3, units)
-    grad_act_one = reduce_blocks(
-        jnp.einsum("sku,kdu->sd", grad_kinds, w_qkv, preferred_element_type=F32).astype(BF), place
-    )
-    _, normal_one, inverse_one = norm_forward(own_inputs, params[0], params[1])
-    grad_norm, ln1_gain_grad, ln1_bias_grad = norm_backward(
-        grad_act_one, normal_one, inverse_one, params[0]
-    )
-    input_grad = grad_hidden + grad_norm
-    input_grad = ordered(r, input_grad[:, :half], swap(input_grad[:, half:], "row"))
+    if place.count == 8:
+        sums, bases, result, result_far, input_grad, input_far, norm_grads, bias_grad = back(
+            inner,
+            cot_all,
+            gate,
+            up,
+            act_two,
+            attended,
+            queries,
+            keys,
+            values,
+            logs,
+            starts,
+            table,
+            act_one,
+            hidden_state,
+            own_inputs,
+            params,
+            w_down,
+            w_gate,
+            w_out,
+            w_qkv,
+        )
+        result = ordered(r, result, result_far)
+        input_grad = ordered(r, input_grad, input_far)
+        ln1_gain_grad, ln1_bias_grad, ln2_gain_grad, ln2_bias_grad = norm_grads[:4]
+        bias_grad = bias_grad[:3]
+        side = r.reshape(1)
+        down_grad = spread_rows(side, sums, bases[0], half, hidden)
+        gate_up_grad = spread_columns(side, sums, bases[1], half, hidden, 2, 256)
+        out_grad = spread_rows(side, sums, bases[2], half, units)
+        qkv_grad = spread_columns(side, sums, bases[3], half, units, 3, 256)
+    else:
+        block = c * 2 + r
+        own_inputs = own_inputs.astype(F32)
+        _, normal_two, inverse_two = norm_forward(hidden_state, params[2], params[3])
+        gate, up = gate.astype(F32), up.astype(F32)
+
+        feed = reduce_blocks(dot(inner, w_down).astype(BF), place)
+        result = (hidden_state + feed).astype(BF)
+        result = ordered(r, result[:, :half], swap(result[:, half:], "row"))
+
+        grad_inner = dot_t(cot_all, w_down)
+        rate = 1.0 / (1.0 + jnp.exp(-gate))
+        silu = gate * rate
+        grad_gate = (grad_inner * up * (rate * (1.0 + gate * (1.0 - rate)))).astype(BF)
+        grad_up = (grad_inner * silu).astype(BF)
+        grad_two = jnp.stack([grad_gate, grad_up])
+        grad_pair = jnp.concatenate([grad_gate, grad_up], axis=1)
+        grad_act_two = reduce_blocks(
+            jnp.einsum("ksf,kdf->sd", grad_two, w_gate, preferred_element_type=F32).astype(BF), place
+        )
+        grad_norm, ln2_gain_grad, ln2_bias_grad = norm_backward(
+            grad_act_two, normal_two, inverse_two, params[2]
+        )
+        own_cot = piece(cot_all, block, 4).astype(F32)
+        grad_hidden = own_cot + grad_norm
+        grad_branch = gather_blocks(grad_hidden.astype(BF), place)
+        grad_attended = dot_t(grad_branch, w_out).astype(BF)
+        grad_joined = attention_backward(
+            queries, keys, values, grad_attended, attended, logs, starts, table
+        )
+        grad_joined = jnp.concatenate(grad_joined, axis=1)
+        bias_grad = jnp.sum(grad_joined, axis=0, dtype=F32)
+        grad_kinds = grad_joined.reshape(length, 3, units)
+        grad_act_one = reduce_blocks(
+            jnp.einsum("sku,kdu->sd", grad_kinds, w_qkv, preferred_element_type=F32).astype(BF), place
+        )
+        _, normal_one, inverse_one = norm_forward(own_inputs, params[0], params[1])
+        grad_norm, ln1_gain_grad, ln1_bias_grad = norm_backward(
+            grad_act_one, normal_one, inverse_one, params[0]
+        )
+        input_grad = grad_hidden + grad_norm
+        input_grad = ordered(r, input_grad[:, :half], swap(input_grad[:, half:], "row"))
+
+        pairs = (
+            ("D", act_two, grad_pair),
+            ("D", act_one, grad_joined),
+            ("U", attended, grad_branch),
+            ("U", inner, cot_all),
+        )
+        sums = []
+        for kind, left, right in pairs:
+            both = t_dot(left, right).astype(BF)
+            axis = 0 if kind == "D" else 1
+            own, sent = jnp.split(both, 2, axis)
+            sums.append([lax.psum(v, "dp").astype(F32) for v in (own, swap(sent, "row"))])
+        gate_up_grad = ordered(r, *[v.reshape(half, 2, hidden) for v in sums[0]], 2)
+        qkv_grad = ordered(r, *[v.reshape(half, 3, units) for v in sums[1]], 2)
+        out_grad = ordered(r, *sums[2])
+        down_grad = ordered(r, *sums[3])
 
     small = jnp.stack([ln1_gain_grad, ln1_bias_grad, ln2_gain_grad, ln2_bias_grad])
     small = small[:, :half] + swap(small[:, half:], "row")
@@ -1136,30 +1734,6 @@
     bias_grad = small[4 * half :].reshape(3, units)
     bias_grad = ordered(r, bias_grad, swap(bias_grad, "row"), 1)
 
-    pairs = (
-        ("D", act_two, grad_pair),
-        ("D", act_one, grad_joined),
-        ("U", attended, grad_branch),
-        ("U", inner, cot_all),
-    )
-    if place.count == 8:
-        sums, bases = gradient_sums(pairs, half)
-        side = r.reshape(1)
-        gate_up_grad = spread_columns(side, sums, bases[0], half, hidden, 2, 256)
-        qkv_grad = spread_columns(side, sums, bases[1], half, units, 3, 256)
-        out_grad = spread_rows(side, sums, bases[2], half, units)
-        down_grad = spread_rows(side, sums, bases[3], half, hidden)
-    else:
-        sums = []
-        for kind, left, right in pairs:
-            both = t_dot(left, right).astype(BF)
-            axis = 0 if kind == "D" else 1
-            own, sent = jnp.split(both, 2, axis)
-            sums.append([lax.psum(v, "dp").astype(F32) for v in (own, swap(sent, "row"))])
-        gate_up_grad = ordered(r, *[v.reshape(half, 2, hidden) for v in sums[0]], 2)
-        qkv_grad = ordered(r, *[v.reshape(half, 3, units) for v in sums[1]], 2)
-        out_grad = ordered(r, *sums[2])
-        down_grad = ordered(r, *sums[3])
     return (
         result,
         input_grad,

time: 946 us -> 740 us (0.78)
  waiting for transfers between devices: 109 us -> 10.8 us
  matrix products: 50.5 us -> 0 us
  other arithmetic: 38.3 us -> 13.7 us
  local copies, waits for them, and re-layouts: 18.9 us -> 5.11 us
    ppermute x14 -> x4, waiting for transfers between devices: 104 us -> 5.4 us  [swap(): return lax.ppermute(v, axis, SWAP)]
    dot_general x5 -> x0, matrix products: 50.5 us -> none  [the longest x1 17 us: local(): jnp.einsum('ksf,kdf->sd', grad_two, w_gate, preferred_element_type=F32)]
    convert_element_type x5 -> x0, other arithmetic: 13.1 us -> none  [the longest x3 6.34 us: add(): return (a.astype(F32) + b.astype(F32)).astype(BF)]
    pallas_call x2 -> x1, Pallas kernels: 489 us -> 480 us  [back(): pl.pallas_call(functools.partial(back_kernel, bases), out_shape=outs, in_...]
  transfers between devices with their start and end apart: 17 -> 7, of which waited for: 11 -> 4; matrix products, arithmetic and copies ran while one was open for 4% -> 2% of each run, Pallas kernels for 54% -> 6%
where the time goes in v4:
time: 740 us; the launch traced here: 735 us
  Pallas kernels  699 us (94%)
  other arithmetic  13.7 us (2%)
  waiting for transfers between devices  10.8 us (1%)
    pallas_call x1, Pallas kernels, back(): pl.pallas_call(functools.partial(back_kernel, bases), out_shape=outs, in_...  480 us
    pallas_call x1, Pallas kernels, front(): pl.pallas_call(front_kernel, out_shape=outs, in_specs=[any_spec] + [vmem_...  177 us
    pallas_call x4, Pallas kernels, spread(): pl.pallas_call(body, grid_spec=pltpu.PrefetchScalarGridSpec(num_scalar_pr...  41.8 us
  transfers between devices with their start and end apart: 7, of which 4 were waited for; matrix products, arithmetic and copies ran while one was open for 2% of the time, Pallas kernels for 6%

profile of v4, /device:TPU:0, one launch (start us, length us, event | category | flops | bytes accessed | tf_op | source)
XLA Modules:
  0.0 735.0 jit_solution(579254241551488013)
XLA Ops:
  1.4 3.0 collective-permute-start
  4.4 0.9 compare_reduce_fusion
  6.2 0.9 subtract_subtract_fusion.starts_ref
  7.0 1.9 multiply_cosine_fusion
  9.0 1.1 concatenate.38
  10.2 1.3 maximum_bitcast_fusion
  11.6 1.3 concatenate.40
  12.9 1.2 pad_maximum_fusion.1.table_ref
  15.4 176.8 %shard_map.203 = (bf16[1024,2048]{1,0:T(8,128)(2,1)}, bf16[1024,512]{1,0:T(8,128)(2,1)}, bf16[1024,512]{1,0:T(8,128)(2,1)}, bf16[1024,512]{1,0:T(8,128)(2,1)}, b...) custom-call(bf16[512,1024]{1,0:T(8,128)(2,1)} %tokens.1, ...), custom_call_target="tpu_custom_call" | custom-call | flops 20401094656 | bytes 104857600 | tf_op jit(solution)/shard_map/pallas_call | solution.py:1553
  192.2 480.0 %shard_map.204 = (bf16[2,60,512,256]{3,2,1,0:T(8,128)(2,1)}, bf16[256,1024]{1,0:T(8,128)(2,1)}, bf16[256,1024]{1,0:T(8,128)(2,1)}, f32[256,1024]{1,0:T(8,128)}, ...) custom-call(bf16[1024,1408]{1,0:T(8,128)(2,1)} %get-tuple-element.35.inner, ...), custom_call_target="tpu_custom_call" | custom-call | flops 55968792576 | bytes 209715200 | tf_op jit(solution)/shard_map/pallas_call | solution.py:1022
  672.2 0.8 slice.81
  673.0 1.0 collective-permute-start.1
  674.0 2.8 collective-permute-done.1
  677.5 1.7 broadcast_select_fusion.1
  679.3 0.8 collective-permute-start.3
  680.2 3.0 collective-permute-done.3
  683.2 1.5 pad_maximum_fusion
  684.7 2.4 collective-permute-done.4
  687.6 1.0 pad_maximum_fusion.2
  688.6 18.4 %shard_map.207 = f32[1024,2,2816]{2,1,0:T(2,128)} custom-call(s32[1]{0:T(128)} %bitcast.11.side_ref, bf16[2,60,512,256]{3,2,1,0:T(8,128)(2,1)} %get-tuple-element.58.block_ref), custom_call_target="tpu_custom_call" | custom-call | tf_op jit(solution)/shard_map/pallas_call | solution.py:1084
  707.0 8.9 %shard_map.205 = f32[3,1024,1024]{2,1,0:T(8,128)} custom-call(s32[1]{0:T(128)} %bitcast.11.side_ref, bf16[2,60,512,256]{3,2,1,0:T(8,128)(2,1)} %get-tuple-element.58.block_ref), custom_call_target="tpu_custom_call" | custom-call | tf_op jit(solution)/shard_map/pallas_call | solution.py:1084
  715.9 8.5 %shard_map.208 = f32[2816,1024]{1,0:T(8,128)} custom-call(s32[1]{0:T(128)} %bitcast.11.side_ref, bf16[2,60,512,256]{3,2,1,0:T(8,128)(2,1)} %get-tuple-element.58.block_ref), custom_call_target="tpu_custom_call" | custom-call | tf_op jit(solution)/shard_map/pallas_call | solution.py:1084
  724.4 6.0 shard_map.206
  731.5 2.6 collective-permute-done.6
  (57 shorter events, 6.2 us)
Async XLA Ops:
  0.6 13.5 %copy-start = (f32[3,1024]{1,0:T(4,128)S(1)}, f32[3,1024]{1,0:T(4,128)}, u32[]{:S(2)}) copy-start(f32[3,1024]{1,0:T(4,128)} %param.17) | copy-start | bytes 36868
  1.4 13.3 %collective-permute-start = (f32[4,1024]{1,0:T(4,128)S(1)}, f32[4,1024]{1,0:T(4,128)S(1)}, u32[]{:S(2)}, u32[]{:S(2)}) collective-permute-start(f32[4,1024]{1,0:T(4,128)S(1)} %pad_maximum_fusion.4), channel_id=1, source_target_pairs={{0,2},{2,0},{1,3},{3,1},{4,6},{6,4},{5,7},{7,5},{8,10},{10,8},{9,1... | collective-permute-start | bytes 49160 | tf_op jit(solution)/shard_map/ppermute | solution.py:23
  11.4 1.4 copy-start.2
  11.5 3.2 copy-start.5
  11.5 3.2 copy-start.6
  11.5 3.2 copy-start.7
  11.6 3.2 copy-start.8
  672.1 7.1 copy-start.9
  672.2 8.0 %copy-start.3 = (bf16[256,1024]{1,0:T(8,128)(2,1)S(1)}, bf16[256,1024]{1,0:T(8,128)(2,1)}, u32[]{:S(2)}) copy-start(bf16[256,1024]{1,0:T(8,128)(2,1)} %get-tuple-element.52) | copy-start | bytes 1572868
  672.2 8.0 %copy-start.4 = (bf16[256,1024]{1,0:T(8,128)(2,1)S(1)}, bf16[256,1024]{1,0:T(8,128)(2,1)}, u32[]{:S(2)}) copy-start(bf16[256,1024]{1,0:T(8,128)(2,1)} %get-tuple-element.53) | copy-start | bytes 1572868
  673.0 3.7 collective-permute-start.1
  677.5 1.8 collective-permute-start.2
  679.3 3.9 collective-permute-start.3
  683.2 3.8 collective-permute-start.4
  687.1 43.3 %collective-permute-start.5 = (f32[5632]{0:T(1024)S(1)}, f32[5632]{0:T(1024)S(1)}, u32[]{:S(2)}, u32[]{:S(2)}) collective-permute-start(f32[5632]{0:T(1024)S(1)} %add.23), channel_id=1, source_target_pairs={{0,16},{4,20},{8,24},{12,28},{16,0},{20,4},{24,8},{28,12},{1,17},{... | collective-permute-start | bytes 67592 | tf_op jit(solution)/shard_map/ppermute | solution.py:1730
  724.4 10.4 %copy-start.1 = (f32[3,1024]{1,0:T(4,128)S(1)}, f32[3,1024]{1,0:T(4,128)}, u32[]{:S(2)}) copy-start(f32[3,1024]{1,0:T(4,128)} %param.17) | copy-start | bytes 36868
  730.4 3.7 collective-permute-start.6

commit v5 on v4

--- a/solution.py
+++ b/solution.py
@@ -106,19 +106,24 @@
     return grad_input, jnp.sum(grad * normal, axis=0), jnp.sum(grad, axis=0)
 
 
-def doc_positions(segment_ids):
-    places = jnp.arange(segment_ids.shape[0], dtype=jnp.int32)
-    starts = jnp.concatenate([jnp.ones((1,), dtype=bool), segment_ids[1:] != segment_ids[:-1]])
-    first_place = lax.cummax(jnp.where(starts, places, jnp.zeros_like(places)), axis=0)
-    return places - first_place
-
-
-def rotary_tables(segment_ids):
-    places = doc_positions(segment_ids).astype(F32)
-    freq_index = jnp.arange(ROT // 2, dtype=F32)
-    inverse = jnp.exp(freq_index * (-2.0 / ROT) * math.log(ROPE_BASE))
-    angles = places[:, None] * inverse[None, :]
-    return (jnp.cos(angles), jnp.sin(angles))
+def first_places(segment_ids):
+    return jnp.sum(segment_ids[None, :] < segment_ids[:, None], axis=1, dtype=jnp.int32)
+
+
+def rotary_table(places):
+    lane = jnp.arange(128, dtype=jnp.int32) % HEAD
+    half_rot = ROT // 2
+    inverse = jnp.exp((lane % half_rot).astype(F32) * (-2.0 / ROT) * math.log(ROPE_BASE))
+    angles = places.astype(F32)[:, None] * inverse[None, :]
+    cosines, sines = jnp.cos(angles), jnp.sin(angles)
+    low, turns = (lane < half_rot)[None, :], (lane < ROT)[None, :]
+    return jnp.stack(
+        [
+            jnp.where(turns, cosines, 1.0),
+            jnp.where(low, -sines, 0.0),
+            jnp.where(turns & ~low, sines, 0.0),
+        ]
+    )
 
 
 LONGEST = 512
@@ -175,16 +180,6 @@
     dv_ref[...] = dv_acc[...].astype(BF)
 
 
-def tables(cosines, sines):
-    length = cosines.shape[0]
-    ones = jnp.ones((length, HEAD - 16), F32)
-    none = jnp.zeros((length, HEAD - 8), F32)
-    one = jnp.concatenate([cosines, cosines, ones], axis=1)
-    ahead = jnp.concatenate([-sines, none], axis=1)
-    behind = jnp.concatenate([none[:, :8], sines, none[:, 8:]], axis=1)
-    return jnp.stack([jnp.concatenate([v, v], axis=1) for v in (one, ahead, behind)])
-
-
 def attention_backward(queries, keys, values, grads, attended, logs, starts, table):
     length, units = queries.shape
     pairs = units // 128
@@ -210,7 +205,10 @@
 BR = 512
 BC = 256
 SLOTS = 5
-SEMAPHORES = 8
+SEMAPHORES = 10
+SHORT = 3
+FAR_SLOTS = 8
+LEAD = 2
 
 
 def back_kernel(
@@ -240,8 +238,11 @@
     res_got,
     grad_own,
     grad_got,
+    small_out,
     norm_sums,
     bias_sums,
+    small_src,
+    small_in,
     turn,
     turn_in,
     joint,
@@ -287,6 +288,7 @@
     once_sem,
     piece_sem,
     gather_sem,
+    small_sem,
     *sems,
 ):
     out_own, out_got = out_ref.at[0], out_ref.at[1]
@@ -377,10 +379,8 @@
             for k, ref in enumerate((queries, keys, values))
         ) + (pltpu.make_async_copy(logs.at[p], head_logs.at[s], once_sem.at[22 + s]),)
 
-    def turn_load(source, i):
-        return tuple(
-            local_copy(7 + side, source.at[:, span(side * half + i * BR, BR)], turn_in.at[side]) for side in range(2)
-        )
+    def turn_load(source, i, side):
+        return local_copy(7 + side, source.at[:, span(side * half + i * BR, BR)], turn_in.at[side])
 
     def start(copies):
         for copy in copies:
@@ -393,7 +393,7 @@
     start((load_inner, load_cot, load_hid, load_own, load_att, load_wo))
     start(down_rows_load(0))
     start(down_columns_load(0))
-    start(turn_load(act_two, 0))
+    start((turn_load(act_two, 0, 0), turn_load(act_two, 0, 1)))
 
     @pl.when(mid)
     def _():
@@ -410,6 +410,12 @@
 
     def slot(u):
         return lax.rem(u, SLOTS)
+
+    def short(u):
+        return lax.rem(u, SHORT)
+
+    def far_slot(u):
+        return lax.rem(u, FAR_SLOTS)
 
     def copy(name, u, src, dst, peer):
         s = lax.rem(u, SEMAPHORES)
@@ -432,37 +438,37 @@
         return ref.at[spot(u), halves(index)]
 
     def x_copy(u):
-        return copy("x", u, x_src.at[slot(u)], x_dst.at[slot(u)], x_peer)
+        return copy("x", u, x_src.at[short(u)], x_dst.at[far_slot(u)], x_peer)
 
     def y_copy(u):
-        return copy("y", u, part.at[slot(u), halves(1 - y)], y_dst.at[slot(u)], y_peer)
+        return copy("y", u, part.at[short(u), halves(1 - y)], y_dst.at[slot(u)], y_peer)
 
     def e_in(u):
-        return copy("ei", u, acc.at[slot(u)], e_dst.at[slot(u)], e_peer)
+        return copy("ei", u, acc.at[short(u)], e_dst.at[slot(u)], e_peer)
 
     def e_out(u):
-        return copy("eo", u, full.at[slot(u)], e_dst.at[slot(u)], e_peer)
+        return copy("eo", u, full.at[short(u)], e_dst.at[slot(u)], e_peer)
 
     def m_copy(u):
-        return copy("m", u, low.at[slot(u)], m_dst.at[slot(u)], m_peer)
+        return copy("m", u, low.at[short(u)], m_dst.at[slot(u)], m_peer)
 
     def g_mid(u):
-        return copy("g", u, full.at[slot(u)], out_half(out_own, u, y), y_peer)
+        return copy("g", u, full.at[short(u)], out_half(out_own, u, y), y_peer)
 
     def g_out(u):
         return copy("g", u, e_dst.at[slot(u)], out_half(out_own, u, y), y_peer)
 
     def f_in(u):
-        return copy("fi", u, x_dst.at[slot(u)], f_dst.at[slot(u)], e_peer)
+        return copy("fi", u, x_dst.at[far_slot(u)], f_dst.at[slot(u)], e_peer)
 
     def f_out(u):
         return copy("fo", u, whole.at[slot(u)], out_got.at[spot(u)], e_peer)
 
     def n_copy(u):
-        return copy("n", u, deep.at[slot(u), halves(1 - upper)], n_dst.at[slot(u)], m_peer)
+        return copy("n", u, deep.at[short(u), halves(1 - upper)], n_dst.at[slot(u)], m_peer)
 
     def k_copy(u):
-        return copy("k", u, key.at[slot(u)], k_dst.at[slot(u)], y_peer)
+        return copy("k", u, key.at[short(u)], k_dst.at[slot(u)], y_peer)
 
     def w_copy(u):
         place = whole.at[slot(u), halves(upper)]
@@ -488,64 +494,64 @@
         def _():
             fn(t - first)
 
-    def unit_block(k, s, lhs, rhs):
+    def unit_block(k, side, ref, s, lhs, rhs):
         left = lhs[:, span(k * size, size)].T
-        for side, ref in ((1, x_src), (0, part)):
-            for q in range(half // BC):
-                right = rhs[:, side * half + q * BC : side * half + (q + 1) * BC]
-                ref[s, q * size : (q + 1) * size] = jnp.dot(left, right, preferred_element_type=F32).astype(BF)
-
-    def feature_block(k, s, rhs, source, following):
+        for q in range(half // BC):
+            right = rhs[:, side * half + q * BC : side * half + (q + 1) * BC]
+            ref[s, q * size : (q + 1) * size] = jnp.dot(left, right, preferred_element_type=F32).astype(BF)
+
+    def feature_block(k, side, ref, s, rhs, source, following):
         columns = rhs.shape[1] // BC
 
         for i in range(half // BR):
 
             @pl.when(k == i * columns)
             def _(i=i):
-                wait(turn_load(source, i))
-                for side in range(2):
-                    turn[side] = turn_in[side].T
-                following_load = following if i + 1 == half // BR else (source, i + 1)
-                if following_load is not None:
-                    start(turn_load(*following_load))
+                turn_load(source, i, side).wait()
+                turn[side] = turn_in[side].T
+                if i + 1 < half // BR:
+                    turn_load(source, i + 1, side).start()
+                elif following is not None:
+                    turn_load(following, 0, side).start()
 
         right = rhs[:, span(lax.rem(k, columns) * BC, BC)]
-        for side, ref in ((1, x_src), (0, part)):
-            ref[s] = jnp.dot(turn[side], right, preferred_element_type=F32).astype(BF)
-
-    def produce(u):
-        s = slot(u)
-
+        ref[s] = jnp.dot(turn[side], right, preferred_element_type=F32).astype(BF)
+
+    def produce(u, side, ref):
+        s = short(u)
+        within(u, firsts[0], segments[0], lambda k: unit_block(k, side, ref, s, joint, branch))
+        within(u, firsts[1], segments[1], lambda k: feature_block(k, side, ref, s, pair, act_two, act_one))
+        within(u, firsts[2], segments[2], lambda k: unit_block(k, side, ref, s, att, branch))
+        within(u, firsts[3], segments[3], lambda k: feature_block(k, side, ref, s, joint, act_one, None))
+
+    def produce_own(u):
+        produce(u, 0, part)
+        y_copy(u).start()
+
+    def produce_far(u):
         @pl.when(u == 0)
         def _():
             wait((load_inner, load_cot))
 
-        within(u, firsts[0], segments[0], lambda k: unit_block(k, s, joint, branch))
-        within(u, firsts[1], segments[1], lambda k: feature_block(k, s, pair, act_two, (act_one, 0)))
-        within(u, firsts[2], segments[2], lambda k: unit_block(k, s, att, branch))
-        within(u, firsts[3], segments[3], lambda k: feature_block(k, s, joint, act_one, None))
+        produce(u, 1, x_src)
         x_copy(u).start()
-        y_copy(u).start()
 
     def t1_a(u):
-        s = slot(u)
         y_copy(u).wait_recv()
-        acc[s] = part[s, halves(y)] + y_dst[s]
+        acc[short(u)] = part[short(u), halves(y)] + y_dst[slot(u)]
         pl.when(outer)(lambda: e_in(u).start())
 
     def t1_b(u):
-        s = slot(u)
         e_in(u).wait_recv()
-        low[s] = acc[s] + e_dst[s]
+        low[short(u)] = acc[short(u)] + e_dst[slot(u)]
         m_copy(u).start()
 
     def t1_c(u):
-        s = slot(u)
         m_copy(u).wait_recv()
-        full[s] = low[s] + m_dst[s]
+        full[short(u)] = low[short(u)] + m_dst[slot(u)]
         e_out(u).start()
         g_mid(u).start()
-        keep_own(u, full.at[s]).start()
+        keep_own(u, full.at[short(u)]).start()
 
     def t1_d(u):
         e_out(u).wait_recv()
@@ -557,21 +563,18 @@
         pl.when(outer)(lambda: f_in(u).start())
 
     def t2_b(u):
-        s = slot(u)
         f_in(u).wait_recv()
-        deep[s] = x_dst[s] + f_dst[s]
+        deep[short(u)] = x_dst[far_slot(u)] + f_dst[slot(u)]
         n_copy(u).start()
 
     def t2_c(u):
-        s = slot(u)
         n_copy(u).wait_recv()
-        key[s] = deep[s, halves(upper)] + n_dst[s]
+        key[short(u)] = deep[short(u), halves(upper)] + n_dst[slot(u)]
         k_copy(u).start()
 
     def t2_d(u):
-        s = slot(u)
         k_copy(u).wait_recv()
-        whole[s, halves(upper)] = key[s] + k_dst[s]
+        whole[slot(u), halves(upper)] = key[short(u)] + k_dst[slot(u)]
         w_copy(u).start()
 
     def t2_e(u):
@@ -830,6 +833,77 @@
         grad_rows[at] = grad_rows[at] + grad
         start(grad_copies(i))
 
+    def small_copy(n, peer, cols=None):
+        src, dst = small_src.at[n], small_in.at[n]
+        if cols is not None:
+            src, dst = src.at[:, cols], dst.at[:, cols]
+        return pltpu.make_async_remote_copy(
+            src_ref=src,
+            dst_ref=dst,
+            send_sem=small_sem.at[n],
+            recv_sem=small_sem.at[8 + n],
+            device_id=peer,
+            device_id_type=MESH,
+        )
+
+    def small_hop(n, peer, step_peer):
+        small_copy(n, peer).wait_recv()
+        small_src[n + 1] = small_src[n] + small_in[n]
+        small_copy(n + 1, step_peer).start()
+
+    first_cols = pl.ds(0, half + units)
+
+    def small_task(i):
+        @pl.when(i == 0)
+        def _():
+            small_src[0, :, :half] = norm_sums[:, half:]
+            small_src[0, :, half : half + units] = bias_sums[...]
+            small_copy(0, x_peer, first_cols).start()
+
+        @pl.when(i == 1)
+        def _():
+            small_copy(0, x_peer, first_cols).wait_recv()
+            small_src[1, :, :half] = norm_sums[:, :half] + small_in[0, :, :half]
+            small_copy(1, c_peer, lo).start()
+
+        @pl.when(i == 2)
+        def _():
+            small_copy(1, c_peer, lo).wait_recv()
+            small_src[2, :, :half] = small_src[1, :, :half] + small_in[1, :, :half]
+            small_src[2, :, half : half + units] = bias_sums[...]
+            small_src[2, :, half + units :] = small_in[0, :, half : half + units]
+            small_copy(2, y_peer).start()
+
+        @pl.when(i == 3)
+        def _():
+            small_hop(2, y_peer, e_peer)
+
+        @pl.when(i == 4)
+        def _():
+            small_copy(3, e_peer).wait_recv()
+            small_src[4] = small_src[3] + small_in[3]
+            pl.when(mid)(lambda: small_copy(4, m_peer).start())
+
+        @pl.when((i == 5) & mid)
+        def _():
+            small_hop(4, m_peer, e_peer)
+
+        @pl.when(i == 6)
+        def _():
+            @pl.when(mid)
+            def _():
+                small_out[...] = small_src[5]
+                small_copy(4, m_peer).wait_send()
+                small_copy(5, e_peer).wait_send()
+
+            @pl.when(outer)
+            def _():
+                small_copy(5, e_peer).wait_recv()
+                small_out[...] = small_in[5]
+
+            for n, cols in ((0, first_cols), (1, lo), (2, None), (3, None)):
+                small_copy(n, x_peer, cols).wait_send()
+
     norm_sums[...] = jnp.zeros_like(norm_sums)
     bias_sums[...] = jnp.zeros_like(bias_sums)
     gates = hidden // 128
@@ -870,10 +944,12 @@
         pl.when(t == at_one - 1)(lambda: start(qkv_load(0)))
         summed(t, at_one, 2 * pieces, act_one_product, qkv_load)
         within(t, at_last, chunks // 2, two(norm_one_task))
-
-    def body(t, carry):
+        within(t, at_last + chunks // 2, 7, small_task)
+
+    def body(step, carry):
+        t = step - LEAD
+
         def free_all(u):
-            x_copy(u).wait_send()
             y_copy(u).wait_send()
 
         def free_mid(u):
@@ -883,7 +959,7 @@
         def free_out(u):
             e_out(u).wait_send()
             g_mid(u).wait_send()
-            keep_own(u, full.at[slot(u)]).wait()
+            keep_own(u, full.at[short(u)]).wait()
 
         def free_far(u):
             g_out(u).wait_send()
@@ -893,6 +969,7 @@
             f_out(u).wait_send()
             keep_got(u).wait()
 
+        stage(t + LEAD - 2, lambda u: x_copy(u).wait_send())
         stage(t - 2, free_all)
         stage(t - 3, lambda u: e_in(u).wait_send(), outer)
         stage(t - 3, lambda u: f_in(u).wait_send(), outer)
@@ -904,21 +981,22 @@
         stage(t - 7, free_got, mid)
         stage(t - 5, lambda u: g_mid(u).wait_recv(), mid)
         stage(t - 6, lambda u: g_out(u).wait_recv(), outer)
-        stage(t - 7, lambda u: f_out(u).wait_recv(), outer)
-        stage(t - 5, t2_e, mid)
-        stage(t - 4, t2_d, mid)
-        stage(t - 3, t2_c, mid)
-        stage(t - 2, t2_b, mid)
-        stage(t - 1, t2_a)
+        stage(t - 6, lambda u: f_out(u).wait_recv(), outer)
+        stage(t - 4, t2_e, mid)
+        stage(t - 3, t2_d, mid)
+        stage(t - 2, t2_c, mid)
+        stage(t - 1, t2_b, mid)
+        stage(t, t2_a)
         stage(t - 4, t1_d, outer)
         stage(t - 3, t1_c, mid)
         stage(t - 2, t1_b, mid)
         stage(t - 1, t1_a)
-        stage(t, produce)
-        tasks(t)
+        stage(t, produce_own)
+        stage(t + LEAD, produce_far)
+        tasks(step)
         return carry
 
-    lax.fori_loop(0, max(total + 8, at_last + chunks // 2), body, 0)
+    lax.fori_loop(0, max(total + 7 + LEAD, at_last + chunks // 2 + 7), body, 0)
     result_copy().wait()
     store_result.wait()
     for i in range(chunks):
@@ -969,12 +1047,15 @@
         bf(block, half),
         f32(block, half),
         f32(block, half),
-        f32(8, width),
-        f32(8, units),
+        f32(8, half + 2 * units),
     ]
     any_spec, vmem_spec = pl.BlockSpec(memory_space=pl.ANY), pl.BlockSpec(memory_space=pltpu.VMEM)
     wide, thin = bf(SLOTS, BR, BC), bf(SLOTS, BR // 2, BC)
     scratch = [
+        f32(8, width),
+        f32(8, units),
+        f32(6, 8, half + 2 * units),
+        f32(6, 8, half + 2 * units),
         bf(2, BR, length),
         bf(2, length, BR),
         bf(length, max(hidden, 3 * units)),
@@ -1001,19 +1082,19 @@
         f32(block, width),
         bf(block, width),
         bf(block, width),
+        bf(SHORT, BR, BC),
+        bf(SHORT, BR, BC),
+        bf(FAR_SLOTS, BR, BC),
+        thin,
+        bf(SHORT, BR // 2, BC),
+        thin,
+        bf(SHORT, BR // 2, BC),
+        thin,
+        bf(SHORT, BR // 2, BC),
         wide,
-        wide,
-        wide,
+        bf(SHORT, BR, BC),
         thin,
-        thin,
-        thin,
-        thin,
-        thin,
-        thin,
-        wide,
-        wide,
-        thin,
-        thin,
+        bf(SHORT, BR // 2, BC),
         thin,
         wide,
     ]
@@ -1023,9 +1104,9 @@
         functools.partial(back_kernel, bases),
         out_shape=outs,
         in_specs=[any_spec] * 10 + [vmem_spec] * 2 + [any_spec] * 3 + [vmem_spec] + [any_spec] * 4,
-        out_specs=[any_spec] * 5 + [vmem_spec] * 2,
+        out_specs=[any_spec] * 5 + [vmem_spec],
         scratch_shapes=[pltpu.VMEM(v.shape, v.dtype) for v in scratch]
-        + [dma((10 + chunks,)), dma((24,)), dma((14,)), dma((2 + 10 * chunks,))]
+        + [dma((10 + chunks,)), dma((24,)), dma((14,)), dma((2 + 10 * chunks,)), dma((16,))]
         + [dma((SEMAPHORES,))] * 22
         + [dma((SLOTS,))] * 2,
         compiler_params=pltpu.CompilerParams(
@@ -1057,90 +1138,136 @@
     return outs[0], bases, *outs[1:]
 
 
-def spread_qkv_kernel(side_ref, block_ref, out_ref):
-    per = out_ref.shape[2] // BC
-    for j in range(block_ref.shape[1]):
-        at = j % per * BC
-        out_ref[j // per, :, at : at + BC] = block_ref[0, j].astype(F32)
-
-
-def spread_pair_kernel(side_ref, block_ref, out_ref):
-    units = out_ref.shape[2]
-    for j in range(block_ref.shape[1]):
-        for at in range(0, BC, 128):
-            unit = j * BC + at
-            out_ref[:, unit // units, unit % units : unit % units + 128] = block_ref[
-                0, j, :, at : at + 128
-            ].astype(F32)
-
-
-def spread_rows_kernel(side_ref, block_ref, out_ref):
-    size = block_ref.shape[2]
-    for k in range(block_ref.shape[1]):
-        out_ref[k * size : (k + 1) * size] = block_ref[0, k].astype(F32)
-
-
-def spread(body, side, blocks, steps, in_spec, out_spec, out_shape):
+def spread_kernel(bases, sums, gate_up_out, qkv_out, out_out, down_out, *scratch):
+    buffers, (load_sem, store_sem) = scratch[:-2], scratch[-2:]
+    r = lax.axis_index("row")
+    half, hidden = gate_up_out.shape[0], gate_up_out.shape[2] // 2
+    units = out_out.shape[0] // 2
+    size = BR * BC // half
+    rows = BR // 2
+
+    def span(start, count):
+        return pl.ds(pl.multiple_of(start, count), count)
+
+    def widen_pair(src, dst, s):
+        def some(i, carry):
+            at = span(i * 64, 64)
+            for j in range(src.shape[1]):
+                for first in range(0, BC, 128):
+                    unit = j * BC + first
+                    dst[s, at, unit // hidden, unit % hidden : unit % hidden + 128] = src[
+                        s, j, at, first : first + 128
+                    ].astype(F32)
+            return carry
+
+        lax.fori_loop(0, rows // 64, some, 0)
+
+    def widen_kinds(src, dst, s):
+        per = units // BC
+        for j in range(src.shape[1]):
+            dst[s, j // per, :, j % per * BC : (j % per + 1) * BC] = src[s, j].astype(F32)
+
+    def widen_rows(src, dst, s):
+        def some(k, carry):
+            dst[s, span(k * size, size)] = src[s, k].astype(F32)
+            return carry
+
+        lax.fori_loop(0, src.shape[1], some, 0)
+
+    tasks = []
+    for w in range(2):
+        side = r if w == 0 else 1 - r
+        for i in range(half // rows):
+            block, at = i * rows // BR, pl.ds(i * rows % BR, rows)
+            per = 2 * hidden // BC
+            tasks.append(
+                (
+                    0,
+                    widen_pair,
+                    sums.at[w, pl.ds(bases[1] + block * per, per), at],
+                    gate_up_out.at[pl.ds(i * rows, rows), :, span(side * hidden, hidden)],
+                )
+            )
+    for w in range(2):
+        side = r if w == 0 else 1 - r
+        for q in range(half // BC):
+            at = pl.ds(q * size, size)
+            for n, base, out, count in ((1, bases[0], down_out, hidden), (3, bases[2], out_out, units)):
+                tasks.append(
+                    (
+                        n,
+                        widen_rows,
+                        sums.at[w, pl.ds(base, count // size), at],
+                        out.at[span(side * count, count), pl.ds(q * BC, BC)],
+                    )
+                )
+        for i in range(half // rows):
+            block, at = i * rows // BR, pl.ds(i * rows % BR, rows)
+            per = 3 * units // BC
+            tasks.append(
+                (
+                    2,
+                    widen_kinds,
+                    sums.at[w, pl.ds(bases[3] + block * per, per), at],
+                    qkv_out.at[:, pl.ds(i * rows, rows), span(side * units, units)],
+                )
+            )
+
+    uses, plan = [0] * 4, []
+    for n, widen, src, dst in tasks:
+        s = uses[n] % 4
+        uses[n] += 1
+        held, wide = buffers[2 * n], buffers[2 * n + 1]
+        load = pltpu.make_async_copy(src, held.at[s], load_sem.at[4 * n + s])
+        store = pltpu.make_async_copy(wide.at[s], dst, store_sem.at[4 * n + s])
+        plan.append((n, s, widen, held, wide, load, store))
+    busy = {}
+    ahead = 4
+    for step in plan[:ahead]:
+        step[5].start()
+    for i, (n, s, widen, held, wide, load, store) in enumerate(plan):
+        load.wait()
+        if (n, s) in busy:
+            busy.pop((n, s)).wait()
+        widen(held, wide, s)
+        store.start()
+        busy[n, s] = store
+        if i + ahead < len(plan):
+            plan[i + ahead][5].start()
+    for store in busy.values():
+        store.wait()
+
+
+def spread(sums, bases, half, units, hidden):
+    size, rows = BR * BC // half, BR // 2
+    shapes = [(half, 2, 2 * hidden), (3, half, 2 * units), (2 * units, half), (2 * hidden, half)]
+    pair, kinds = 2 * hidden // BC, 3 * units // BC
+    buffers = [
+        ((4, pair, rows, BC), BF),
+        ((4, rows, 2, hidden), F32),
+        ((4, hidden // size, size, BC), BF),
+        ((4, hidden, BC), F32),
+        ((4, kinds, rows, BC), BF),
+        ((4, 3, rows, units), F32),
+        ((4, units // size, size, BC), BF),
+        ((4, units, BC), F32),
+    ]
+    any_spec = pl.BlockSpec(memory_space=pl.ANY)
     return pl.pallas_call(
-        body,
-        grid_spec=pltpu.PrefetchScalarGridSpec(
-            num_scalar_prefetch=1, grid=(2, steps), in_specs=[in_spec], out_specs=out_spec
-        ),
-        out_shape=jax.ShapeDtypeStruct(out_shape, F32),
-        compiler_params=pltpu.CompilerParams(vmem_limit_bytes=48 * 2**20),
-    )(side, blocks)
-
-
-def place_of(which, side_ref):
-    return which + side_ref[0] - 2 * which * side_ref[0]
-
-
-def spread_columns(side, blocks, base, half, units, kinds, rows):
-    columns, per = kinds * units // BC, BR // rows
-    first = base // columns
-    in_spec = pl.BlockSpec(
-        (1, columns, rows, BC), lambda w, i, s: (w, first + i // per, i % per, 0)
-    )
-    if kinds == 3:
-        return spread(
-            spread_qkv_kernel,
-            side,
-            blocks,
-            half // rows,
-            in_spec,
-            pl.BlockSpec((3, rows, units), lambda w, i, s: (0, i, place_of(w, s))),
-            (3, half, 2 * units),
-        ).transpose(1, 0, 2)
-    return spread(
-        spread_pair_kernel,
-        side,
-        blocks,
-        half // rows,
-        in_spec,
-        pl.BlockSpec((rows, 2, units), lambda w, i, s: (i, 0, place_of(w, s))),
-        (half, 2, 2 * units),
-    )
-
-
-def spread_rows(side, blocks, base, half, units):
-    size = BR * BC // half
-    count = units // size
-    return spread(
-        spread_rows_kernel,
-        side,
-        blocks,
-        half // BC,
-        pl.BlockSpec((1, count, size, BC), lambda w, q, s: (w, base // count, q, 0)),
-        pl.BlockSpec((units, BC), lambda w, q, s: (place_of(w, s), q)),
-        (2 * units, half),
-    )
+        functools.partial(spread_kernel, bases),
+        out_shape=[jax.ShapeDtypeStruct(v, F32) for v in shapes],
+        in_specs=[any_spec],
+        out_specs=[any_spec] * 4,
+        scratch_shapes=[pltpu.VMEM(*v) for v in buffers] + [pltpu.SemaphoreType.DMA((16,))] * 2,
+        compiler_params=pltpu.CompilerParams(vmem_limit_bytes=56 * 2**20),
+    )(sums)
 
 
 def front_kernel(
     tokens,
     starts_ref,
     table_ref,
-    params_ref,
+    params_in,
     bias_ref,
     qkv_w,
     out_w,
@@ -1164,6 +1291,7 @@
     wd_out,
     cot_out,
     own_out,
+    params_ref,
     tok,
     act,
     wq,
@@ -1288,6 +1416,8 @@
     ag_c = remote(26, tok.at[own_block], tok.at[own_block], col_peer)
     ag_f = remote(27, tok.at[x_block], tok.at[x_block], col_peer)
 
+    p_x = remote(28, params_in, params_ref.at[:, hi], row_peer)
+
     def start(copies):
         for copy in copies:
             copy.start()
@@ -1301,6 +1431,8 @@
         wg[1, at] = ref[:, 1, :]
 
     pl.semaphore_wait(barrier, 5)
+    p_x.start()
+    params_ref[:, :half] = params_in[...]
     q_x.start()
     tok_c.start()
     c_c.start()
@@ -1319,6 +1451,7 @@
     g_x.start()
 
     load_tok.wait()
+    p_x.wait_recv()
     tok_c.wait_recv()
 
     def normed(v, at):
@@ -1491,7 +1624,7 @@
     arrived(d_n)
     c_c.wait_recv()
     c_f.wait_recv()
-    for copy in [q_x, tok_x, tok_c, o_x, g_x, d_x, c_x, c_c, c_f, rs_c, rs_x, ag_c, ag_f] + (
+    for copy in [p_x, q_x, tok_x, tok_c, o_x, g_x, d_x, c_x, c_c, c_f, rs_c, rs_x, ag_c, ag_f] + (
         q_n + o_n + g_n + d_n + ag_x
     ):
         copy.wait_send()
@@ -1528,6 +1661,7 @@
         bf(hidden, width),
         bf(length, width),
         bf(block, width),
+        f32(8, width),
     ]
     scratch = [
         bf(length, width),
@@ -1554,9 +1688,9 @@
         front_kernel,
         out_shape=outs,
         in_specs=[any_spec] + [vmem_spec] * 4 + [any_spec] * 5,
-        out_specs=[any_spec] * len(outs),
+        out_specs=[any_spec] * (len(outs) - 1) + [vmem_spec],
         scratch_shapes=[pltpu.VMEM(v.shape, v.dtype) for v in scratch]
-        + [dma((28,)), dma((28,)), dma((13,)), dma((16,))],
+        + [dma((29,)), dma((29,)), dma((13,)), dma((16,))],
         compiler_params=pltpu.CompilerParams(
             collective_id=2, has_side_effects=True, vmem_limit_bytes=62 * 2**20
         ),
@@ -1592,11 +1726,11 @@
     heads = units // HEAD
     hidden = gate_up_weight.shape[2] // 2
 
-    params = jnp.stack([ln1_gain, ln1_bias, ln2_gain, ln2_bias])
-    params = jnp.concatenate([params, swap(params, "row")], axis=1)
-    cosines, sines = rotary_tables(ids)
-    table = tables(cosines, sines)
-    starts = (jnp.arange(length, dtype=jnp.int32) - doc_positions(ids))[:, None]
+    none = jnp.zeros_like(ln1_gain)
+    params = jnp.stack([ln1_gain, ln1_bias, ln2_gain, ln2_bias] + [none] * 4)
+    firsts = first_places(ids)
+    table = rotary_table(jnp.arange(length, dtype=jnp.int32) - firsts)
+    starts = firsts[:, None]
     bias = piece(qkv_bias, r, 2, 1)
     (
         act_one,
@@ -1616,6 +1750,7 @@
         w_down,
         cot_all,
         own_inputs,
+        params,
     ) = front(
         tokens,
         starts,
@@ -1629,7 +1764,7 @@
         cotangent,
     )
     if place.count == 8:
-        sums, bases, result, result_far, input_grad, input_far, norm_grads, bias_grad = back(
+        sums, bases, result, result_far, input_grad, input_far, small = back(
             inner,
             cot_all,
             gate,
@@ -1653,13 +1788,10 @@
         )
         result = ordered(r, result, result_far)
         input_grad = ordered(r, input_grad, input_far)
-        ln1_gain_grad, ln1_bias_grad, ln2_gain_grad, ln2_bias_grad = norm_grads[:4]
-        bias_grad = bias_grad[:3]
-        side = r.reshape(1)
-        down_grad = spread_rows(side, sums, bases[0], half, hidden)
-        gate_up_grad = spread_columns(side, sums, bases[1], half, hidden, 2, 256)
-        out_grad = spread_rows(side, sums, bases[2], half, units)
-        qkv_grad = spread_columns(side, sums, bases[3], half, units, 3, 256)
+        norms = small[:4, :half]
+        bias_grad = ordered(r, small[:3, half : half + units], small[:3, half + units :], 1)
+        gate_up_grad, qkv_grad, out_grad, down_grad = spread(sums, bases, half, units, hidden)
+        qkv_grad = qkv_grad.transpose(1, 0, 2)
     else:
         block = c * 2 + r
         own_inputs = own_inputs.astype(F32)
@@ -1720,19 +1852,11 @@
         out_grad = ordered(r, *sums[2])
         down_grad = ordered(r, *sums[3])
 
-    small = jnp.stack([ln1_gain_grad, ln1_bias_grad, ln2_gain_grad, ln2_bias_grad])
-    small = small[:, :half] + swap(small[:, half:], "row")
-    small = small + swap(small, "col")
-    bias_grad = bias_grad.reshape(3, units)
-    small = jnp.concatenate([small.reshape(-1), bias_grad.reshape(-1)])
-    if place.count == 8:
-        for bit in (1, 2, 4):
-            small = small + lax.ppermute(small, "dp", dp_perm(bit, 8))
-    else:
-        small = lax.psum(small, "dp")
-    norms = small[: 4 * half].reshape(4, half)
-    bias_grad = small[4 * half :].reshape(3, units)
-    bias_grad = ordered(r, bias_grad, swap(bias_grad, "row"), 1)
+        small = jnp.stack([ln1_gain_grad, ln1_bias_grad, ln2_gain_grad, ln2_bias_grad])
+        small = small[:, :half] + swap(small[:, half:], "row")
+        norms = lax.psum(small, ("dp", "col"))
+        bias_grad = lax.psum(bias_grad.reshape(3, units), "dp")
+        bias_grad = ordered(r, bias_grad, swap(bias_grad, "row"), 1)
 
     return (
         result,

time: 740 us -> 706 us (0.954)
  Pallas kernels: 699 us -> 683 us
  waiting for transfers between devices: 10.8 us -> 0 us
    pallas_call x4 -> x1, Pallas kernels: 41.8 us -> 29.1 us  [spread(): pl.pallas_call(functools.partial(spread_kernel, bases), out_shape=[jax.Sh...]
    ppermute x7 -> x0, waiting for transfers between devices: 10.8 us -> none  [the longest x4 5.4 us: swap(): return lax.ppermute(v, axis, SWAP)]
  transfers between devices with their start and end apart: 7 -> 0, of which waited for: 4 -> 0; matrix products, arithmetic and copies ran while one was open for 2% -> 0% of each run, Pallas kernels for 6% -> 0%
where the time goes in v5:
time: 706 us; the launch traced here: 697 us
  Pallas kernels  683 us (97%)
  other arithmetic  9.3 us (1%)
    pallas_call x1, Pallas kernels, back(): pl.pallas_call(functools.partial(back_kernel, bases), out_shape=outs, in_...  473 us
    pallas_call x1, Pallas kernels, front(): pl.pallas_call(front_kernel, out_shape=outs, in_specs=[any_spec] + [vmem_...  181 us
    pallas_call x1, Pallas kernels, spread(): pl.pallas_call(functools.partial(spread_kernel, bases), out_shape=[jax.Sh...  29.1 us

profile of v5, /device:TPU:0, one launch (start us, length us, event | category | flops | bytes accessed | tf_op | source)
XLA Modules:
  0.0 696.6 jit_solution(15833979546235134812)
XLA Ops:
  0.6 0.0 copy-start
  0.7 1.3 convert_reduce_fusion
  2.0 0.0 copy-done
  2.1 0.6 constant_dynamic-slice_fusion.bias_ref
  2.7 1.4 stack.30.params_in
  4.0 1.0 copy.25.starts_ref
  5.1 2.0 fusion.3
  7.0 1.2 pad_maximum_fusion.1.table_ref
  8.3 180.6 %shard_map.203 = (bf16[1024,2048]{1,0:T(8,128)(2,1)}, bf16[1024,512]{1,0:T(8,128)(2,1)}, bf16[1024,512]{1,0:T(8,128)(2,1)}, bf16[1024,512]{1,0:T(8,128)(2,1)}, b...) custom-call(bf16[512,1024]{1,0:T(8,128)(2,1)} %tokens.1, ...), custom_call_target="tpu_custom_call" | custom-call | flops 20401094656 | bytes 104857600 | tf_op jit(solution)/shard_map/pallas_call | solution.py:1687
  188.9 472.9 %shard_map.204 = (bf16[2,60,512,256]{3,2,1,0:T(8,128)(2,1)}, bf16[256,1024]{1,0:T(8,128)(2,1)}, bf16[256,1024]{1,0:T(8,128)(2,1)}, f32[256,1024]{1,0:T(8,128)}, f32[256,1024]{1,0:T(8,128)}, /*index=5*/f32[8,2048]{1,0:T(8,128)}) custom-call(bf16[1024,1408]{1,0:T(8,128)(2,1)} %get-tuple-element.39.inner, bf16[1024,2048]{1,0:T(8,128)(2,1)} %get-tuple-element.40.cotangent, ...), custom_call_target="tpu_custom_call" | custom-call | flops 55968792576 | bytes 209715200 | tf_op jit(solution)/shard_map/pallas_call | solution.py:1103
  661.8 0.0 copy-start.4
  661.8 0.0 copy-start.2
  661.8 0.0 copy-start.3
  661.8 1.4 broadcast_select_fusion.3
  663.2 1.0 pad_maximum_fusion.2
  664.3 0.0 copy-done.4
  664.3 0.6 fusion.8
  664.9 0.0 copy-done.2
  664.9 0.0 copy-done.3
  664.9 0.2 broadcast_select_fusion.1
  665.2 1.5 pad_maximum_fusion
  666.6 0.6 pad_maximum_fusion.3
  667.2 29.1 %shard_map.205 = (f32[1024,2,2816]{2,1,0:T(2,128)}, f32[3,1024,1024]{2,1,0:T(8,128)}, f32[1024,1024]{1,0:T(8,128)}, f32[2816,1024]{1,0:T(8,128)}) custom-call(bf16[2,60,512,256]{3,2,1,0:T(8,128)(2,1)} %get-tuple-element.62.sums), custom_call_target="tpu_custom_call" | custom-call | tf_op jit(solution)/shard_map/pallas_call | solution.py:1256
  696.3 0.0 copy-done.1
  (7 shorter events, 0.0 us)
Async XLA Ops:
  0.6 1.4 copy-start
  661.8 2.5 copy-start.4
  661.8 3.1 copy-start.2
  661.8 3.1 copy-start.3
  667.2 29.1 %copy-start.1 = (f32[3,1024]{1,0:T(4,128)S(1)}, f32[3,1024]{1,0:T(4,128)}, u32[]{:S(2)}) copy-start(f32[3,1024]{1,0:T(4,128)} %param.17) | copy-start | bytes 36868

commit v6 on v5

--- a/solution.py
+++ b/solution.py
@@ -214,6 +214,7 @@
 def back_kernel(
     bases,
     inner,
+    cot_own,
     cotangent,
     gate,
     up,
@@ -229,6 +230,7 @@
     hidden_state,
     own_inputs,
     params_ref,
+    down_own,
     w_down,
     w_gate,
     w_out,
@@ -334,9 +336,17 @@
     x_block = span(c * part_rows + (1 - r) * block, block)
     lo, hi = pl.ds(0, half), pl.ds(half, half)
     load_inner = local_copy(0, inner, joint.at[:, pl.ds(0, hidden)])
-    load_cot = local_copy(1, cotangent, branch)
+    near_rows, far_rows = span(c * part_rows, part_rows), span((1 - c) * part_rows, part_rows)
+    load_cot = (
+        local_copy(1, cot_own, branch.at[near_rows, lo]),
+        local_copy(10 + block // 64, cotangent.at[near_rows, hi], branch.at[near_rows, hi]),
+        local_copy(11 + block // 64, cotangent.at[far_rows], branch.at[far_rows]),
+    )
     load_hid = local_copy(2, hidden_state, hid)
-    load_own = local_copy(3, cotangent.at[own_block], own)
+    load_own = (
+        local_copy(3, cot_own.at[span(r * block, block)], own.at[:, lo]),
+        local_copy(12 + block // 64, cotangent.at[own_block, hi], own.at[:, hi]),
+    )
     load_att = local_copy(4, attended, att)
     load_wo = local_copy(5, w_out, w_o)
     load_inputs = local_copy(6, own_inputs, own)
@@ -345,7 +355,10 @@
         s = lax.rem(i, 2)
         at = span(i * 128, 128)
         return (
-            pltpu.make_async_copy(w_down.at[at], down_rows.at[s], once_sem.at[s]),
+            pltpu.make_async_copy(
+                down_own.at[span(r * hidden + i * 128, 128)], down_rows.at[s, :, lo], once_sem.at[s]
+            ),
+            pltpu.make_async_copy(w_down.at[at], down_rows.at[s, :, hi], once_sem.at[24 + s]),
             pltpu.make_async_copy(gate.at[:, at], gate_in.at[s, 0], once_sem.at[2 + s]),
             pltpu.make_async_copy(up.at[:, at], gate_in.at[s, 1], once_sem.at[4 + s]),
         )
@@ -353,9 +366,31 @@
     def order(i):
         return lax.rem(i, 2) * (half // BC) + i // 2
 
+    class Either:
+        def __init__(self, flag, first, second):
+            self.flag, self.first, self.second = flag, first, second
+
+        def start(self):
+            pl.when(self.flag)(lambda: self.first().start())
+            pl.when(jnp.logical_not(self.flag))(lambda: self.second().start())
+
+        def wait(self):
+            self.first().wait()
+
     def down_columns_load(i):
         s = lax.rem(i, 2)
-        return (pltpu.make_async_copy(w_down.at[:, span(order(i) * BC, BC)], down_columns.at[s], once_sem.at[6 + s]),)
+        cols = span(i // 2 * BC, BC)
+
+        def of(ref):
+            return pltpu.make_async_copy(ref, down_columns.at[s], once_sem.at[6 + s])
+
+        return (
+            Either(
+                s == 0,
+                lambda: of(down_own.at[span(r * hidden, hidden), cols]),
+                lambda: of(w_down.at[:, cols]),
+            ),
+        )
 
     def gate_load(i):
         s = lax.rem(i, 2)
@@ -390,7 +425,7 @@
         for copy in copies:
             copy.wait()
 
-    start((load_inner, load_cot, load_hid, load_own, load_att, load_wo))
+    start((load_inner, *load_cot, load_hid, *load_own, load_att, load_wo))
     start(down_rows_load(0))
     start(down_columns_load(0))
     start((turn_load(act_two, 0, 0), turn_load(act_two, 0, 1)))
@@ -531,7 +566,7 @@
     def produce_far(u):
         @pl.when(u == 0)
         def _():
-            wait((load_inner, load_cot))
+            wait((load_inner, *load_cot))
 
         produce(u, 1, x_src)
         x_copy(u).start()
@@ -688,7 +723,7 @@
 
     def result_task(i):
         load_hid.wait()
-        load_own.wait()
+        wait(load_own)
         result[...] = (hid[...] + acc_rows[...]).astype(BF)
         result_copy().start()
         store_result.start()
@@ -949,13 +984,6 @@
     def body(step, carry):
         t = step - LEAD
 
-        def free_all(u):
-            y_copy(u).wait_send()
-
-        def free_mid(u):
-            m_copy(u).wait_send()
-            n_copy(u).wait_send()
-
         def free_out(u):
             e_out(u).wait_send()
             g_mid(u).wait_send()
@@ -969,30 +997,31 @@
             f_out(u).wait_send()
             keep_got(u).wait()
 
-        stage(t + LEAD - 2, lambda u: x_copy(u).wait_send())
-        stage(t - 2, free_all)
-        stage(t - 3, lambda u: e_in(u).wait_send(), outer)
+        stage(step - 2, lambda u: x_copy(u).wait_send())
+        stage(step - 2, lambda u: y_copy(u).wait_send())
+        stage(step - 3, lambda u: e_in(u).wait_send(), outer)
+        stage(step - 4, lambda u: m_copy(u).wait_send(), mid)
+        stage(step - 5, free_out, mid)
+        stage(step - 5, free_far, outer)
+        stage(step - 5, lambda u: g_mid(u).wait_recv(), mid)
+        stage(step - 6, lambda u: g_out(u).wait_recv(), outer)
         stage(t - 3, lambda u: f_in(u).wait_send(), outer)
-        stage(t - 4, free_mid, mid)
+        stage(t - 4, lambda u: n_copy(u).wait_send(), mid)
         stage(t - 5, lambda u: k_copy(u).wait_send(), mid)
         stage(t - 6, lambda u: w_copy(u).wait_send(), mid)
-        stage(t - 5, free_out, mid)
-        stage(t - 5, free_far, outer)
         stage(t - 7, free_got, mid)
-        stage(t - 5, lambda u: g_mid(u).wait_recv(), mid)
-        stage(t - 6, lambda u: g_out(u).wait_recv(), outer)
         stage(t - 6, lambda u: f_out(u).wait_recv(), outer)
         stage(t - 4, t2_e, mid)
         stage(t - 3, t2_d, mid)
         stage(t - 2, t2_c, mid)
         stage(t - 1, t2_b, mid)
         stage(t, t2_a)
-        stage(t - 4, t1_d, outer)
-        stage(t - 3, t1_c, mid)
-        stage(t - 2, t1_b, mid)
-        stage(t - 1, t1_a)
-        stage(t, produce_own)
-        stage(t + LEAD, produce_far)
+        stage(step - 4, t1_d, outer)
+        stage(step - 3, t1_c, mid)
+        stage(step - 2, t1_b, mid)
+        stage(step - 1, t1_a)
+        stage(step, produce_far)
+        stage(step, produce_own)
         tasks(step)
         return carry
 
@@ -1005,6 +1034,7 @@
 
 def back(
     inner,
+    cot_own,
     cotangent,
     gate,
     up,
@@ -1020,6 +1050,7 @@
     hidden_state,
     own_inputs,
     params,
+    down_own,
     w_down,
     w_gate,
     w_out,
@@ -1103,10 +1134,10 @@
     outs = pl.pallas_call(
         functools.partial(back_kernel, bases),
         out_shape=outs,
-        in_specs=[any_spec] * 10 + [vmem_spec] * 2 + [any_spec] * 3 + [vmem_spec] + [any_spec] * 4,
+        in_specs=[any_spec] * 11 + [vmem_spec] * 2 + [any_spec] * 3 + [vmem_spec] + [any_spec] * 5,
         out_specs=[any_spec] * 5 + [vmem_spec],
         scratch_shapes=[pltpu.VMEM(v.shape, v.dtype) for v in scratch]
-        + [dma((10 + chunks,)), dma((24,)), dma((14,)), dma((2 + 10 * chunks,)), dma((16,))]
+        + [dma((13 + chunks,)), dma((26,)), dma((14,)), dma((2 + 10 * chunks,)), dma((16,))]
         + [dma((SEMAPHORES,))] * 22
         + [dma((SLOTS,))] * 2,
         compiler_params=pltpu.CompilerParams(
@@ -1115,6 +1146,7 @@
         cost_estimate=pl.CostEstimate(flops=flops, bytes_accessed=200 * 2**20, transcendentals=length * 8192),
     )(
         inner,
+        cot_own,
         cotangent,
         gate,
         up,
@@ -1130,6 +1162,7 @@
         hidden_state,
         own_inputs,
         params,
+        down_own,
         w_down,
         w_gate,
         w_out,
@@ -1138,8 +1171,10 @@
     return outs[0], bases, *outs[1:]
 
 
-def spread_kernel(bases, sums, gate_up_out, qkv_out, out_out, down_out, *scratch):
-    buffers, (load_sem, store_sem) = scratch[:-2], scratch[-2:]
+def spread_kernel(
+    bases, sums, res_own, res_got, grad_own, grad_got, gate_up_out, qkv_out, out_out, down_out, res_out, grad_out, *scratch
+):
+    buffers, (load_sem, store_sem, row_sem) = scratch[:-3], scratch[-3:]
     r = lax.axis_index("row")
     half, hidden = gate_up_out.shape[0], gate_up_out.shape[2] // 2
     units = out_out.shape[0] // 2
@@ -1174,6 +1209,13 @@
 
         lax.fori_loop(0, src.shape[1], some, 0)
 
+    block = res_own.shape[0]
+    moves, places = [], []
+    for n, (src, dst) in enumerate(((res_own, res_out), (grad_own, grad_out), (res_got, res_out), (grad_got, grad_out))):
+        held = buffers[8 + n % 2].at[n // 2]
+        side = r if n < 2 else 1 - r
+        moves.append(pltpu.make_async_copy(src, held, row_sem.at[n]))
+        places.append(pltpu.make_async_copy(held, dst.at[span(side * block, block)], row_sem.at[4 + n]))
     tasks = []
     for w in range(2):
         side = r if w == 0 else 1 - r
@@ -1225,7 +1267,13 @@
     ahead = 4
     for step in plan[:ahead]:
         step[5].start()
+    for copy in moves:
+        copy.start()
     for i, (n, s, widen, held, wide, load, store) in enumerate(plan):
+        if i == ahead:
+            for copy, placing in zip(moves, places):
+                copy.wait()
+                placing.start()
         load.wait()
         if (n, s) in busy:
             busy.pop((n, s)).wait()
@@ -1234,11 +1282,12 @@
         busy[n, s] = store
         if i + ahead < len(plan):
             plan[i + ahead][5].start()
-    for store in busy.values():
-        store.wait()
-
-
-def spread(sums, bases, half, units, hidden):
+    for copy in list(busy.values()) + places:
+        copy.wait()
+
+
+def spread(sums, bases, rows_of, half, units, hidden):
+    block = rows_of[0].shape[0]
     size, rows = BR * BC // half, BR // 2
     shapes = [(half, 2, 2 * hidden), (3, half, 2 * units), (2 * units, half), (2 * hidden, half)]
     pair, kinds = 2 * hidden // BC, 3 * units // BC
@@ -1251,16 +1300,20 @@
         ((4, 3, rows, units), F32),
         ((4, units // size, size, BC), BF),
         ((4, units, BC), F32),
+        ((2, block, half), BF),
+        ((2, block, half), F32),
     ]
     any_spec = pl.BlockSpec(memory_space=pl.ANY)
     return pl.pallas_call(
         functools.partial(spread_kernel, bases),
-        out_shape=[jax.ShapeDtypeStruct(v, F32) for v in shapes],
-        in_specs=[any_spec],
-        out_specs=[any_spec] * 4,
-        scratch_shapes=[pltpu.VMEM(*v) for v in buffers] + [pltpu.SemaphoreType.DMA((16,))] * 2,
+        out_shape=[jax.ShapeDtypeStruct(v, F32) for v in shapes]
+        + [jax.ShapeDtypeStruct((2 * block, half), BF), jax.ShapeDtypeStruct((2 * block, half), F32)],
+        in_specs=[any_spec] * 5,
+        out_specs=[any_spec] * 6,
+        scratch_shapes=[pltpu.VMEM(*v) for v in buffers] + [pltpu.SemaphoreType.DMA((16,))] * 2
+        + [pltpu.SemaphoreType.DMA((8,))],
         compiler_params=pltpu.CompilerParams(vmem_limit_bytes=56 * 2**20),
-    )(sums)
+    )(sums, *rows_of)
 
 
 def front_kernel(
@@ -1325,10 +1378,19 @@
     dy, dz = 1 - 2 * y, 2 - 4 * zp
     row_peer, col_peer = {"row": 1 - r}, {"col": 1 - c}
     near = ({"dp": d + dy}, {"dp": d + dz}, {"dp": d + dy + dz})
+    level = lax.rem(d // 2, 4)
+    mid = (level == 1) | (level == 2)
+    line = level * 2 + y
+    next_peer, last_peer = {"dp": d + 2}, {"dp": d - 2}
+    mid_peer = {"dp": d + 2 - 4 * (level // 2)}
 
     barrier = pltpu.get_barrier_semaphore()
     for peer in (row_peer, col_peer) + near:
         pl.semaphore_signal(barrier, inc=1, device_id=peer, device_id_type=MESH)
+
+    @pl.when(mid)
+    def _():
+        pl.semaphore_signal(barrier, inc=1, device_id=mid_peer, device_id_type=MESH)
 
     stores = []
 
@@ -1370,8 +1432,6 @@
     def load_gate(i):
         return load(3 + i % 2, gate_w.at[pl.ds(i * eighth, eighth), :, gate_cols], gate_own.at[i % 2])
 
-    load_d = load(5, down_w.at[span(r * hidden, hidden)], wd_out.at[:, lo])
-    load_c = load(6, cotangent, cot_out.at[own_rows, lo])
     gates = [load_gate(0), load_gate(1)]
 
     rows_sub = span(sub * quarter, quarter)
@@ -1387,19 +1447,71 @@
         7, out_w.at[span((1 - r) * units + sub * out_rows, out_rows)], wo.at[out_sub, hi], row_peer
     )
     o_n = [remote(8 + k, wo.at[out_sub, hi], wo.at[out_sub, hi], p) for k, p in enumerate(near)]
+    rows_line = span(line * eighth, eighth)
     g_x = remote(
-        11, gate_w.at[rows_sub, :, span((1 - r) * hidden, hidden)], gate_far.at[sub], row_peer
+        11, gate_w.at[rows_line, :, span((1 - r) * hidden, hidden)], gate_far.at[line], row_peer
     )
-    g_n = [remote(12 + k, gate_far.at[sub], gate_far.at[sub], p) for k, p in enumerate(near)]
+
+    def gate_copy(n, at, peer):
+        place = gate_far.at[lax.rem(at + 4, 4) * 2 + y]
+        return remote(29 + n, place, place, peer)
+
+    def upward(h):
+        return gate_copy(h, level - h, next_peer)
+
+    def downward(h):
+        return gate_copy(3 + h, level + h, last_peer)
+
+    def across(n, at):
+        return gate_copy(6 + n, at, near[0])
+
+    def gate_hop(h):
+        if h == 0:
+            g_x.wait_recv()
+            pl.when(level < 3)(lambda: upward(0).start())
+            pl.when(level > 0)(lambda: downward(0).start())
+            across(0, level).start()
+            return
+
+        @pl.when(level >= h)
+        def _():
+            upward(h - 1).wait_recv()
+            if h < 3:
+                pl.when(level < 3)(lambda: upward(h).start())
+            across(h, level - h).start()
+
+        @pl.when(level + h <= 3)
+        def _():
+            downward(h - 1).wait_recv()
+            if h < 3:
+                pl.when(level > 0)(lambda: downward(h).start())
+            across(3 + h, level + h).start()
+
+    def gates_across(act):
+        act(across(0, level))
+        for h in range(1, 4):
+            pl.when(level >= h)(lambda h=h: act(across(h, level - h)))
+            pl.when(level + h <= 3)(lambda h=h: act(across(3 + h, level + h)))
+
+    def gates_sent():
+        gates_across(lambda copy: copy.wait_send())
+        for h in range(3):
+            pl.when((level < 3) & (level >= h))(lambda h=h: upward(h).wait_send())
+            pl.when((level > 0) & (level + h <= 3))(lambda h=h: downward(h).wait_send())
+
+    def part_level(at, side):
+        block_of = at * 2 + side
+        part_gate(gate_far.at[block_of], span(half + block_of * eighth, eighth))
+
     down_sub = span(sub * down_quarter, down_quarter)
     d_x = remote(
         15,
         down_w.at[span((1 - r) * hidden + sub * down_quarter, down_quarter)],
-        wd_out.at[down_sub, hi],
+        wd_out.at[down_sub],
         row_peer,
     )
     d_n = [
-        remote(16 + k, wd_out.at[down_sub, hi], wd_out.at[down_sub, hi], p)
+        remote(16 + k, wd_out.at[down_sub], wd_out.at[down_sub], p)
         for k, p in enumerate(near)
     ]
     c_x = remote(19, cotangent, cot_out.at[own_rows, hi], row_peer)
@@ -1430,7 +1542,14 @@
         wg[0, at] = ref[:, 0, :]
         wg[1, at] = ref[:, 1, :]
 
-    pl.semaphore_wait(barrier, 5)
+    @pl.when(mid)
+    def _():
+        pl.semaphore_wait(barrier, 6)
+
+    @pl.when(jnp.logical_not(mid))
+    def _():
+        pl.semaphore_wait(barrier, 5)
+
     p_x.start()
     params_ref[:, :half] = params_in[...]
     q_x.start()
@@ -1502,6 +1621,8 @@
         return carry
 
     lax.fori_loop(0, length // chunk, project, 0)
+    gate_hop(0)
+    d_x.start()
     for ref, out in ((qs, q_out), (ks, k_out), (vs, v_out)):
         store(ref, out)
 
@@ -1510,9 +1631,9 @@
     def attend(p, carry):
         @pl.when(p == pairs // 2)
         def _():
-            g_x.wait_recv()
-            start(g_n)
-            d_x.start()
+            gate_hop(1)
+            c_x.start()
+
 
         lane0 = p * 128
         q2 = qs[:, span(lane0, 128)]
@@ -1536,6 +1657,7 @@
         return carry
 
     lax.fori_loop(0, pairs, attend, 0)
+    gate_hop(2)
     store(att, att_out)
     store(logs, log_out)
 
@@ -1559,8 +1681,9 @@
     rs_c.wait_recv()
     row_src[...] = act[x_block] + core_in[span((1 - r) * block, block)]
     rs_x.start()
-    part_gate(gate_far.at[sub], span(half + sub * quarter, quarter))
-    subs = (zp * 2 + 1 - y, (1 - zp) * 2 + y, (1 - zp) * 2 + 1 - y)
+    gate_hop(3)
+    for at in range(4):
+        part_level(at, y)
     rs_x.wait_recv()
     hid_rows = 64
 
@@ -1581,10 +1704,11 @@
     store(hid, hid_out)
     d_x.wait_recv()
     start(d_n)
-    c_x.start()
-    for k in range(3):
-        g_n[k].wait_recv()
-        part_gate(gate_far.at[subs[k]], span(half + subs[k] * quarter, quarter))
+    c_x.wait_recv()
+    c_f.start()
+    gates_across(lambda copy: copy.wait_recv())
+    for at in range(4):
+        part_level(at, 1 - y)
     store(wg, wg_out)
 
     stores_of = []
@@ -1616,18 +1740,16 @@
             copy.start()
             stores_of.append(copy)
     store(tok, act_two)
-    c_x.wait_recv()
-    load_c.wait()
-    c_f.start()
-    for copy in stores_of[6:] + stores[1:] + [load_d]:
+    for copy in stores_of[6:] + stores[1:]:
         copy.wait()
     arrived(d_n)
     c_c.wait_recv()
     c_f.wait_recv()
     for copy in [p_x, q_x, tok_x, tok_c, o_x, g_x, d_x, c_x, c_c, c_f, rs_c, rs_x, ag_c, ag_f] + (
-        q_n + o_n + g_n + d_n + ag_x
+        q_n + o_n + d_n + ag_x
     ):
         copy.wait_send()
+    gates_sent()
 
 
 def front(tokens, starts, table, params, bias, qkv_w, out_w, gate_w, down_w, cotangent):
@@ -1658,7 +1780,7 @@
         bf(3, width, units),
         bf(units, width),
         bf(2, width, hidden),
-        bf(hidden, width),
+        bf(hidden, half),
         bf(length, width),
         bf(block, width),
         f32(8, width),
@@ -1669,7 +1791,7 @@
         bf(3, width, units),
         bf(units, width),
         bf(2, width, hidden),
-        bf(4, half // 4, 2, hidden),
+        bf(8, half // 8, 2, hidden),
         bf(2, half // 8, 2, hidden),
         bf(length, units),
         bf(length, units),
@@ -1690,7 +1812,7 @@
         in_specs=[any_spec] + [vmem_spec] * 4 + [any_spec] * 5,
         out_specs=[any_spec] * (len(outs) - 1) + [vmem_spec],
         scratch_shapes=[pltpu.VMEM(v.shape, v.dtype) for v in scratch]
-        + [dma((29,)), dma((29,)), dma((13,)), dma((16,))],
+        + [dma((42,)), dma((42,)), dma((13,)), dma((16,))],
         compiler_params=pltpu.CompilerParams(
             collective_id=2, has_side_effects=True, vmem_limit_bytes=62 * 2**20
         ),
@@ -1766,6 +1888,7 @@
     if place.count == 8:
         sums, bases, result, result_far, input_grad, input_far, small = back(
             inner,
+            cotangent,
             cot_all,
             gate,
             up,
@@ -1781,19 +1904,22 @@
             hidden_state,
             own_inputs,
             params,
+            down_weight,
             w_down,
             w_gate,
             w_out,
             w_qkv,
         )
-        result = ordered(r, result, result_far)
-        input_grad = ordered(r, input_grad, input_far)
         norms = small[:4, :half]
         bias_grad = ordered(r, small[:3, half : half + units], small[:3, half + units :], 1)
-        gate_up_grad, qkv_grad, out_grad, down_grad = spread(sums, bases, half, units, hidden)
+        gate_up_grad, qkv_grad, out_grad, down_grad, result, input_grad = spread(
+            sums, bases, (result, result_far, input_grad, input_far), half, units, hidden
+        )
         qkv_grad = qkv_grad.transpose(1, 0, 2)
     else:
         block = c * 2 + r
+        w_down = jnp.concatenate([piece(down_weight, r, 2), w_down], axis=1)
+        cot_all = lax.dynamic_update_slice(cot_all, cotangent, (c * (length // 2), 0))
         own_inputs = own_inputs.astype(F32)
         _, normal_two, inverse_two = norm_forward(hidden_state, params[2], params[3])
         gate, up = gate.astype(F32), up.astype(F32)

time: 706 us -> 684 us (0.969)
  Pallas kernels: 683 us -> 669 us
    pallas_call x1, Pallas kernels: 181 us -> 169 us  [front(): pl.pallas_call(front_kernel, out_shape=outs, in_specs=[any_spec] + [vmem_...]
where the time goes in v6:
time: 684 us; the launch traced here: 680 us
  Pallas kernels  669 us (98%)
    pallas_call x1, Pallas kernels, back(): pl.pallas_call(functools.partial(back_kernel, bases), out_shape=outs, in_...  471 us
    pallas_call x1, Pallas kernels, front(): pl.pallas_call(front_kernel, out_shape=outs, in_specs=[any_spec] + [vmem_...  169 us
    pallas_call x1, Pallas kernels, spread(): pl.pallas_call(functools.partial(spread_kernel, bases), out_shape=[jax.Sh...  29.2 us

profile of v6, /device:TPU:0, one launch (start us, length us, event | category | flops | bytes accessed | tf_op | source)
XLA Modules:
  0.0 680.4 jit_solution(18055075159438526760)
XLA Ops:
  0.6 0.0 copy-start
  0.7 1.3 convert_reduce_fusion
  2.0 0.0 copy-done
  2.1 0.6 constant_dynamic-slice_fusion.bias_ref
  2.7 1.4 stack.30.params_in
  4.0 1.0 copy.25.starts_ref
  5.1 2.0 fusion.3
  7.0 1.2 pad_maximum_fusion.table_ref
  8.3 168.6 %shard_map.203 = (bf16[1024,2048]{1,0:T(8,128)(2,1)}, bf16[1024,512]{1,0:T(8,128)(2,1)}, bf16[1024,512]{1,0:T(8,128)(2,1)}, bf16[1024,512]{1,0:T(8,128)(2,1)}, b...) custom-call(bf16[512,1024]{1,0:T(8,128)(2,1)} %tokens.1, ...), custom_call_target="tpu_custom_call" | custom-call | flops 20401094656 | bytes 104857600 | tf_op jit(solution)/shard_map/pallas_call | solution.py:1809
  176.8 471.2 %shard_map.204 = (bf16[2,60,512,256]{3,2,1,0:T(8,128)(2,1)}, bf16[256,1024]{1,0:T(8,128)(2,1)}, bf16[256,1024]{1,0:T(8,128)(2,1)}, f32[256,1024]{1,0:T(8,128)}, f32[256,1024]{1,0:T(8,128)}, /*index=5*/f32[8,2048]{1,0:T(8,128)}) custom-call(bf16[1024,1408]{1,0:T(8,128)(2,1)} %get-tuple-element.41.inner, bf16[512,1024]{1,0:T(8,128)(2,1)} %cot_own.1, ...), custom_call_target="tpu_custom_call" | custom-call | flops 55968792576 | bytes 209715200 | tf_op jit(solution)/shard_map/pallas_call | solution.py:1134
  648.1 0.7 slice_select_fusion.1
  648.8 1.5 fusion.8
  650.4 0.6 pad_maximum_fusion.1
  651.0 0.0 copy-start.1
  651.0 29.2 %shard_map.205 = (f32[1024,2,2816]{2,1,0:T(2,128)}, f32[3,1024,1024]{2,1,0:T(8,128)}, f32[1024,1024]{1,0:T(8,128)}, f32[2816,1024]{1,0:T(8,128)}, bf16[512,1024]{1,0:T(8,128)(2,1)}, /*index=5*/f32[512,1024]{1,0:T(8,128)}) custom-call(bf16[2,60,512,256]{3,2,1,0:T(8,128)(2,1)} %get-tuple-element.59.sums, bf16[256,1024]{1,0:T(8,128)(2,1)} %get-tuple-element.60.res_own, ...), custom_call_target="tpu_custom_call" | custom-call | tf_op jit(solution)/shard_map/pallas_call | solution.py:1307
  680.2 0.0 copy-done.1
  (5 shorter events, 0.0 us)
Async XLA Ops:
  0.6 1.4 copy-start
  651.0 29.2 %copy-start.1 = (f32[3,1024]{1,0:T(4,128)S(1)}, f32[3,1024]{1,0:T(4,128)}, u32[]{:S(2)}) copy-start(f32[3,1024]{1,0:T(4,128)} %param.17) | copy-start | bytes 36868

commit v7 on v6

--- a/solution.py
+++ b/solution.py
@@ -107,22 +107,22 @@
 
 
 def first_places(segment_ids):
-    return jnp.sum(segment_ids[None, :] < segment_ids[:, None], axis=1, dtype=jnp.int32)
+    return jnp.sum(
+        segment_ids[None, :] < segment_ids[:, None], axis=1, keepdims=True, dtype=jnp.int32
+    )
 
 
 def rotary_table(places):
     lane = jnp.arange(128, dtype=jnp.int32) % HEAD
     half_rot = ROT // 2
     inverse = jnp.exp((lane % half_rot).astype(F32) * (-2.0 / ROT) * math.log(ROPE_BASE))
-    angles = places.astype(F32)[:, None] * inverse[None, :]
+    angles = places.astype(F32) * inverse[None, :]
     cosines, sines = jnp.cos(angles), jnp.sin(angles)
     low, turns = (lane < half_rot)[None, :], (lane < ROT)[None, :]
-    return jnp.stack(
-        [
-            jnp.where(turns, cosines, 1.0),
-            jnp.where(low, -sines, 0.0),
-            jnp.where(turns & ~low, sines, 0.0),
-        ]
+    return (
+        jnp.where(turns, cosines, 1.0),
+        jnp.where(low, -sines, 0.0),
+        jnp.where(turns & ~low, sines, 0.0),
     )
 
 
@@ -225,7 +225,9 @@
     values,
     logs,
     starts_ref,
-    table_ref,
+    one_ref,
+    ahead_ref,
+    behind_ref,
     act_one,
     hidden_state,
     own_inputs,
@@ -817,7 +819,7 @@
                 grads = (weights * (nt(g, v) - inside)).astype(BF)
                 outs.append(jnp.dot(grads, k, preferred_element_type=F32))
                 dks.append(tn(grads, q))
-            table = (table_ref[0, begin:end], -table_ref[1, begin:end], -table_ref[2, begin:end])
+            table = (one_ref[begin:end], -ahead_ref[begin:end], -behind_ref[begin:end])
             dq = turned(jnp.concatenate(outs, axis=1) * HEAD ** (-0.5), table).astype(BF)
             joint[begin:end, lanes0] = dq
             bias_sums[0:1, lanes0] = bias_sums[0:1, lanes0] + jnp.sum(dq.astype(F32), axis=0, keepdims=True)
@@ -836,7 +838,7 @@
         def _():
             for one in spans[middle:]:
                 window(*one)
-            table = (table_ref[0], -table_ref[1], -table_ref[2])
+            table = (one_ref[...], -ahead_ref[...], -behind_ref[...])
             dk = turned(key_sums[...], table).astype(BF)
             dv = value_sums[...].astype(BF)
             for k, v in ((1, dk), (2, dv)):
@@ -1134,7 +1136,7 @@
     outs = pl.pallas_call(
         functools.partial(back_kernel, bases),
         out_shape=outs,
-        in_specs=[any_spec] * 11 + [vmem_spec] * 2 + [any_spec] * 3 + [vmem_spec] + [any_spec] * 5,
+        in_specs=[any_spec] * 11 + [vmem_spec] * 4 + [any_spec] * 3 + [vmem_spec] + [any_spec] * 5,
         out_specs=[any_spec] * 5 + [vmem_spec],
         scratch_shapes=[pltpu.VMEM(v.shape, v.dtype) for v in scratch]
         + [dma((13 + chunks,)), dma((26,)), dma((14,)), dma((2 + 10 * chunks,)), dma((16,))]
@@ -1157,7 +1159,7 @@
         values,
         logs,
         starts,
-        table,
+        *table,
         act_one,
         hidden_state,
         own_inputs,
@@ -1319,8 +1321,13 @@
 def front_kernel(
     tokens,
     starts_ref,
-    table_ref,
-    params_in,
+    one_ref,
+    ahead_ref,
+    behind_ref,
+    gain1_ref,
+    shift1_ref,
+    gain2_ref,
+    shift2_ref,
     bias_ref,
     qkv_w,
     out_w,
@@ -1384,6 +1391,9 @@
     next_peer, last_peer = {"dp": d + 2}, {"dp": d - 2}
     mid_peer = {"dp": d + 2 - 4 * (level // 2)}
 
+    for i, ref in enumerate((gain1_ref, shift1_ref, gain2_ref, shift2_ref)):
+        params_ref[i : i + 1, :half] = ref[...]
+    params_ref[4:, :half] = jnp.zeros((4, half), F32)
     barrier = pltpu.get_barrier_semaphore()
     for peer in (row_peer, col_peer) + near:
         pl.semaphore_signal(barrier, inc=1, device_id=peer, device_id_type=MESH)
@@ -1528,7 +1538,7 @@
     ag_c = remote(26, tok.at[own_block], tok.at[own_block], col_peer)
     ag_f = remote(27, tok.at[x_block], tok.at[x_block], col_peer)
 
-    p_x = remote(28, params_in, params_ref.at[:, hi], row_peer)
+    p_x = remote(28, params_ref.at[:, lo], params_ref.at[:, hi], row_peer)
 
     def start(copies):
         for copy in copies:
@@ -1551,7 +1561,6 @@
         pl.semaphore_wait(barrier, 5)
 
     p_x.start()
-    params_ref[:, :half] = params_in[...]
     q_x.start()
     tok_c.start()
     c_c.start()
@@ -1611,7 +1620,7 @@
             if kind == 2:
                 ref[at] = out.astype(BF)
                 continue
-            table = (table_ref[0, at], table_ref[1, at], table_ref[2, at])
+            table = (one_ref[at], ahead_ref[at], behind_ref[at])
             for g in range(units // 128):
                 lanes = slice(g * 128, (g + 1) * 128)
                 v = turned(out[:, lanes], table).astype(BF)
@@ -1646,11 +1655,10 @@
                 lanes = slice(h * HEAD, (h + 1) * HEAD)
                 scores = nt(q2[begin:end, lanes], k2[low:end, lanes]) + bar
                 maxima = jnp.max(scores, axis=1, keepdims=True)
-                shifted = jnp.exp(scores - maxima).astype(BF)
-                wide = jnp.concatenate([v2[low:end, lanes], jnp.ones((end - low, HEAD), BF)], axis=1)
-                got = jnp.dot(shifted, wide, preferred_element_type=F32)
-                totals = got[:, HEAD : HEAD + 1]
-                outs.append(got[:, :HEAD] / totals)
+                shifted = jnp.exp(scores - maxima)
+                totals = jnp.sum(shifted, axis=1, keepdims=True)
+                got = jnp.dot(shifted.astype(BF), v2[low:end, lanes], preferred_element_type=F32)
+                outs.append(got / totals)
                 logs[p, begin:end, h : h + 1] = maxima + jnp.log(totals)
             out = jnp.concatenate(outs, axis=1)
             att[begin:end, span(lane0, 128)] = out.astype(BF)
@@ -1809,19 +1817,19 @@
     return pl.pallas_call(
         front_kernel,
         out_shape=outs,
-        in_specs=[any_spec] + [vmem_spec] * 4 + [any_spec] * 5,
+        in_specs=[any_spec] + [vmem_spec] * 9 + [any_spec] * 5,
         out_specs=[any_spec] * (len(outs) - 1) + [vmem_spec],
         scratch_shapes=[pltpu.VMEM(v.shape, v.dtype) for v in scratch]
         + [dma((42,)), dma((42,)), dma((13,)), dma((16,))],
         compiler_params=pltpu.CompilerParams(
-            collective_id=2, has_side_effects=True, vmem_limit_bytes=62 * 2**20
+            collective_id=2, has_side_effects=True, vmem_limit_bytes=63 * 2**20
         ),
         cost_estimate=pl.CostEstimate(
             flops=2 * length * width * (4 * units + 2 * hidden),
             bytes_accessed=100 * 2**20,
             transcendentals=length * 2048,
         ),
-    )(tokens, starts, table, params, bias, qkv_w, out_w, gate_w, down_w, cotangent)
+    )(tokens, starts, *table, *params, bias, qkv_w, out_w, gate_w, down_w, cotangent)
 
 
 def local(
@@ -1848,11 +1856,9 @@
     heads = units // HEAD
     hidden = gate_up_weight.shape[2] // 2
 
-    none = jnp.zeros_like(ln1_gain)
-    params = jnp.stack([ln1_gain, ln1_bias, ln2_gain, ln2_bias] + [none] * 4)
-    firsts = first_places(ids)
-    table = rotary_table(jnp.arange(length, dtype=jnp.int32) - firsts)
-    starts = firsts[:, None]
+    params = [v[None] for v in (ln1_gain, ln1_bias, ln2_gain, ln2_bias)]
+    starts = first_places(ids)
+    table = rotary_table(jnp.arange(length, dtype=jnp.int32)[:, None] - starts)
     bias = piece(qkv_bias, r, 2, 1)
     (
         act_one,
@@ -1946,7 +1952,7 @@
         grad_branch = gather_blocks(grad_hidden.astype(BF), place)
         grad_attended = dot_t(grad_branch, w_out).astype(BF)
         grad_joined = attention_backward(
-            queries, keys, values, grad_attended, attended, logs, starts, table
+            queries, keys, values, grad_attended, attended, logs, starts, jnp.stack(table)
         )
         grad_joined = jnp.concatenate(grad_joined, axis=1)
         bias_grad = jnp.sum(grad_joined, axis=0, dtype=F32)

time: 684 us -> 689 us (level)
  no operation moved by 1% of the time
where the time goes in v7:
time: 689 us; the launch traced here: 679 us
  Pallas kernels  669 us (97%)
    pallas_call x1, Pallas kernels, back(): pl.pallas_call(functools.partial(back_kernel, bases), out_shape=outs, in_...  471 us
    pallas_call x1, Pallas kernels, front(): pl.pallas_call(front_kernel, out_shape=outs, in_specs=[any_spec] + [vmem_...  168 us
    pallas_call x1, Pallas kernels, spread(): pl.pallas_call(functools.partial(spread_kernel, bases), out_shape=[jax.Sh...  29.2 us

profile of v7, /device:TPU:0, one launch (start us, length us, event | category | flops | bytes accessed | tf_op | source)
XLA Modules:
  0.0 678.8 jit_solution(17171681307387233922)
XLA Ops:
  0.6 0.0 copy-start
  0.7 1.3 convert_reduce_fusion
  2.0 0.0 copy-done
  2.1 0.6 constant_dynamic-slice_fusion.bias_ref
  2.7 1.0 copy.25.starts_ref
  3.7 3.2 fusion
  6.8 168.3 %shard_map.203 = (bf16[1024,2048]{1,0:T(8,128)(2,1)}, bf16[1024,512]{1,0:T(8,128)(2,1)}, bf16[1024,512]{1,0:T(8,128)(2,1)}, bf16[1024,512]{1,0:T(8,128)(2,1)}, b...) custom-call(bf16[512,1024]{1,0:T(8,128)(2,1)} %tokens.1, ...), custom_call_target="tpu_custom_call" | custom-call | flops 20401094656 | bytes 104857600 | tf_op jit(solution)/shard_map/pallas_call | solution.py:1817
  175.2 471.3 %shard_map.204 = (bf16[2,60,512,256]{3,2,1,0:T(8,128)(2,1)}, bf16[256,1024]{1,0:T(8,128)(2,1)}, bf16[256,1024]{1,0:T(8,128)(2,1)}, f32[256,1024]{1,0:T(8,128)}, f32[256,1024]{1,0:T(8,128)}, /*index=5*/f32[8,2048]{1,0:T(8,128)}) custom-call(bf16[1024,1408]{1,0:T(8,128)(2,1)} %get-tuple-element.41.inner, bf16[512,1024]{1,0:T(8,128)(2,1)} %cot_own.1, ...), custom_call_target="tpu_custom_call" | custom-call | flops 55968792576 | bytes 209715200 | tf_op jit(solution)/shard_map/pallas_call | solution.py:1136
  646.5 0.7 slice_select_fusion.1
  647.2 1.5 fusion.8
  648.8 0.6 pad_maximum_fusion
  649.4 0.0 copy-start.1
  649.4 29.2 %shard_map.205 = (f32[1024,2,2816]{2,1,0:T(2,128)}, f32[3,1024,1024]{2,1,0:T(8,128)}, f32[1024,1024]{1,0:T(8,128)}, f32[2816,1024]{1,0:T(8,128)}, bf16[512,1024]{1,0:T(8,128)(2,1)}, /*index=5*/f32[512,1024]{1,0:T(8,128)}) custom-call(bf16[2,60,512,256]{3,2,1,0:T(8,128)(2,1)} %get-tuple-element.59.sums, bf16[256,1024]{1,0:T(8,128)(2,1)} %get-tuple-element.60.res_own, ...), custom_call_target="tpu_custom_call" | custom-call | tf_op jit(solution)/shard_map/pallas_call | solution.py:1309
  678.6 0.0 copy-done.1
  (4 shorter events, 0.0 us)
Async XLA Ops:
  0.6 1.4 copy-start
  649.4 29.2 %copy-start.1 = (f32[3,1024]{1,0:T(4,128)S(1)}, f32[3,1024]{1,0:T(4,128)}, u32[]{:S(2)}) copy-start(f32[3,1024]{1,0:T(4,128)} %param.17) | copy-start | bytes 36868
